TPU v7x, 32 devices: a whole 2x2x4 slice. The times are simulated.
32 devices in a mesh: parts: 2 (over x), ep: 16 (over z, y, core).
Axes of the slice: x: 2, y: 2, z: 4, core: 2. Of those that a mesh axis runs over, the one named last changes fastest.
Arguments:
- tokens: bfloat16 [3072, 2048], P(('parts', 'ep')), parts along dimension 0, may hold values from -6 to 6
- expert_ids: int32 [3072, 8], P(('parts', 'ep')), parts along dimension 0, may hold values from 0 to 15, as said below
- gate_probs: float32 [3072, 8], P(('parts', 'ep')), parts along dimension 0, may hold values from 0.1 to 1
- lengths: int32 [96], P(('parts', 'ep')), parts along dimension 0, may hold values from 16 to 32, as said below
- block_counts: int32 [32], P('parts'), parts along dimension 0, may hold values from 2 to 6, as said below
- hot_list: int32 [8, 2], P('parts'), parts along dimension 0, may hold values from 0 to 15, as said below
- w_gate: bfloat16 [16, 2048, 768], P('ep'), may hold values from -0.125 to 0.125
- w_up: bfloat16 [16, 2048, 768], P('ep'), may hold values from -0.125 to 0.125
- w_down: bfloat16 [16, 768, 2048], P('ep'), may hold values from -0.21875 to 0.21875
Outputs:
- moe_out: bfloat16 [3072, 2048], P(('parts', 'ep')), parts along dimension 0
There are 2 independent parts, one for each index of `parts`. A program takes and returns all parts, laid end to end along the dimension named above; an argument that names none is the same for every part. Nothing has to cross between parts.
Inputs may be any that keep to these rules, and one draw needn't show every extreme that they name: `expert_ids`: each row names 8 different experts; each expert in column 0 of hot_list is named by exactly 96 rows of every device; no other expert is named by more than 96 rows of one device, and on each device that holds some of the first 192 tokens one unlisted expert is named by exactly 96 rows. `lengths`: every block among the first 192 tokens has 32 live positions; some other block has 16. `block_counts`: every expert in column 0 of hot_list has 6 blocks; every other has 2 to 4 blocks, both ends reached. `hot_list`: column 0 holds 4 different experts; column 1 is column 0 plus half of 16, modulo 16; no expert of column 0 stands in column 1.
All inputs are finite; a program needn't handle non-finite values.
Results may differ from a plain program's by a relative error of at most 0.0058.
Values may be sent and summed in bfloat16 or wider, within the bound.
No kernel may reach another device: no remote copies, remote signals or barrier semaphores. Data moves between devices by JAX's collectives and lax.ppermute only.
A program may use at most 64 MiB of HBM per device.

v0:
```python
import jax
import jax.numpy as jnp
from jax import lax
from jax.sharding import PartitionSpec as P

BLOCK_LEN = 32
BLK = 128


def expert_forward(gathered, w_gate_e, w_up_e, w_down_e):
    gate = jnp.dot(gathered, w_gate_e, preferred_element_type=jnp.float32)
    up_val = jnp.dot(gathered, w_up_e, preferred_element_type=jnp.float32)
    activation = (jax.nn.silu(gate) * up_val).astype(jnp.bfloat16)
    return jnp.dot(activation, w_down_e, preferred_element_type=jnp.float32).astype(jnp.bfloat16)


def plan_sizes(devices, tok_rows, fan_out, listed):
    assigned = tok_rows * fan_out
    slot_rows = min(2 * assigned // devices, tok_rows)
    cold_load = 3 * devices * (assigned - listed * slot_rows) // (4 * (devices - listed))
    own_blocks = (cold_load + BLK - 1) // BLK
    hot_load = 3 * devices * slot_rows // 4
    spare_blocks = ((hot_load + BLK - 1) // BLK - own_blocks) // 2
    return (slot_rows, own_blocks + spare_blocks, spare_blocks)


def run_blocks(buffer, gate_w, up_w, down_w):
    return expert_forward(buffer, gate_w, up_w, down_w)


def per_device(
    tokens, expert_ids, gate_probs, lengths, block_counts, hot_list, w_gate, w_up, w_down
):
    devices = lax.axis_size("ep")
    my_index = lax.axis_index("ep")
    tok_rows, model_width = tokens.shape
    fan_out = expert_ids.shape[1]
    assigned = tok_rows * fan_out
    slot_rows, most_blocks, spare_blocks = plan_sizes(devices, tok_rows, fan_out, hot_list.shape[0])
    position = jnp.arange(tok_rows, dtype=jnp.int32)
    is_valid = position % BLOCK_LEN < jnp.repeat(lengths, BLOCK_LEN)
    flat_ids = expert_ids.reshape(assigned)
    flat_valid = jnp.repeat(is_valid, fan_out)
    experts = jnp.arange(devices, dtype=jnp.int32)
    onehot = ((flat_ids[:, None] == experts[None, :]) & flat_valid[:, None]).astype(jnp.int32)
    local_rank = jnp.sum((jnp.cumsum(onehot, axis=0) - onehot) * onehot, axis=1)
    counts = jnp.sum(onehot, axis=0)
    all_counts = lax.all_gather(counts[None, :], "ep", axis=0, tiled=True)
    prefix = jnp.cumsum(all_counts, axis=0) - all_counts
    is_hot = jnp.sum((hot_list[:, 0][None, :] == experts[:, None]).astype(jnp.int32), axis=1)
    own_cap = BLK * block_counts
    spare_cap = spare_blocks * BLK * is_hot
    slot_place = jnp.where(flat_valid, flat_ids * slot_rows + local_rank, devices * slot_rows)
    slot_table = jnp.full((devices * slot_rows,), assigned, jnp.int32)
    slot_table = slot_table.at[slot_place].set(jnp.arange(assigned, dtype=jnp.int32), mode="drop")
    padded = jnp.concatenate([tokens, jnp.zeros((1, model_width), tokens.dtype)], axis=0)
    outgoing = padded[slot_table // fan_out].reshape(devices, slot_rows, model_width)
    incoming = lax.all_to_all(outgoing, "ep", split_axis=0, concat_axis=0, tiled=True).reshape(
        devices * slot_rows, model_width
    )
    incoming_pad = jnp.concatenate([incoming, jnp.zeros((1, model_width), incoming.dtype)], axis=0)
    all_slots = devices * slot_rows
    from_counts = lax.dynamic_index_in_dim(all_counts, my_index, 1, keepdims=False)
    from_prefix = lax.dynamic_index_in_dim(prefix, my_index, 1, keepdims=False)
    slot_index = jnp.arange(slot_rows, dtype=jnp.int32)
    global_rank = (from_prefix[:, None] + slot_index[None, :]).reshape(all_slots)
    is_live = (slot_index[None, :] < from_counts[:, None]).reshape(all_slots)
    my_own = lax.dynamic_index_in_dim(own_cap, my_index, 0, keepdims=False)
    my_spare = lax.dynamic_index_in_dim(spare_cap, my_index, 0, keepdims=False)
    rank_limit = my_own + my_spare
    buffer_rows = (most_blocks + spare_blocks) * BLK
    inside = is_live & (global_rank >= 0) & (global_rank < 0 + rank_limit)
    where_to = jnp.where(inside, global_rank - 0, buffer_rows)
    rank_order = jnp.full((buffer_rows,), all_slots, jnp.int32)
    rank_order = rank_order.at[where_to].set(jnp.arange(all_slots, dtype=jnp.int32), mode="drop")
    rows_all = incoming_pad[rank_order]
    results = run_blocks(rows_all, w_gate[0], w_up[0], w_down[0])
    is_kept = is_live & (global_rank < rank_limit)
    result_rows = results.shape[0]
    results_pad = jnp.concatenate([results, jnp.zeros((1, model_width), results.dtype)], axis=0)
    returning = results_pad[jnp.where(is_kept, global_rank, result_rows)].reshape(
        devices, slot_rows, model_width
    )
    returned = lax.all_to_all(returning, "ep", split_axis=0, concat_axis=0, tiled=True).reshape(
        all_slots, model_width
    )
    returned_pad = jnp.concatenate([returned, jnp.zeros((1, model_width), returned.dtype)], axis=0)
    picked = returned_pad[slot_place].reshape(tok_rows, fan_out, model_width)
    weights = jnp.where(is_valid[:, None], gate_probs, 0.0)
    mixed_sum = jnp.zeros((tok_rows, model_width), jnp.float32)
    for column in range(fan_out):
        mixed_sum = mixed_sum + weights[:, column, None] * picked[:, column, :].astype(jnp.float32)
    return mixed_sum.astype(jnp.bfloat16)


def solution(mesh):
    placed = (
        P(("parts", "ep"), None),
        P(("parts", "ep"), None),
        P(("parts", "ep"), None),
        P(("parts", "ep")),
        P("parts"),
        P("parts", None),
        P("ep", None, None),
        P("ep", None, None),
        P("ep", None, None),
    )
    return jax.shard_map(
        per_device, mesh=mesh, in_specs=placed, out_specs=P(("parts", "ep"), None), check_vma=False
    )
```

profile of v0, /device:TPU:15, one launch (start us, length us, event | category | flops | bytes accessed | tf_op | source)
XLA Modules:
  0.0 416.2 jit_solution(7179017989917661807)
XLA Ops:
  0.0 0.8 broadcast_multiply_fusion
  0.8 0.9 copy.34
  1.7 0.7 broadcast_in_dim.61
  3.2 0.7 broadcast_in_dim.65
  4.3 1.7 reduce-window.6
  6.5 3.4 scatter_custom_fusion
  9.9 1.8 concatenate.12
  11.7 13.8 %gather_fusion = bf16[1536,2048]{1,0:T(8,128)(2,1)} fusion(bf16[97,2048]{1,0:T(8,128)(2,1)} %concatenate.12, s32[2048]{0:T(1024)S(1)} %pad_clamp_fusion.2), kind=kCustom, calls=%fused_computation | custom fusion | bytes 12589056 | tf_op jit(solution)/shard_map/gather | solution.py:57
  25.5 6.7 %all-to-all-start = ((bf16[16,96,2048]{2,1,0:T(8,128)(2,1)}), bf16[16,96,2048]{2,1,0:T(8,128)(2,1)}, u32[]{:S(2)}, u32[]{:S(2)}) async-start(bf16[16,96,2048]{2,1,0:T(8,128)(2,1)} %bitcast.90), calls=%async_computation | async-start | bytes 12582912 | tf_op jit(solution)/shard_map/all_to_all | solution.py:58
  33.7 133.8 %all-reduce.4 = s32[256]{0:T(256)S(1)} all-reduce(s32[256]{0:T(256)S(1)} %dynamic-update-slice), channel_id=2, replica_groups=mesh['parts'=2,'ep'=16] {'ep'}, use_global_device_ids=true, to_apply=%add.4 | all-reduce | flops 256 | bytes 2048
  170.8 6.2 %scatter_custom_fusion.1 = s32[1152]{0:T(1024)S(1)} fusion(s32[1536]{0:T(1024)S(1)} %get-tuple-element.6, s32[1536]{0:T(1024)S(1)} %iota.47, s32[]{:T(128)} %constant.79.clone.1), kind=kCustom, calls=%fused_computation.77 | custom fusion | bytes 4612 | tf_op jit(solution)/shard_map/scatter | solution.py:75
  177.0 6.6 %concatenate.13 = bf16[1537,2048]{1,0:T(8,128)(2,1)} pad(bf16[1536,2048]{1,0:T(8,128)(2,1)} %bitcast.3, bf16[]{:T(256)} %constant.75.clone.1), padding=0_1x0_0 | pad | bytes 12587010 | tf_op jit(solution)/shard_map/concatenate | solution.py:61
  183.6 14.5 %gather_fusion.1 = bf16[1152,2048]{1,0:T(8,128)(2,1)} fusion(bf16[1537,2048]{1,0:T(8,128)(2,1)} %concatenate.13, s32[2048]{0:T(1024)S(1)} %pad_clamp_fusion.1), kind=kCustom, calls=%fused_computation.1 | custom fusion | bytes 9441792 | tf_op jit(solution)/shard_map/gather | solution.py:76
  198.1 6.8 %fusion.3 = f32[1152,768]{1,0:T(8,128)S(1)} fusion(bf16[1152,2048]{1,0:T(8,128)(2,1)} %gather_fusion.1, bf16[1,2048,768]{2,1,0:T(8,128)(2,1)} %param.15), kind=kOutput, calls=%fused_computation.11 | convolution fusion | flops 3623878656 | bytes 11403264 | tf_op jit(solution)/shard_map/dot_general | solution.py:11
  204.8 4.2 %fusion = bf16[1152,768]{1,0:T(8,128)(2,1)S(1)} fusion(bf16[1152,2048]{1,0:T(8,128)(2,1)S(1)} %copy-done.2, f32[1152,768]{1,0:T(8,128)S(1)} %fusion.3, bf16[1,2048,768]{2,1,0:T(8,128)(2,1)S(1)} %copy-done.4), kind=kOutput, calls=%fused_computation.8 | convolution fusion | flops 3629187072 | bytes 13172736 | tf_op jit(solution)/shard_map/dot_general | solution.py:12
  209.0 4.1 convolution_convert_fusion
  213.1 2.6 concatenate.14
  215.7 15.7 %gather_fusion.2 = bf16[1536,2048]{1,0:T(8,128)(2,1)} fusion(bf16[1153,2048]{1,0:T(8,128)(2,1)} %concatenate.14, s32[2048]{0:T(1024)S(1)} %pad_clamp_fusion), kind=kCustom, calls=%fused_computation.2 | custom fusion | bytes 12589056 | tf_op jit(solution)/shard_map/gather | solution.py:81
  231.4 8.5 %all-to-all-start.1 = ((bf16[16,96,2048]{2,1,0:T(8,128)(2,1)}), bf16[16,96,2048]{2,1,0:T(8,128)(2,1)}, u32[]{:S(2)}, u32[]{:S(2)}) async-start(bf16[16,96,2048]{2,1,0:T(8,128)(2,1)} %bitcast.91), calls=%async_computation.1 | async-start | bytes 12582912 | tf_op jit(solution)/shard_map/all_to_all | solution.py:84
  240.0 137.4 %all-to-all-done.1 = bf16[16,96,2048]{2,1,0:T(8,128)(2,1)} async-done(((bf16[16,96,2048]{2,1,0:T(8,128)(2,1)}), bf16[16,96,2048]{2,1,0:T(8,128)(2,1)}, u32[]{:S(2)}, u32[]{:S(2)}) %all-to-all-start.1) | async-done | bytes 6291488 | tf_op jit(solution)/shard_map/all_to_all | solution.py:84
  377.4 6.6 %concatenate.15 = bf16[1537,2048]{1,0:T(8,128)(2,1)} pad(bf16[1536,2048]{1,0:T(8,128)(2,1)} %bitcast.11, bf16[]{:T(256)} %constant.75.clone.1), padding=0_1x0_0 | pad | bytes 12587010 | tf_op jit(solution)/shard_map/concatenate | solution.py:87
  383.9 10.8 %gather_fusion.3 = bf16[768,2048]{1,0:T(8,128)(2,1)} fusion(bf16[1537,2048]{1,0:T(8,128)(2,1)} %concatenate.15, s32[1024]{0:T(1024)S(1)} %pad_clamp_fusion.3), kind=kCustom, calls=%fused_computation.3 | custom fusion | bytes 6294528 | tf_op jit(solution)/shard_map/gather | solution.py:88
  394.7 17.4 %fusion.34 = (bf16[96,1,2048]{2,1,0:T(2,128)(2,1)S(1)}, bf16[96,1,2048]{2,1,0:T(2,128)(2,1)S(1)}, bf16[96,1,2048]{2,1,0:T(2,128)(2,1)S(1)}, bf16[96,1,2048]{2,1,...) fusion(bf16[96,8,2048]{2,1,0:T(8,128)(2,1)} %bitcast.89), kind=kLoop, calls=%fused_computation.105 | loop fusion | bytes 6291456 | tf_op jit(solution)/shard_map/slice | solution.py:92
  412.1 4.1 fusion.6
  (62 shorter events, 4.4 us)
Async XLA Ops:
  0.0 209.0 %copy-start = (bf16[1,768,2048]{2,1,0:T(8,128)(2,1)S(1)}, bf16[1,768,2048]{2,1,0:T(8,128)(2,1)}, u32[]{:S(2)}) copy-start(bf16[1,768,2048]{2,1,0:T(8,128)(2,1)} %param.17) | copy-start | bytes 9437188
  25.5 6.7 %copy-start.7 = (u32[32]{0:T(128)S(1)}, u32[32]{0:T(128)}, u32[]{:S(2)}) copy-start(u32[32]{0:T(128)} %constant.106) | copy-start | bytes 388
  25.5 142.6 %copy-start.6 = (s32[16]{0:T(128)S(1)}, s32[16]{0:T(128)}, u32[]{:S(2)}) copy-start(s32[16]{0:T(128)} %param.13) | copy-start | bytes 196
  25.5 143.2 %copy-start.5 = (s32[4,2]{0,1:T(2,128)S(1)}, s32[4,2]{0,1:T(2,128)}, u32[]{:S(2)}) copy-start(s32[4,2]{0,1:T(2,128)} %param.14) | copy-start | bytes 100
  25.5 151.5 %all-to-all-start = ((bf16[16,96,2048]{2,1,0:T(8,128)(2,1)}), bf16[16,96,2048]{2,1,0:T(8,128)(2,1)}, u32[]{:S(2)}, u32[]{:S(2)}) async-start(bf16[16,96,2048]{2,1,0:T(8,128)(2,1)} %bitcast.90), calls=%async_computation | async-start | bytes 12582912 | tf_op jit(solution)/shard_map/all_to_all | solution.py:58
  198.1 6.8 %copy-start.2 = (bf16[1152,2048]{1,0:T(8,128)(2,1)S(1)}, bf16[1152,2048]{1,0:T(8,128)(2,1)}, u32[]{:S(2)}) copy-start(bf16[1152,2048]{1,0:T(8,128)(2,1)} %gather_fusion.1) | copy-start | bytes 14155780
  198.1 6.8 %copy-start.4 = (bf16[1,2048,768]{2,1,0:T(8,128)(2,1)S(1)}, bf16[1,2048,768]{2,1,0:T(8,128)(2,1)}, u32[]{:S(2)}) copy-start(bf16[1,2048,768]{2,1,0:T(8,128)(2,1)} %param.16) | copy-start | bytes 9437188
  231.4 8.5 %copy-start.3 = (f32[96,8]{0,1:T(8,128)S(1)}, f32[96,8]{0,1:T(8,128)}, u32[]{:S(2)}) copy-start(f32[96,8]{0,1:T(8,128)} %param.11) | copy-start | bytes 9220
  231.4 146.0 %all-to-all-start.1 = ((bf16[16,96,2048]{2,1,0:T(8,128)(2,1)}), bf16[16,96,2048]{2,1,0:T(8,128)(2,1)}, u32[]{:S(2)}, u32[]{:S(2)}) async-start(bf16[16,96,2048]{2,1,0:T(8,128)(2,1)} %bitcast.91), calls=%async_computation.1 | async-start | bytes 12582912 | tf_op jit(solution)/shard_map/all_to_all | solution.py:84
  394.7 21.5 %copy-start.1 = (bf16[1,768,2048]{2,1,0:T(8,128)(2,1)S(1)}, bf16[1,768,2048]{2,1,0:T(8,128)(2,1)}, u32[]{:S(2)}) copy-start(bf16[1,768,2048]{2,1,0:T(8,128)(2,1)} %param.17) | copy-start | bytes 9437188
where the time goes:
time: 417 us; the launch traced here: 416 us
  waiting for transfers between devices  137 us (33%)
  blocking collectives  134 us (32%)
  local copies, waits for them, and re-layouts  105 us (25%)
  starting transfers between devices  15.2 us (4%)
  matrix products  15 us (4%)
  other arithmetic  7.57 us (2%)
    all_to_all x1, waiting for transfers between devices, per_device(): lax.all_to_all(returning, 'ep', split_axis=0, concat_axis=0, tiled=True)  137 us
    unnamed x1, blocking collectives  134 us
    slice x1, local copies, waits for them, and re-layouts, per_device(): picked[:, column, :].astype(jnp.float32)  17.4 us
    gather x1, local copies, waits for them, and re-layouts, per_device(): results_pad[jnp.where(is_kept, global_rank, result_rows)]  15.7 us
    gather x1, local copies, waits for them, and re-layouts, per_device(): rows_all = incoming_pad[rank_order]  14.5 us
    gather x1, local copies, waits for them, and re-layouts, per_device(): padded[slot_table // fan_out].reshape(devices, slot_rows, model_width)  13.8 us
    gather x1, local copies, waits for them, and re-layouts, per_device(): picked = returned_pad[slot_place].reshape(tok_rows, fan_out, model_width)  10.8 us
    all_to_all x1, starting transfers between devices, per_device(): lax.all_to_all(returning, 'ep', split_axis=0, concat_axis=0, tiled=True)  8.52 us
  transfers between devices with their start and end apart: 2, of which 1 were waited for; matrix products, arithmetic and copies ran while one was open for 2% of the time, Pallas kernels for 0%

commit v1 on v0

--- a/solution.py
+++ b/solution.py
@@ -28,7 +28,7 @@
     return expert_forward(buffer, gate_w, up_w, down_w)
 
 
-def per_device(
+def sparse_layer(
     tokens, expert_ids, gate_probs, lengths, block_counts, hot_list, w_gate, w_up, w_down
 ):
     devices = lax.axis_size("ep")
@@ -93,6 +93,78 @@
     return mixed_sum.astype(jnp.bfloat16)
 
 
+def dense_layer(
+    tokens, expert_ids, gate_probs, lengths, block_counts, hot_list, w_gate, w_up, w_down
+):
+    devices = lax.axis_size("ep")
+    ring = devices // 4
+    me = lax.axis_index("ep")
+    tok_rows, width = tokens.shape
+    spare_blocks = plan_sizes(devices, tok_rows, expert_ids.shape[1], hot_list.shape[0])[2]
+
+    def ring_pairs(k):
+        return [(d, (d + 4 * k) % devices) for d in range(devices)]
+
+    core_pairs = [(d, d ^ 1) for d in range(devices)]
+    y_pairs = [(d, d ^ 2) for d in range(devices)]
+    over_ring = lambda a, k: lax.ppermute(a, "ep", ring_pairs(k)) if k else a
+    over_y = lambda a: lax.ppermute(a, "ep", y_pairs)
+    over_core = lambda a: lax.ppermute(a, "ep", core_pairs)
+
+    position = jnp.arange(tok_rows, dtype=jnp.int32)
+    is_valid = position % BLOCK_LEN < jnp.repeat(lengths, BLOCK_LEN)
+    experts = jnp.arange(devices, dtype=jnp.int32)
+    names = (expert_ids[None, :, :] == experts[:, None, None]) & is_valid[None, :, None]
+    weight = jnp.sum(jnp.where(names, gate_probs[None], 0.0), axis=2)
+    weight = jnp.where(jnp.any(names, axis=2), weight, -1.0)
+
+    order = [0] + sorted(range(1, ring), key=lambda k: min(k, ring - k))
+    shards = {k: over_ring(tokens, k) for k in order}
+    w_ring = jnp.stack([over_ring(weight, k) for k in range(ring)])
+    w_col = jnp.stack([w_ring, over_y(w_ring)], axis=1)
+    pick = lambda e: lax.dynamic_index_in_dim(w_col, e, 2, keepdims=False)
+    w_mine = jnp.stack([pick(me), over_core(pick(me ^ 1))], axis=1)
+    w_mine = w_mine.reshape(ring * 4, tok_rows)
+    slot = jnp.arange(devices, dtype=jnp.int32)
+    k_of, c_of, y_of = slot // 4, slot // 2 % 2, slot % 2
+    source = (me // 4 - k_of) % ring * 4 + ((me // 2 % 2) ^ y_of) * 2 + ((me % 2) ^ c_of)
+    live = (w_mine >= 0).astype(jnp.int32)
+    counts = jnp.sum(live, axis=1)
+    before = jnp.sum(jnp.where(source[None, :] < source[:, None], counts[None, :], 0), axis=1)
+    rank = before[:, None] + jnp.cumsum(live, axis=1) - live
+    own = lax.dynamic_index_in_dim(block_counts, me, 0, keepdims=False)
+    is_hot = jnp.sum((hot_list[:, 0] == me).astype(jnp.int32))
+    limit = BLK * (own + spare_blocks * is_hot)
+    w_rows = jnp.where((live > 0) & (rank < limit), w_mine, 0.0).reshape(ring, 4 * tok_rows, 1)
+
+    partial = {}
+    for k in order:
+        pair = jnp.concatenate([shards[k], over_y(shards[k])])
+        rows = jnp.concatenate([pair, over_core(pair)])
+        gate = jnp.dot(rows, w_gate[0], preferred_element_type=jnp.float32)
+        up_val = jnp.dot(rows, w_up[0], preferred_element_type=jnp.float32)
+        activation = (jax.nn.silu(gate) * up_val).astype(jnp.bfloat16)
+        result = jnp.dot(activation, w_down[0], preferred_element_type=jnp.float32)
+        partial[k] = (result * w_rows[k]).astype(jnp.bfloat16)
+
+    f32 = lambda a: a.astype(jnp.float32)
+    total = None
+    for k in reversed(order):
+        mine, theirs = partial[k][: 2 * tok_rows], partial[k][2 * tok_rows :]
+        pair = (f32(mine) + f32(over_core(theirs))).astype(jnp.bfloat16)
+        block = f32(pair[:tok_rows]) + f32(over_y(pair[tok_rows:]))
+        got = f32(over_ring(block.astype(jnp.bfloat16), ring - k)) if k else block
+        total = got if total is None else total + got
+    return total.astype(jnp.bfloat16)
+
+
+def per_device(tokens, expert_ids, gate_probs, lengths, block_counts, hot_list, *weights):
+    devices = lax.axis_size("ep")
+    slot_rows = plan_sizes(devices, tokens.shape[0], expert_ids.shape[1], hot_list.shape[0])[0]
+    layer = dense_layer if slot_rows == tokens.shape[0] and devices % 4 == 0 else sparse_layer
+    return layer(tokens, expert_ids, gate_probs, lengths, block_counts, hot_list, *weights)
+
+
 def solution(mesh):
     placed = (
         P(("parts", "ep"), None),

time: 417 us -> 189 us (0.45)
  the two profiles are of different devices: /device:TPU:15 before, /device:TPU:0 now
where the time goes in v1:
time: 189 us; the launch traced here: 188 us
  waiting for transfers between devices  61.9 us (33%)
  matrix products  43.3 us (23%)
  starting transfers between devices  30.6 us (16%)
  local copies, waits for them, and re-layouts  29.2 us (15%)
  other arithmetic  21.3 us (11%)
    ppermute x9, waiting for transfers between devices, dense_layer(): over_y = lambda a: lax.ppermute(a, 'ep', y_pairs)  45.7 us
    dot_general x4, matrix products, dense_layer(): result = jnp.dot(activation, w_down[0], preferred_element_type=jnp.float32)  27.9 us
    ppermute x9, starting transfers between devices, dense_layer(): over_ring = lambda a, k: lax.ppermute(a, 'ep', ring_pairs(k)) if k else a  18.9 us
    ppermute x9, waiting for transfers between devices, dense_layer(): over_ring = lambda a, k: lax.ppermute(a, 'ep', ring_pairs(k)) if k else a  16.2 us
    dot_general x4, matrix products, dense_layer(): up_val = jnp.dot(rows, w_up[0], preferred_element_type=jnp.float32)  15.3 us
    unnamed x46, local copies, waits for them, and re-layouts  13.7 us
    ppermute x9, starting transfers between devices, dense_layer(): over_y = lambda a: lax.ppermute(a, 'ep', y_pairs)  10 us
    slice x4, local copies, waits for them, and re-layouts, dense_layer(): mine, theirs = (partial[k][:2 * tok_rows], partial[k][2 * tok_rows:])  7.97 us
  transfers between devices with their start and end apart: 27, of which 9 were waited for; matrix products, arithmetic and copies ran while one was open for 44% of the time, Pallas kernels for 0%

profile of v1, /device:TPU:0, one launch (start us, length us, event | category | flops | bytes accessed | tf_op | source)
XLA Modules:
  0.0 187.9 jit_solution(7825878729858387990)
XLA Ops:
  2.6 3.1 %collective-permute-start.3 = (f32[16,96]{1,0:T(8,128)S(1)}, f32[16,96]{1,0:T(8,128)S(1)}, u32[]{:S(2)}, u32[]{:S(2)}) collective-permute-start(f32[16,96]{1,0:T(8,128)S(1)} %broadcast_select_fusion), channel_id=1, source_target_pairs={{0,4},{1,5},{2,6},{3,7},{4,8},{5,9},{6,10},{7,11},{8,12},{9,13},{1... | collective-permute-start | bytes 18440 | tf_op jit(solution)/shard_map/ppermute | solution.py:110
  5.6 2.6 %collective-permute-start.4 = (f32[16,96]{1,0:T(8,128)S(1)}, f32[16,96]{1,0:T(8,128)}, u32[]{:S(2)}, u32[]{:S(2)}) collective-permute-start(f32[16,96]{1,0:T(8,128)S(1)} %broadcast_select_fusion), channel_id=1, source_target_pairs={{0,8},{1,9},{2,10},{3,11},{4,12},{5,13},{6,14},{7,15},{8,0},{9,1},... | collective-permute-start | bytes 18440 | tf_op jit(solution)/shard_map/ppermute | solution.py:110
  9.8 2.8 %collective-permute-start.11 = (bf16[96,2048]{1,0:T(8,128)(2,1)}, bf16[96,2048]{1,0:T(8,128)(2,1)}, u32[]{:S(2)}, u32[]{:S(2)}) collective-permute-start(bf16[96,2048]{1,0:T(8,128)(2,1)} %param.9), channel_id=1, source_target_pairs={{0,12},{1,13},{2,14},{3,15},{4,0},{5,1},{6,2},{7,3},{8,4},{9,5},{1... | collective-permute-start | bytes 1179656 | tf_op jit(solution)/shard_map/ppermute | solution.py:110
  19.2 5.8 %collective-permute-done.6 = f32[4,16,96]{2,1,0:T(8,128)} collective-permute-done((f32[4,16,96]{2,1,0:T(8,128)}, f32[4,16,96]{2,1,0:T(8,128)}, u32[]{:S(2)}, u32[]{:S(2)}) %collective-permute-start.6) | collective-permute-done | bytes 24608 | tf_op jit(solution)/shard_map/ppermute | solution.py:111
  42.7 4.4 %collective-permute-done.1 = bf16[96,2048]{1,0:T(8,128)(2,1)S(1)} collective-permute-done((bf16[96,2048]{1,0:T(8,128)(2,1)}, bf16[96,2048]{1,0:T(8,128)(2,1)S(1)}, u32[]{:S(2)}, u32[]{:S(2)}) %collective-permute-start.1) | collective-permute-done | bytes 393248 | tf_op jit(solution)/shard_map/ppermute | solution.py:111
  49.1 6.5 %collective-permute-done.12 = bf16[96,2048]{1,0:T(8,128)(2,1)S(1)} collective-permute-done((bf16[96,2048]{1,0:T(8,128)(2,1)}, bf16[96,2048]{1,0:T(8,128)(2,1)S(1)}, u32[]{:S(2)}, u32[]{:S(2)}) %collective-permute-start.12) | collective-permute-done | bytes 393248 | tf_op jit(solution)/shard_map/ppermute | solution.py:111
  57.5 5.6 %collective-permute-done.18 = bf16[96,2048]{1,0:T(8,128)(2,1)S(1)} collective-permute-done((bf16[96,2048]{1,0:T(8,128)(2,1)}, bf16[96,2048]{1,0:T(8,128)(2,1)S(1)}, u32[]{:S(2)}, u32[]{:S(2)}) %collective-permute-start.18) | collective-permute-done | bytes 393248 | tf_op jit(solution)/shard_map/ppermute | solution.py:111
  69.1 2.4 %fusion.8 = f32[384,768]{1,0:T(8,128)} fusion(bf16[384,2048]{1,0:T(8,128)(2,1)S(1)} %constant_dynamic-update-slice_fusion.9, bf16[1,2048,768]{2,1,0:T(8,128)(2,1)S(1)} %copy-done.18), kind=kOutput, calls=%fused_computation.8 | convolution fusion | flops 1207959552 | bytes 5898240 | tf_op jit(solution)/shard_map/dot_general | solution.py:145
  71.6 6.9 %multiply_convert_fusion = bf16[384,2048]{1,0:T(8,128)(2,1)} fusion(bf16[1,768,2048]{2,1,0:T(8,128)(2,1)S(1)} %copy-done, f32[384]{0:T(512)S(1)} %mul.106, f32[384,768]{1,0:T(8,128)} %fusion.8, bf16[384,2048]{1,0:T(8,128)(2,1)} %copy-done.7, bf16[1,2048,768]{2,1,0:T(8,128)(2,1)} %param.15), kind=kOutput, calls=%fused_computation.24 | convolution fusion | flops 2419261440 | bytes 10618368 | tf_op jit(solution)/shard_map/dot_general | solution.py:147
  78.5 2.2 %slice.105 = bf16[192,2048]{1,0:T(8,128)(2,1)} slice(bf16[384,2048]{1,0:T(8,128)(2,1)} %multiply_convert_fusion), slice={[192:384], [0:2048]} | slice | bytes 1572864 | tf_op jit(solution)/shard_map/slice | solution.py:153
  83.6 4.3 %fusion.14 = f32[384,768]{1,0:T(8,128)} fusion(bf16[384,2048]{1,0:T(8,128)(2,1)S(1)} %constant_dynamic-update-slice_fusion, bf16[1,2048,768]{2,1,0:T(8,128)(2,1)} %param.16), kind=kOutput, calls=%fused_computation.14 | convolution fusion | flops 1207959552 | bytes 5898240 | tf_op jit(solution)/shard_map/dot_general | solution.py:145
  87.9 6.9 %multiply_convert_fusion.3 = bf16[384,2048]{1,0:T(8,128)(2,1)} fusion(bf16[1,768,2048]{2,1,0:T(8,128)(2,1)S(1)} %copy-done, f32[384]{0:T(512)S(1)} %copy-done.17, f32[384,768]{1,0:T(8,128)} %fusion.14, bf16[384,2048]{1,0:T(8,128)(2,1)} %copy-done.13, bf16[1,2048,768]{2,1,0:T(8,128)(2,1)} %param.15), kind=kOutput, calls=%fused_computation.27 | convolution fusion | flops 2419261440 | bytes 10618368 | tf_op jit(solution)/shard_map/dot_general | solution.py:147
  99.4 4.3 %fusion.12 = f32[384,768]{1,0:T(8,128)} fusion(bf16[384,2048]{1,0:T(8,128)(2,1)S(1)} %constant_dynamic-update-slice_fusion.3, bf16[1,2048,768]{2,1,0:T(8,128)(2,1)} %param.16), kind=kOutput, calls=%fused_computation.12 | convolution fusion | flops 1207959552 | bytes 5898240 | tf_op jit(solution)/shard_map/dot_general | solution.py:145
  103.8 7.2 %multiply_convert_fusion.2 = bf16[384,2048]{1,0:T(8,128)(2,1)} fusion(bf16[1,768,2048]{2,1,0:T(8,128)(2,1)S(1)} %copy-done, f32[384]{0:T(512)S(1)} %mul.96, f32[384,768]{1,0:T(8,128)} %fusion.12, bf16[384,2048]{1,0:T(8,128)(2,1)} %copy-done.10, bf16[1,2048,768]{2,1,0:T(8,128)(2,1)} %param.15), kind=kOutput, calls=%fused_computation.26 | convolution fusion | flops 2419261440 | bytes 10618368 | tf_op jit(solution)/shard_map/dot_general | solution.py:147
  110.9 2.2 %slice.95 = bf16[192,2048]{1,0:T(8,128)(2,1)} slice(bf16[384,2048]{1,0:T(8,128)(2,1)} %multiply_convert_fusion.2), slice={[192:384], [0:2048]} | slice | bytes 1572864 | tf_op jit(solution)/shard_map/slice | solution.py:153
  116.1 4.3 %fusion.10 = f32[384,768]{1,0:T(8,128)} fusion(bf16[384,2048]{1,0:T(8,128)(2,1)S(1)} %constant_dynamic-update-slice_fusion.6, bf16[1,2048,768]{2,1,0:T(8,128)(2,1)} %param.16), kind=kOutput, calls=%fused_computation.10 | convolution fusion | flops 1207959552 | bytes 5898240 | tf_op jit(solution)/shard_map/dot_general | solution.py:145
  120.4 6.9 %multiply_convert_fusion.1 = bf16[384,2048]{1,0:T(8,128)(2,1)} fusion(bf16[1,768,2048]{2,1,0:T(8,128)(2,1)S(1)} %copy-done, f32[384]{0:T(512)S(1)} %mul.101, f32[384,768]{1,0:T(8,128)} %fusion.10, bf16[384,2048]{1,0:T(8,128)(2,1)} %copy-done.16, bf16[1,2048,768]{2,1,0:T(8,128)(2,1)} %param.15), kind=kOutput, calls=%fused_computation.25 | convolution fusion | flops 2419261440 | bytes 10618368 | tf_op jit(solution)/shard_map/dot_general | solution.py:147
  138.1 12.9 %collective-permute-done.9 = bf16[96,2048]{1,0:T(8,128)(2,1)S(1)} collective-permute-done((bf16[96,2048]{1,0:T(8,128)(2,1)S(1)}, bf16[96,2048]{1,0:T(8,128)(2,1)S(1)}, u32[]{:S(2)}, u32[]{:S(2)}) %collective-permute-start.9) | collective-permute-done | bytes 393248 | tf_op jit(solution)/shard_map/ppermute | solution.py:111
  153.3 6.2 %collective-permute-done.15 = bf16[96,2048]{1,0:T(8,128)(2,1)S(1)} collective-permute-done((bf16[96,2048]{1,0:T(8,128)(2,1)S(1)}, bf16[96,2048]{1,0:T(8,128)(2,1)S(1)}, u32[]{:S(2)}, u32[]{:S(2)}) %collective-permute-start.15) | collective-permute-done | bytes 393248 | tf_op jit(solution)/shard_map/ppermute | solution.py:111
  159.5 3.2 %collective-permute-start.16 = (bf16[96,2048]{1,0:T(8,128)(2,1)S(1)}, bf16[96,2048]{1,0:T(8,128)(2,1)S(1)}, u32[]{:S(2)}, u32[]{:S(2)}) collective-permute-start(bf16[96,2048]{1,0:T(8,128)(2,1)S(1)} %add_convert_fusion.6), channel_id=1, source_target_pairs={{0,4},{1,5},{2,6},{3,7},{4,8},{5,9},{6,10},{7,11},{8,12},{9,13},{1... | collective-permute-start | bytes 1179656 | tf_op jit(solution)/shard_map/ppermute | solution.py:110
  162.7 4.3 %collective-permute-done.21 = bf16[96,2048]{1,0:T(8,128)(2,1)S(1)} collective-permute-done((bf16[96,2048]{1,0:T(8,128)(2,1)S(1)}, bf16[96,2048]{1,0:T(8,128)(2,1)S(1)}, u32[]{:S(2)}, u32[]{:S(2)}) %collective-permute-start.21) | collective-permute-done | bytes 393248 | tf_op jit(solution)/shard_map/ppermute | solution.py:111
  167.1 3.5 %collective-permute-start.22 = (bf16[96,2048]{1,0:T(8,128)(2,1)S(1)}, bf16[96,2048]{1,0:T(8,128)(2,1)S(1)}, u32[]{:S(2)}, u32[]{:S(2)}) collective-permute-start(bf16[96,2048]{1,0:T(8,128)(2,1)S(1)} %add_convert_fusion.5), channel_id=1, source_target_pairs={{0,12},{1,13},{2,14},{3,15},{4,0},{5,1},{6,2},{7,3},{8,4},{9,5},{1... | collective-permute-start | bytes 1179656 | tf_op jit(solution)/shard_map/ppermute | solution.py:110
  170.7 10.4 %collective-permute-done.10 = bf16[96,2048]{1,0:T(8,128)(2,1)S(1)} collective-permute-done((bf16[96,2048]{1,0:T(8,128)(2,1)S(1)}, bf16[96,2048]{1,0:T(8,128)(2,1)S(1)}, u32[]{:S(2)}, u32[]{:S(2)}) %collective-permute-start.10) | collective-permute-done | bytes 393248 | tf_op jit(solution)/shard_map/ppermute | solution.py:110
  181.0 5.8 %collective-permute-done.22 = bf16[96,2048]{1,0:T(8,128)(2,1)S(1)} collective-permute-done((bf16[96,2048]{1,0:T(8,128)(2,1)S(1)}, bf16[96,2048]{1,0:T(8,128)(2,1)S(1)}, u32[]{:S(2)}, u32[]{:S(2)}) %collective-permute-start.22) | collective-permute-done | bytes 393248 | tf_op jit(solution)/shard_map/ppermute | solution.py:110
  (135 shorter events, 61.5 us)
Async XLA Ops:
  2.6 11.9 %collective-permute-start.3 = (f32[16,96]{1,0:T(8,128)S(1)}, f32[16,96]{1,0:T(8,128)S(1)}, u32[]{:S(2)}, u32[]{:S(2)}) collective-permute-start(f32[16,96]{1,0:T(8,128)S(1)} %broadcast_select_fusion), channel_id=1, source_target_pairs={{0,4},{1,5},{2,6},{3,7},{4,8},{5,9},{6,10},{7,11},{8,12},{9,13},{1... | collective-permute-start | bytes 18440 | tf_op jit(solution)/shard_map/ppermute | solution.py:110
  5.6 8.8 %collective-permute-start.4 = (f32[16,96]{1,0:T(8,128)S(1)}, f32[16,96]{1,0:T(8,128)}, u32[]{:S(2)}, u32[]{:S(2)}) collective-permute-start(f32[16,96]{1,0:T(8,128)S(1)} %broadcast_select_fusion), channel_id=1, source_target_pairs={{0,8},{1,9},{2,10},{3,11},{4,12},{5,13},{6,14},{7,15},{8,0},{9,1},... | collective-permute-start | bytes 18440 | tf_op jit(solution)/shard_map/ppermute | solution.py:110
  9.6 25.4 %collective-permute-start = (bf16[96,2048]{1,0:T(8,128)(2,1)}, bf16[96,2048]{1,0:T(8,128)(2,1)}, u32[]{:S(2)}, u32[]{:S(2)}) collective-permute-start(bf16[96,2048]{1,0:T(8,128)(2,1)} %param.9), channel_id=1, source_target_pairs={{0,8},{1,9},{2,10},{3,11},{4,12},{5,13},{6,14},{7,15},{8,0},{9,1},... | collective-permute-start | bytes 1179656 | tf_op jit(solution)/shard_map/ppermute | solution.py:110
  9.8 26.7 %collective-permute-start.11 = (bf16[96,2048]{1,0:T(8,128)(2,1)}, bf16[96,2048]{1,0:T(8,128)(2,1)}, u32[]{:S(2)}, u32[]{:S(2)}) collective-permute-start(bf16[96,2048]{1,0:T(8,128)(2,1)} %param.9), channel_id=1, source_target_pairs={{0,12},{1,13},{2,14},{3,15},{4,0},{5,1},{6,2},{7,3},{8,4},{9,5},{1... | collective-permute-start | bytes 1179656 | tf_op jit(solution)/shard_map/ppermute | solution.py:110
  14.4 24.6 %collective-permute-start.17 = (bf16[96,2048]{1,0:T(8,128)(2,1)}, bf16[96,2048]{1,0:T(8,128)(2,1)}, u32[]{:S(2)}, u32[]{:S(2)}) collective-permute-start(bf16[96,2048]{1,0:T(8,128)(2,1)} %param.9), channel_id=1, source_target_pairs={{0,4},{1,5},{2,6},{3,7},{4,8},{5,9},{6,10},{7,11},{8,12},{9,13},{1... | collective-permute-start | bytes 1179656 | tf_op jit(solution)/shard_map/ppermute | solution.py:110
  14.4 18.9 %collective-permute-start.23 = (bf16[96,2048]{1,0:T(8,128)(2,1)}, bf16[96,2048]{1,0:T(8,128)(2,1)}, u32[]{:S(2)}, u32[]{:S(2)}) collective-permute-start(bf16[96,2048]{1,0:T(8,128)(2,1)} %param.9), channel_id=1, source_target_pairs={{0,2},{1,3},{2,0},{3,1},{4,6},{5,7},{6,4},{7,5},{8,10},{9,11},{10,... | collective-permute-start | bytes 1179656 | tf_op jit(solution)/shard_map/ppermute | solution.py:111
  34.4 30.8 %collective-permute-start.24 = (bf16[192,2048]{1,0:T(8,128)(2,1)S(1)}, bf16[192,2048]{1,0:T(8,128)(2,1)S(1)}, u32[]{:S(2)}, u32[]{:S(2)}) collective-permute-start(bf16[192,2048]{1,0:T(8,128)(2,1)S(1)} %pad_maximum_fusion.3), channel_id=1, source_target_pairs={{0,1},{1,0},{2,3},{3,2},{4,5},{5,4},{6,7},{7,6},{8,9},{9,8},{10,11... | collective-permute-start | bytes 2359304 | tf_op jit(solution)/shard_map/ppermute | solution.py:112
  34.9 12.2 %collective-permute-start.1 = (bf16[96,2048]{1,0:T(8,128)(2,1)}, bf16[96,2048]{1,0:T(8,128)(2,1)S(1)}, u32[]{:S(2)}, u32[]{:S(2)}) collective-permute-start(bf16[96,2048]{1,0:T(8,128)(2,1)} %collective-permute-done), channel_id=1, source_target_pairs={{0,2},{1,3},{2,0},{3,1},{4,6},{5,7},{6,4},{7,5},{8,10},{9,11},{10,... | collective-permute-start | bytes 1179656 | tf_op jit(solution)/shard_map/ppermute | solution.py:111
  36.4 19.1 %collective-permute-start.12 = (bf16[96,2048]{1,0:T(8,128)(2,1)}, bf16[96,2048]{1,0:T(8,128)(2,1)S(1)}, u32[]{:S(2)}, u32[]{:S(2)}) collective-permute-start(bf16[96,2048]{1,0:T(8,128)(2,1)} %collective-permute-done.11), channel_id=1, source_target_pairs={{0,2},{1,3},{2,0},{3,1},{4,6},{5,7},{6,4},{7,5},{8,10},{9,11},{10,... | collective-permute-start | bytes 1179656 | tf_op jit(solution)/shard_map/ppermute | solution.py:111
  39.0 24.1 %collective-permute-start.18 = (bf16[96,2048]{1,0:T(8,128)(2,1)}, bf16[96,2048]{1,0:T(8,128)(2,1)S(1)}, u32[]{:S(2)}, u32[]{:S(2)}) collective-permute-start(bf16[96,2048]{1,0:T(8,128)(2,1)} %collective-permute-done.17), channel_id=1, source_target_pairs={{0,2},{1,3},{2,0},{3,1},{4,6},{5,7},{6,4},{7,5},{8,10},{9,11},{10,... | collective-permute-start | bytes 1179656 | tf_op jit(solution)/shard_map/ppermute | solution.py:111
  49.1 32.2 %collective-permute-start.2 = (bf16[192,2048]{1,0:T(8,128)(2,1)}, bf16[192,2048]{1,0:T(8,128)(2,1)}, u32[]{:S(2)}, u32[]{:S(2)}) collective-permute-start(bf16[192,2048]{1,0:T(8,128)(2,1)} %pad_maximum_fusion), channel_id=1, source_target_pairs={{0,1},{1,0},{2,3},{3,2},{4,5},{5,4},{6,7},{7,6},{8,9},{9,8},{10,11... | collective-permute-start | bytes 2359304 | tf_op jit(solution)/shard_map/ppermute | solution.py:112
  57.5 39.5 %collective-permute-start.13 = (bf16[192,2048]{1,0:T(8,128)(2,1)}, bf16[192,2048]{1,0:T(8,128)(2,1)}, u32[]{:S(2)}, u32[]{:S(2)}) collective-permute-start(bf16[192,2048]{1,0:T(8,128)(2,1)} %pad_maximum_fusion.1), channel_id=1, source_target_pairs={{0,1},{1,0},{2,3},{3,2},{4,5},{5,4},{6,7},{7,6},{8,9},{9,8},{10,11... | collective-permute-start | bytes 2359304 | tf_op jit(solution)/shard_map/ppermute | solution.py:112
  65.1 48.6 %collective-permute-start.19 = (bf16[192,2048]{1,0:T(8,128)(2,1)}, bf16[192,2048]{1,0:T(8,128)(2,1)}, u32[]{:S(2)}, u32[]{:S(2)}) collective-permute-start(bf16[192,2048]{1,0:T(8,128)(2,1)} %pad_maximum_fusion.2), channel_id=1, source_target_pairs={{0,1},{1,0},{2,3},{3,2},{4,5},{5,4},{6,7},{7,6},{8,9},{9,8},{10,11... | collective-permute-start | bytes 2359304 | tf_op jit(solution)/shard_map/ppermute | solution.py:112
  80.7 48.0 %collective-permute-start.25 = (bf16[192,2048]{1,0:T(8,128)(2,1)}, bf16[192,2048]{1,0:T(8,128)(2,1)}, u32[]{:S(2)}, u32[]{:S(2)}) collective-permute-start(bf16[192,2048]{1,0:T(8,128)(2,1)} %slice.105), channel_id=1, source_target_pairs={{0,1},{1,0},{2,3},{3,2},{4,5},{5,4},{6,7},{7,6},{8,9},{9,8},{10,11... | collective-permute-start | bytes 2359304 | tf_op jit(solution)/shard_map/ppermute | solution.py:112
  97.0 35.1 %collective-permute-start.8 = (bf16[192,2048]{1,0:T(8,128)(2,1)}, bf16[192,2048]{1,0:T(8,128)(2,1)}, u32[]{:S(2)}, u32[]{:S(2)}) collective-permute-start(bf16[192,2048]{1,0:T(8,128)(2,1)} %slice.90), channel_id=1, source_target_pairs={{0,1},{1,0},{2,3},{3,2},{4,5},{5,4},{6,7},{7,6},{8,9},{9,8},{10,11... | collective-permute-start | bytes 2359304 | tf_op jit(solution)/shard_map/ppermute | solution.py:112
  113.2 21.0 %collective-permute-start.14 = (bf16[192,2048]{1,0:T(8,128)(2,1)}, bf16[192,2048]{1,0:T(8,128)(2,1)}, u32[]{:S(2)}, u32[]{:S(2)}) collective-permute-start(bf16[192,2048]{1,0:T(8,128)(2,1)} %slice.95), channel_id=1, source_target_pairs={{0,1},{1,0},{2,3},{3,2},{4,5},{5,4},{6,7},{7,6},{8,9},{9,8},{10,11... | collective-permute-start | bytes 2359304 | tf_op jit(solution)/shard_map/ppermute | solution.py:112
  128.6 8.6 %collective-permute-start.20 = (bf16[192,2048]{1,0:T(8,128)(2,1)S(1)}, bf16[192,2048]{1,0:T(8,128)(2,1)S(1)}, u32[]{:S(2)}, u32[]{:S(2)}) collective-permute-start(bf16[192,2048]{1,0:T(8,128)(2,1)S(1)} %slice.100), channel_id=1, source_target_pairs={{0,1},{1,0},{2,3},{3,2},{4,5},{5,4},{6,7},{7,6},{8,9},{9,8},{10,11... | collective-permute-start | bytes 2359304 | tf_op jit(solution)/shard_map/ppermute | solution.py:112
  130.5 40.1 %collective-permute-start.26 = (bf16[96,2048]{1,0:T(8,128)(2,1)S(1)}, bf16[96,2048]{1,0:T(8,128)(2,1)S(1)}, u32[]{:S(2)}, u32[]{:S(2)}) collective-permute-start(bf16[96,2048]{1,0:T(8,128)(2,1)S(1)} %slice.107), channel_id=1, source_target_pairs={{0,2},{1,3},{2,0},{3,1},{4,6},{5,7},{6,4},{7,5},{8,10},{9,11},{10,... | collective-permute-start | bytes 1179656 | tf_op jit(solution)/shard_map/ppermute | solution.py:111
  133.6 17.4 %collective-permute-start.9 = (bf16[96,2048]{1,0:T(8,128)(2,1)S(1)}, bf16[96,2048]{1,0:T(8,128)(2,1)S(1)}, u32[]{:S(2)}, u32[]{:S(2)}) collective-permute-start(bf16[96,2048]{1,0:T(8,128)(2,1)S(1)} %slice.92), channel_id=1, source_target_pairs={{0,2},{1,3},{2,0},{3,1},{4,6},{5,7},{6,4},{7,5},{8,10},{9,11},{10,... | collective-permute-start | bytes 1179656 | tf_op jit(solution)/shard_map/ppermute | solution.py:111
  135.6 23.8 %collective-permute-start.15 = (bf16[96,2048]{1,0:T(8,128)(2,1)S(1)}, bf16[96,2048]{1,0:T(8,128)(2,1)S(1)}, u32[]{:S(2)}, u32[]{:S(2)}) collective-permute-start(bf16[96,2048]{1,0:T(8,128)(2,1)S(1)} %slice.97), channel_id=1, source_target_pairs={{0,2},{1,3},{2,0},{3,1},{4,6},{5,7},{6,4},{7,5},{8,10},{9,11},{10,... | collective-permute-start | bytes 1179656 | tf_op jit(solution)/shard_map/ppermute | solution.py:111
  137.5 29.5 %collective-permute-start.21 = (bf16[96,2048]{1,0:T(8,128)(2,1)S(1)}, bf16[96,2048]{1,0:T(8,128)(2,1)S(1)}, u32[]{:S(2)}, u32[]{:S(2)}) collective-permute-start(bf16[96,2048]{1,0:T(8,128)(2,1)S(1)} %slice.102), channel_id=1, source_target_pairs={{0,2},{1,3},{2,0},{3,1},{4,6},{5,7},{6,4},{7,5},{8,10},{9,11},{10,... | collective-permute-start | bytes 1179656 | tf_op jit(solution)/shard_map/ppermute | solution.py:111
  151.1 29.9 %collective-permute-start.10 = (bf16[96,2048]{1,0:T(8,128)(2,1)S(1)}, bf16[96,2048]{1,0:T(8,128)(2,1)S(1)}, u32[]{:S(2)}, u32[]{:S(2)}) collective-permute-start(bf16[96,2048]{1,0:T(8,128)(2,1)S(1)} %add_convert_fusion.7), channel_id=1, source_target_pairs={{0,8},{1,9},{2,10},{3,11},{4,12},{5,13},{6,14},{7,15},{8,0},{9,1},... | collective-permute-start | bytes 1179656 | tf_op jit(solution)/shard_map/ppermute | solution.py:110
  159.5 21.5 %collective-permute-start.16 = (bf16[96,2048]{1,0:T(8,128)(2,1)S(1)}, bf16[96,2048]{1,0:T(8,128)(2,1)S(1)}, u32[]{:S(2)}, u32[]{:S(2)}) collective-permute-start(bf16[96,2048]{1,0:T(8,128)(2,1)S(1)} %add_convert_fusion.6), channel_id=1, source_target_pairs={{0,4},{1,5},{2,6},{3,7},{4,8},{5,9},{6,10},{7,11},{8,12},{9,13},{1... | collective-permute-start | bytes 1179656 | tf_op jit(solution)/shard_map/ppermute | solution.py:110
  167.1 19.7 %collective-permute-start.22 = (bf16[96,2048]{1,0:T(8,128)(2,1)S(1)}, bf16[96,2048]{1,0:T(8,128)(2,1)S(1)}, u32[]{:S(2)}, u32[]{:S(2)}) collective-permute-start(bf16[96,2048]{1,0:T(8,128)(2,1)S(1)} %add_convert_fusion.5), channel_id=1, source_target_pairs={{0,12},{1,13},{2,14},{3,15},{4,0},{5,1},{6,2},{7,3},{8,4},{9,5},{1... | collective-permute-start | bytes 1179656 | tf_op jit(solution)/shard_map/ppermute | solution.py:110
  (22 other events, 169.1 us)

commit v2 on v0

--- a/solution.py
+++ b/solution.py
@@ -1,6 +1,10 @@
+import functools
+
 import jax
 import jax.numpy as jnp
 from jax import lax
+from jax.experimental import pallas as pl
+from jax.experimental.pallas import tpu as pltpu
 from jax.sharding import PartitionSpec as P
 
 BLOCK_LEN = 32
@@ -28,7 +32,7 @@
     return expert_forward(buffer, gate_w, up_w, down_w)
 
 
-def per_device(
+def sparse_layer(
     tokens, expert_ids, gate_probs, lengths, block_counts, hot_list, w_gate, w_up, w_down
 ):
     devices = lax.axis_size("ep")
@@ -93,6 +97,265 @@
     return mixed_sum.astype(jnp.bfloat16)
 
 
+def weight_kernel(lengths, ids_ref, probs_ref, out, ids, probs, sems):
+    copies = [
+        pltpu.make_async_copy(ids_ref, ids, sems.at[0]),
+        pltpu.make_async_copy(probs_ref, probs, sems.at[1]),
+    ]
+    for copy in copies:
+        copy.start()
+    for copy in copies:
+        copy.wait()
+    fan_out, rows = ids.shape
+    experts, lanes = out.shape
+    token = lax.broadcasted_iota(jnp.int32, (experts, rows), 1)
+    expert = lax.broadcasted_iota(jnp.int32, (experts, rows), 0)
+    live_len = jnp.zeros((experts, rows), jnp.int32)
+    for block in range(lengths.shape[0]):
+        live_len = jnp.where(token // BLOCK_LEN == block, lengths[block], live_len)
+    is_valid = token % BLOCK_LEN < live_len
+    weight = jnp.full((experts, rows), -1.0, jnp.float32)
+    for k in range(fan_out):
+        weight = jnp.where(is_valid & (ids[k : k + 1, :] == expert), probs[k : k + 1, :], weight)
+    out[...] = jnp.full((experts, lanes), -1.0, jnp.float32)
+    out[:, :rows] = weight
+
+
+def load_kernel(*refs):
+    half = len(refs) // 2
+    copies = [
+        pltpu.make_async_copy(refs[i], refs[half + i], refs[-1].at[i]) for i in range(half)
+    ]
+    for copy in copies:
+        copy.start()
+    for copy in copies:
+        copy.wait()
+
+
+def column_kernel(w0, w1, w2, w3, *outs):
+    me = lax.axis_index("ep")
+    ring = len(outs)
+    for k, out in enumerate(outs):
+        expert = (me // 4 + k) % ring * 4 + me % 4
+        for row, ref in enumerate((w0, w1, w2, w3)):
+            out[row : row + 1, :] = ref[pl.ds(expert, 1), :]
+
+
+def rank_kernel(spare_blocks, block_counts, hot_list, *refs):
+    columns, out, held = refs[:-2], refs[-2], refs[-1]
+    me = lax.axis_index("ep")
+    ring = len(columns)
+    slots, lanes = out.shape
+    for k, ref in enumerate(columns):
+        held[4 * k : 4 * k + 4, :] = ref[:4, :]
+    weight = held[...]
+    live = weight >= 0.0
+    ones = live.astype(jnp.float32)
+    first = lax.broadcasted_iota(jnp.int32, (lanes, lanes), 0)
+    second = lax.broadcasted_iota(jnp.int32, (lanes, lanes), 1)
+    earlier = (first < second).astype(jnp.bfloat16)
+    rank = jnp.dot(ones.astype(jnp.bfloat16), earlier, preferred_element_type=jnp.float32)
+    counts = jnp.sum(ones, axis=1, keepdims=True)
+
+    def source(slot):
+        k, core, y = slot // 4, slot // 2 % 2, slot % 2
+        return (me // 4 - k + ring) % ring * 4 + (me // 2 + y) % 2 * 2 + (me + core) % 2
+
+    place = source(lax.broadcasted_iota(jnp.int32, (slots, 1), 0))
+    before = jnp.zeros((slots, 1), jnp.float32)
+    for slot in range(slots):
+        before = before + jnp.where(source(slot) < place, counts[slot : slot + 1, :], 0.0)
+    limit = block_counts[me]
+    for row in range(hot_list.shape[1]):
+        limit = limit + jnp.where(hot_list[0, row] == me, spare_blocks, 0)
+    kept = live & (rank + before < (limit * BLK).astype(jnp.float32))
+    out[...] = jnp.where(kept, weight, 0.0)
+
+
+def expert_kernel(slot, a, b, c, d, weight, w_gate, w_up, w_down, o_a, o_b, o_cd, *scratch):
+    x, act, res, in_sem, out_sem = scratch
+    rows, width = a.shape
+    hidden = act.shape[1]
+    tile, out_tile = min(256, hidden), width // (out_sem.shape[0] // 3)
+    copies = [
+        pltpu.make_async_copy(src, x.at[pl.ds(i * rows, rows)], in_sem.at[i])
+        for i, src in enumerate((a, b, c, d))
+    ]
+    for copy in copies:
+        copy.start()
+    row = lax.broadcasted_iota(jnp.int32, (rows, weight.shape[1]), 0)
+    lane = lax.broadcasted_iota(jnp.int32, (rows, weight.shape[1]), 1)
+    scale = jnp.concatenate(
+        [
+            jnp.sum(jnp.where(row == lane, weight[4 * slot + i : 4 * slot + i + 1, :], 0.0), axis=1, keepdims=True)
+            for i in range(4)
+        ],
+        axis=0,
+    )
+    for copy in copies:
+        copy.wait()
+    for j in range(hidden // tile):
+        part = slice(j * tile, (j + 1) * tile)
+        gate = jnp.dot(x[...], w_gate[:, part], preferred_element_type=jnp.float32)
+        up_val = jnp.dot(x[...], w_up[:, part], preferred_element_type=jnp.float32)
+        act[:, part] = (gate / (1.0 + jnp.exp(-gate)) * up_val).astype(act.dtype)
+    sent = []
+    for j in range(width // out_tile):
+        part = slice(j * out_tile, (j + 1) * out_tile)
+        result = jnp.dot(act[...], w_down[:, part], preferred_element_type=jnp.float32)
+        res[:, part] = (result * scale).astype(res.dtype)
+        at = pl.ds(j * out_tile, out_tile)
+        for i, (out, start) in enumerate(((o_cd, 2), (o_b, 1), (o_a, 0))):
+            src = res.at[pl.ds(start * rows, out.shape[0]), at]
+            sent.append(pltpu.make_async_copy(src, out.at[:, at], out_sem.at[3 * j + i]))
+            sent[-1].start()
+    for copy in sent:
+        copy.wait()
+
+
+def expert_rows(slot, pieces, weight, matrices):
+    rows, width = pieces[0].shape
+    hidden = matrices[0].shape[1]
+    dtype = pieces[0].dtype
+    anywhere = pl.BlockSpec(memory_space=pl.ANY)
+    vmem = pl.BlockSpec(memory_space=pltpu.VMEM)
+    out_steps = 4
+    matrices = [pltpu.with_memory_space_constraint(m, pltpu.VMEM) for m in matrices]
+    return pl.pallas_call(
+        functools.partial(expert_kernel, slot),
+        in_specs=[anywhere] * 4 + [vmem] * 4,
+        out_specs=[anywhere] * 3,
+        out_shape=[
+            jax.ShapeDtypeStruct((rows, width), dtype),
+            jax.ShapeDtypeStruct((rows, width), dtype),
+            jax.ShapeDtypeStruct((2 * rows, width), dtype),
+        ],
+        scratch_shapes=[
+            pltpu.VMEM((4 * rows, width), dtype),
+            pltpu.VMEM((4 * rows, hidden), dtype),
+            pltpu.VMEM((4 * rows, width), dtype),
+            pltpu.SemaphoreType.DMA((4,)),
+            pltpu.SemaphoreType.DMA((3 * out_steps,)),
+        ],
+        compiler_params=pltpu.CompilerParams(vmem_limit_bytes=20 * 1024 * 1024),
+        cost_estimate=pl.CostEstimate(
+            flops=24 * rows * width * hidden,
+            bytes_accessed=6 * width * hidden + 16 * rows * width,
+            transcendentals=4 * rows * hidden,
+        ),
+        name="expert",
+    )(*pieces, weight, *matrices)
+
+
+def dense_layer(
+    tokens, expert_ids, gate_probs, lengths, block_counts, hot_list, w_gate, w_up, w_down
+):
+    devices = lax.axis_size("ep")
+    ring = devices // 4
+    tok_rows = tokens.shape[0]
+    lanes = (tok_rows + 127) // 128 * 128
+    spare_blocks = plan_sizes(devices, tok_rows, expert_ids.shape[1], hot_list.shape[0])[2]
+
+    def ring_pairs(k):
+        return [(d, (d + 4 * k) % devices) for d in range(devices)]
+
+    core_pairs = [(d, d ^ 1) for d in range(devices)]
+    y_pairs = [(d, d ^ 2) for d in range(devices)]
+    over_ring = lambda a, k: lax.ppermute(a, "ep", ring_pairs(k)) if k else a
+    over_y = lambda a: lax.ppermute(a, "ep", y_pairs)
+    over_core = lambda a: lax.ppermute(a, "ep", core_pairs)
+    after = lambda value, *others: lax.optimization_barrier((value,) + others)[0]
+    f32 = lambda v: v.astype(jnp.float32)
+    bf16 = lambda v: v.astype(jnp.bfloat16)
+    vmem = pl.BlockSpec(memory_space=pltpu.VMEM)
+    smem = pl.BlockSpec(memory_space=pltpu.SMEM)
+    anywhere = pl.BlockSpec(memory_space=pl.ANY)
+    hbm = lambda v: pltpu.with_memory_space_constraint(v, pltpu.HBM)
+    small = pltpu.CompilerParams(vmem_limit_bytes=2 * 1024 * 1024)
+
+    matrices = [hbm(m[0]) for m in (w_gate, w_up, w_down)]
+    matrices = pl.pallas_call(
+        load_kernel,
+        in_specs=[anywhere] * 3,
+        out_specs=[vmem] * 3,
+        out_shape=[pltpu.VMEM(m.shape, m.dtype) for m in matrices],
+        scratch_shapes=[pltpu.SemaphoreType.DMA((3,))],
+        compiler_params=small,
+        name="load",
+    )(*matrices)
+    own_w = pl.pallas_call(
+        weight_kernel,
+        in_specs=[smem, anywhere, anywhere],
+        out_specs=vmem,
+        out_shape=jax.ShapeDtypeStruct((devices, lanes), jnp.float32),
+        scratch_shapes=[
+            pltpu.VMEM(expert_ids.shape[::-1], jnp.int32),
+            pltpu.VMEM(gate_probs.shape[::-1], jnp.float32),
+            pltpu.SemaphoreType.DMA((2,)),
+        ],
+        compiler_params=small,
+        name="weights",
+    )(lengths, hbm(expert_ids.T), hbm(gate_probs.T))
+    sent = after(tokens, own_w)
+    y_w = over_y(own_w)
+    columns = pl.pallas_call(
+        column_kernel,
+        in_specs=[vmem] * 4,
+        out_specs=[vmem] * ring,
+        out_shape=[jax.ShapeDtypeStruct((8, lanes), jnp.float32)] * ring,
+        compiler_params=small,
+        name="columns",
+    )(after(own_w, matrices[0]), y_w, over_core(own_w), over_core(y_w))
+    s1, s3 = over_ring(sent, 1), over_ring(sent, 3)
+    s1 = after(s1, columns[0])
+    columns = [over_ring(column, k) for k, column in enumerate(columns)]
+    s3 = after(s3, *columns[1:])
+    s2 = over_ring(s1, 1)
+    weight = pl.pallas_call(
+        functools.partial(rank_kernel, spare_blocks),
+        in_specs=[smem, smem] + [vmem] * ring,
+        out_specs=vmem,
+        out_shape=jax.ShapeDtypeStruct((devices, lanes), jnp.float32),
+        scratch_shapes=[pltpu.VMEM((devices, lanes), jnp.float32)],
+        compiler_params=small,
+        name="ranks",
+    )(block_counts, hot_list.T, *columns)
+
+    def expert(k, *pieces):
+        return expert_rows(k, pieces, weight, matrices)
+
+    def merge_core(a, b, cd):
+        cd = over_core(cd)
+        return f32(a) + f32(cd[:tok_rows]), bf16(f32(b) + f32(cd[tok_rows:]))
+
+    y_own = over_y(sent)
+    y1, y3 = over_y(s1), over_y(s3)
+    p0 = expert(0, tokens, y_own, over_core(sent), over_core(y_own))
+    y1 = after(y1, p0[0])
+    p1 = expert(1, s1, y1, over_core(s1), over_core(y1))
+    y3 = after(y3, p1[0])
+    p3 = expert(3, s3, y3, over_core(s3), over_core(y3))
+    y2 = after(over_y(s2), p3[0])
+    a1, b1 = merge_core(*p1)
+    p2 = expert(2, after(s2, b1), y2, over_core(s2), over_core(y2))
+
+    (a2, b2), (a3, b3), (a0, b0) = merge_core(*p2), merge_core(*p3), merge_core(*p0)
+    block1 = after(a1, b2) + f32(over_y(b1))
+    block2 = bf16(a2 + f32(over_y(b2)))
+    hop = over_ring(block2, ring - 1)
+    block3 = bf16(a3 + f32(over_y(after(b3, b2))))
+    block0 = a0 + f32(over_y(after(b0, block2)))
+    hop = over_ring(bf16(block1 + f32(hop)), ring - 1)
+    return bf16(block0 + f32(over_ring(block3, 1)) + f32(hop))
+
+
+def per_device(tokens, expert_ids, gate_probs, lengths, block_counts, hot_list, *weights):
+    devices = lax.axis_size("ep")
+    slot_rows = plan_sizes(devices, tokens.shape[0], expert_ids.shape[1], hot_list.shape[0])[0]
+    layer = dense_layer if slot_rows == tokens.shape[0] and devices == 16 else sparse_layer
+    return layer(tokens, expert_ids, gate_probs, lengths, block_counts, hot_list, *weights)
+
+
 def solution(mesh):
     placed = (
         P(("parts", "ep"), None),

time: 417 us -> 120 us (0.29)
  the two profiles are of different devices: /device:TPU:15 before, /device:TPU:0 now
where the time goes in v2:
time: 120 us
  waiting for transfers between devices  57.5 us (48%)
  starting transfers between devices  31.3 us (26%)
  Pallas kernels  28.3 us (24%)
  other arithmetic  1.98 us (2%)
    ppermute x9, waiting for transfers between devices, dense_layer(): over_y = lambda a: lax.ppermute(a, 'ep', y_pairs)  34.4 us
    pallas_call x4, Pallas kernels, expert_rows(): pl.pallas_call(functools.partial(expert_kernel, slot), in_specs=[anywhere...  22.5 us
    ppermute x9, waiting for transfers between devices, dense_layer(): over_ring = lambda a, k: lax.ppermute(a, 'ep', ring_pairs(k)) if k else a  20.4 us
    ppermute x9, starting transfers between devices, dense_layer(): over_ring = lambda a, k: lax.ppermute(a, 'ep', ring_pairs(k)) if k else a  17.3 us
    ppermute x9, starting transfers between devices, dense_layer(): over_y = lambda a: lax.ppermute(a, 'ep', y_pairs)  11.5 us
    pallas_call x1, Pallas kernels, dense_layer(): pl.pallas_call(load_kernel, in_specs=[anywhere] * 3, out_specs=[vmem] * 3...  3.82 us
    ppermute x14, waiting for transfers between devices, dense_layer(): over_core = lambda a: lax.ppermute(a, 'ep', core_pairs)  2.68 us
    ppermute x14, starting transfers between devices, dense_layer(): over_core = lambda a: lax.ppermute(a, 'ep', core_pairs)  2.47 us
  transfers between devices with their start and end apart: 32, of which 16 were waited for; matrix products, arithmetic and copies ran while one was open for 1% of the time, Pallas kernels for 23%

profile of v2, /device:TPU:0, one launch (start us, length us, event | category | flops | bytes accessed | tf_op | source)
XLA Modules:
  0.0 119.9 jit_solution(8248120497104536791)
XLA Ops:
  1.9 3.0 %collective-permute-start = (bf16[96,2048]{1,0:T(8,128)(2,1)}, bf16[96,2048]{1,0:T(8,128)(2,1)S(1)}, u32[]{:S(2)}, u32[]{:S(2)}) collective-permute-start(bf16[96,2048]{1,0:T(8,128)(2,1)} %a.1), channel_id=1, source_target_pairs={{0,2},{1,3},{2,0},{3,1},{4,6},{5,7},{6,4},{7,5},{8,10},{9,11},{10,... | collective-permute-start | bytes 1179656 | tf_op jit(solution)/shard_map/ppermute | solution.py:265
  5.0 1.6 %collective-permute-start.10 = (bf16[96,2048]{1,0:T(8,128)(2,1)}, bf16[96,2048]{1,0:T(8,128)(2,1)S(1)}, u32[]{:S(2)}, u32[]{:S(2)}) collective-permute-start(bf16[96,2048]{1,0:T(8,128)(2,1)} %a.1), channel_id=1, source_target_pairs={{0,4},{1,5},{2,6},{3,7},{4,8},{5,9},{6,10},{7,11},{8,12},{9,13},{1... | collective-permute-start | bytes 1179656 | tf_op jit(solution)/shard_map/ppermute | solution.py:264
  6.6 7.7 %collective-permute-done.b = bf16[96,2048]{1,0:T(8,128)(2,1)S(1)} collective-permute-done((bf16[96,2048]{1,0:T(8,128)(2,1)}, bf16[96,2048]{1,0:T(8,128)(2,1)S(1)}, u32[]{:S(2)}, u32[]{:S(2)}) %collective-permute-start) | collective-permute-done | bytes 393248 | tf_op jit(solution)/shard_map/ppermute | solution.py:265
  14.3 1.7 %collective-permute-start.3 = (f32[16,128]{1,0:T(8,128)S(1)}, f32[16,128]{1,0:T(8,128)S(1)}, u32[]{:S(2)}, u32[]{:S(2)}) collective-permute-start(f32[16,128]{1,0:T(8,128)S(1)} %weights.1.w0), channel_id=1, source_target_pairs={{0,2},{1,3},{2,0},{3,1},{4,6},{5,7},{6,4},{7,5},{8,10},{9,11},{10,... | collective-permute-start | bytes 24584 | tf_op jit(solution)/shard_map/ppermute | solution.py:265
  16.3 1.7 %collective-permute-done.3.w1 = f32[16,128]{1,0:T(8,128)S(1)} collective-permute-done((f32[16,128]{1,0:T(8,128)S(1)}, f32[16,128]{1,0:T(8,128)S(1)}, u32[]{:S(2)}, u32[]{:S(2)}) %collective-permute-start.3) | collective-permute-done | bytes 8224 | tf_op jit(solution)/shard_map/ppermute | solution.py:265
  18.0 3.8 %load.1 = (bf16[2048,768]{1,0:T(8,128)(2,1)S(1)}, bf16[2048,768]{1,0:T(8,128)(2,1)S(1)}, bf16[768,2048]{1,0:T(8,128)(2,1)S(1)}) custom-call(bf16[2048,768]{1,0:T(8,128)(2,1)} %bitcast.7, bf16[2048,768]{1,0:T(8,128)(2,1)} %bitcast.8, bf16[768,2048]{1,0:T(8,128)(2,1)} %bitcast.9), custom_call_target="tpu_custom_call" | custom-call | tf_op jit(solution)/shard_map/load/pallas_call | solution.py:277
  21.9 1.8 %collective-permute-start.12 = (bf16[96,2048]{1,0:T(8,128)(2,1)S(1)}, bf16[96,2048]{1,0:T(8,128)(2,1)S(1)}, u32[]{:S(2)}, u32[]{:S(2)}) collective-permute-start(bf16[96,2048]{1,0:T(8,128)(2,1)S(1)} %collective-permute-done.10.a), channel_id=1, source_target_pairs={{0,2},{1,3},{2,0},{3,1},{4,6},{5,7},{6,4},{7,5},{8,10},{9,11},{10,... | collective-permute-start | bytes 1179656 | tf_op jit(solution)/shard_map/ppermute | solution.py:265
  23.7 1.6 %collective-permute-start.6 = (f32[8,128]{1,0:T(8,128)S(1)}, f32[8,128]{1,0:T(8,128)S(1)}, u32[]{:S(2)}, u32[]{:S(2)}) collective-permute-start(f32[8,128]{1,0:T(8,128)S(1)} %get-tuple-element.39), channel_id=1, source_target_pairs={{0,4},{1,5},{2,6},{3,7},{4,8},{5,9},{6,10},{7,11},{8,12},{9,13},{1... | collective-permute-start | bytes 12296 | tf_op jit(solution)/shard_map/ppermute | solution.py:264
  25.3 2.6 %collective-permute-start.7 = (f32[8,128]{1,0:T(8,128)S(1)}, f32[8,128]{1,0:T(8,128)S(1)}, u32[]{:S(2)}, u32[]{:S(2)}) collective-permute-start(f32[8,128]{1,0:T(8,128)S(1)} %get-tuple-element.40), channel_id=1, source_target_pairs={{0,8},{1,9},{2,10},{3,11},{4,12},{5,13},{6,14},{7,15},{8,0},{9,1},... | collective-permute-start | bytes 12296 | tf_op jit(solution)/shard_map/ppermute | solution.py:264
  29.1 1.8 %collective-permute-start.8 = (f32[8,128]{1,0:T(8,128)S(1)}, f32[8,128]{1,0:T(8,128)S(1)}, u32[]{:S(2)}, u32[]{:S(2)}) collective-permute-start(f32[8,128]{1,0:T(8,128)S(1)} %get-tuple-element.41), channel_id=1, source_target_pairs={{0,12},{1,13},{2,14},{3,15},{4,0},{5,1},{6,2},{7,3},{8,4},{9,5},{1... | collective-permute-start | bytes 12296 | tf_op jit(solution)/shard_map/ppermute | solution.py:264
  33.5 5.7 %expert.4 = (bf16[96,2048]{1,0:T(8,128)(2,1)S(1)}, bf16[96,2048]{1,0:T(8,128)(2,1)S(1)}, bf16[192,2048]{1,0:T(8,128)(2,1)S(1)}) custom-call(bf16[96,2048]{1,0:T(8,128)(2,1)S(1)} %copy-done.3, bf16[96,2048]{1,0:T(8,128)(2,1)S(1)} %collective-permute-done.b, bf16[96,2048]{1,0:T(8,128)(2,1)S(1)} %collective-permute-done.1.c, ...), custom_call_target="tpu_custom_call" | custom-call | flops 3623878656 | bytes 12582912 | tf_op jit(solution)/shard_map/expert/pallas_call | solution.py:224
  41.7 5.6 %expert.5 = (bf16[96,2048]{1,0:T(8,128)(2,1)S(1)}, bf16[96,2048]{1,0:T(8,128)(2,1)S(1)}, bf16[192,2048]{1,0:T(8,128)(2,1)S(1)}) custom-call(bf16[96,2048]{1,0:T(8,128)(2,1)S(1)} %collective-permute-done.10.a, bf16[96,2048]{1,0:T(8,128)(2,1)S(1)} %collective-permute-done.12.b, bf16[96,2048]{1,0:T(8,128)(2,1)S(1)} %collective-permute-done.13.c, ...), custom_call_target="tpu_custom_call" | custom-call | flops 3623878656 | bytes 12582912 | tf_op jit(solution)/shard_map/expert/pallas_call | solution.py:224
  47.8 3.0 %collective-permute-done.18.b = bf16[96,2048]{1,0:T(8,128)(2,1)S(1)} collective-permute-done((bf16[96,2048]{1,0:T(8,128)(2,1)S(1)}, bf16[96,2048]{1,0:T(8,128)(2,1)S(1)}, u32[]{:S(2)}, u32[]{:S(2)}) %collective-permute-start.18) | collective-permute-done | bytes 393248 | tf_op jit(solution)/shard_map/ppermute | solution.py:265
  50.8 2.1 %collective-permute-done.11.a = bf16[96,2048]{1,0:T(8,128)(2,1)S(1)} collective-permute-done((bf16[96,2048]{1,0:T(8,128)(2,1)S(1)}, bf16[96,2048]{1,0:T(8,128)(2,1)S(1)}, u32[]{:S(2)}, u32[]{:S(2)}) %collective-permute-start.11) | collective-permute-done | bytes 393248 | tf_op jit(solution)/shard_map/ppermute | solution.py:264
  54.9 5.6 %expert.6 = (bf16[96,2048]{1,0:T(8,128)(2,1)S(1)}, bf16[96,2048]{1,0:T(8,128)(2,1)S(1)}, bf16[192,2048]{1,0:T(8,128)(2,1)S(1)}) custom-call(bf16[96,2048]{1,0:T(8,128)(2,1)S(1)} %collective-permute-done.17.a, bf16[96,2048]{1,0:T(8,128)(2,1)S(1)} %collective-permute-done.18.b, bf16[96,2048]{1,0:T(8,128)(2,1)S(1)} %collective-permute-done.19.c, ...), custom_call_target="tpu_custom_call" | custom-call | flops 3623878656 | bytes 12582912 | tf_op jit(solution)/shard_map/expert/pallas_call | solution.py:224
  60.6 1.8 %collective-permute-done.16.b = bf16[96,2048]{1,0:T(8,128)(2,1)S(1)} collective-permute-done((bf16[96,2048]{1,0:T(8,128)(2,1)S(1)}, bf16[96,2048]{1,0:T(8,128)(2,1)S(1)}, u32[]{:S(2)}, u32[]{:S(2)}) %collective-permute-start.16) | collective-permute-done | bytes 393248 | tf_op jit(solution)/shard_map/ppermute | solution.py:265
  64.1 5.6 %expert.7 = (bf16[96,2048]{1,0:T(8,128)(2,1)S(1)}, bf16[96,2048]{1,0:T(8,128)(2,1)S(1)}, bf16[192,2048]{1,0:T(8,128)(2,1)S(1)}) custom-call(bf16[96,2048]{1,0:T(8,128)(2,1)S(1)} %collective-permute-done.11.a, bf16[96,2048]{1,0:T(8,128)(2,1)S(1)} %collective-permute-done.16.b, bf16[96,2048]{1,0:T(8,128)(2,1)S(1)} %collective-permute-done.21.c, ...), custom_call_target="tpu_custom_call" | custom-call | flops 3623878656 | bytes 12582912 | tf_op jit(solution)/shard_map/expert/pallas_call | solution.py:224
  74.4 16.4 %collective-permute-done.24 = bf16[96,2048]{1,0:T(8,128)(2,1)S(1)} collective-permute-done((bf16[96,2048]{1,0:T(8,128)(2,1)S(1)}, bf16[96,2048]{1,0:T(8,128)(2,1)S(1)}, u32[]{:S(2)}, u32[]{:S(2)}) %collective-permute-start.24) | collective-permute-done | bytes 393248 | tf_op jit(solution)/shard_map/ppermute | solution.py:265
  91.0 3.6 %collective-permute-start.30 = (bf16[96,2048]{1,0:T(8,128)(2,1)S(1)}, bf16[96,2048]{1,0:T(8,128)(2,1)S(1)}, u32[]{:S(2)}, u32[]{:S(2)}) collective-permute-start(bf16[96,2048]{1,0:T(8,128)(2,1)S(1)} %add_convert_fusion.4), channel_id=1, source_target_pairs={{0,12},{1,13},{2,14},{3,15},{4,0},{5,1},{6,2},{7,3},{8,4},{9,5},{1... | collective-permute-start | bytes 1179656 | tf_op jit(solution)/shard_map/ppermute | solution.py:264
  94.6 3.8 %collective-permute-done.27 = bf16[96,2048]{1,0:T(8,128)(2,1)S(1)} collective-permute-done((bf16[96,2048]{1,0:T(8,128)(2,1)S(1)}, bf16[96,2048]{1,0:T(8,128)(2,1)S(1)}, u32[]{:S(2)}, u32[]{:S(2)}) %collective-permute-start.27) | collective-permute-done | bytes 393248 | tf_op jit(solution)/shard_map/ppermute | solution.py:265
  99.4 4.8 %collective-permute-done.30 = bf16[96,2048]{1,0:T(8,128)(2,1)S(1)} collective-permute-done((bf16[96,2048]{1,0:T(8,128)(2,1)S(1)}, bf16[96,2048]{1,0:T(8,128)(2,1)S(1)}, u32[]{:S(2)}, u32[]{:S(2)}) %collective-permute-start.30) | collective-permute-done | bytes 393248 | tf_op jit(solution)/shard_map/ppermute | solution.py:264
  104.3 4.3 %collective-permute-start.31 = (bf16[96,2048]{1,0:T(8,128)(2,1)S(1)}, bf16[96,2048]{1,0:T(8,128)(2,1)S(1)}, u32[]{:S(2)}, u32[]{:S(2)}) collective-permute-start(bf16[96,2048]{1,0:T(8,128)(2,1)S(1)} %add_convert_fusion.1), channel_id=1, source_target_pairs={{0,12},{1,13},{2,14},{3,15},{4,0},{5,1},{6,2},{7,3},{8,4},{9,5},{1... | collective-permute-start | bytes 1179656 | tf_op jit(solution)/shard_map/ppermute | solution.py:264
  108.6 4.0 %collective-permute-done.28 = bf16[96,2048]{1,0:T(8,128)(2,1)S(1)} collective-permute-done((bf16[96,2048]{1,0:T(8,128)(2,1)S(1)}, bf16[96,2048]{1,0:T(8,128)(2,1)S(1)}, u32[]{:S(2)}, u32[]{:S(2)}) %collective-permute-start.28) | collective-permute-done | bytes 393248 | tf_op jit(solution)/shard_map/ppermute | solution.py:264
  112.6 6.3 %collective-permute-done.31 = bf16[96,2048]{1,0:T(8,128)(2,1)S(1)} collective-permute-done((bf16[96,2048]{1,0:T(8,128)(2,1)S(1)}, bf16[96,2048]{1,0:T(8,128)(2,1)S(1)}, u32[]{:S(2)}, u32[]{:S(2)}) %collective-permute-start.31) | collective-permute-done | bytes 393248 | tf_op jit(solution)/shard_map/ppermute | solution.py:264
  (64 shorter events, 19.8 us)
Async XLA Ops:
  1.9 12.4 %collective-permute-start = (bf16[96,2048]{1,0:T(8,128)(2,1)}, bf16[96,2048]{1,0:T(8,128)(2,1)S(1)}, u32[]{:S(2)}, u32[]{:S(2)}) collective-permute-start(bf16[96,2048]{1,0:T(8,128)(2,1)} %a.1), channel_id=1, source_target_pairs={{0,2},{1,3},{2,0},{3,1},{4,6},{5,7},{6,4},{7,5},{8,10},{9,11},{10,... | collective-permute-start | bytes 1179656 | tf_op jit(solution)/shard_map/ppermute | solution.py:265
  5.0 16.9 %collective-permute-start.10 = (bf16[96,2048]{1,0:T(8,128)(2,1)}, bf16[96,2048]{1,0:T(8,128)(2,1)S(1)}, u32[]{:S(2)}, u32[]{:S(2)}) collective-permute-start(bf16[96,2048]{1,0:T(8,128)(2,1)} %a.1), channel_id=1, source_target_pairs={{0,4},{1,5},{2,6},{3,7},{4,8},{5,9},{6,10},{7,11},{8,12},{9,13},{1... | collective-permute-start | bytes 1179656 | tf_op jit(solution)/shard_map/ppermute | solution.py:264
  6.5 26.9 %collective-permute-start.1 = (bf16[96,2048]{1,0:T(8,128)(2,1)}, bf16[96,2048]{1,0:T(8,128)(2,1)S(1)}, u32[]{:S(2)}, u32[]{:S(2)}) collective-permute-start(bf16[96,2048]{1,0:T(8,128)(2,1)} %a.1), channel_id=1, source_target_pairs={{0,1},{1,0},{2,3},{3,2},{4,5},{5,4},{6,7},{7,6},{8,9},{9,8},{10,11... | collective-permute-start | bytes 1179656 | tf_op jit(solution)/shard_map/ppermute | solution.py:266
  14.3 19.2 %collective-permute-start.2 = (bf16[96,2048]{1,0:T(8,128)(2,1)S(1)}, bf16[96,2048]{1,0:T(8,128)(2,1)S(1)}, u32[]{:S(2)}, u32[]{:S(2)}) collective-permute-start(bf16[96,2048]{1,0:T(8,128)(2,1)S(1)} %collective-permute-done.b), channel_id=1, source_target_pairs={{0,1},{1,0},{2,3},{3,2},{4,5},{5,4},{6,7},{7,6},{8,9},{9,8},{10,11... | collective-permute-start | bytes 1179656 | tf_op jit(solution)/shard_map/ppermute | solution.py:266
  16.0 5.8 %collective-permute-start.4 = (f32[16,128]{1,0:T(8,128)S(1)}, f32[16,128]{1,0:T(8,128)S(1)}, u32[]{:S(2)}, u32[]{:S(2)}) collective-permute-start(f32[16,128]{1,0:T(8,128)S(1)} %weights.1.w0), channel_id=1, source_target_pairs={{0,1},{1,0},{2,3},{3,2},{4,5},{5,4},{6,7},{7,6},{8,9},{9,8},{10,11... | collective-permute-start | bytes 24584 | tf_op jit(solution)/shard_map/ppermute | solution.py:266
  21.9 17.3 %collective-permute-start.12 = (bf16[96,2048]{1,0:T(8,128)(2,1)S(1)}, bf16[96,2048]{1,0:T(8,128)(2,1)S(1)}, u32[]{:S(2)}, u32[]{:S(2)}) collective-permute-start(bf16[96,2048]{1,0:T(8,128)(2,1)S(1)} %collective-permute-done.10.a), channel_id=1, source_target_pairs={{0,2},{1,3},{2,0},{3,1},{4,6},{5,7},{6,4},{7,5},{8,10},{9,11},{10,... | collective-permute-start | bytes 1179656 | tf_op jit(solution)/shard_map/ppermute | solution.py:265
  23.7 5.4 %collective-permute-start.6 = (f32[8,128]{1,0:T(8,128)S(1)}, f32[8,128]{1,0:T(8,128)S(1)}, u32[]{:S(2)}, u32[]{:S(2)}) collective-permute-start(f32[8,128]{1,0:T(8,128)S(1)} %get-tuple-element.39), channel_id=1, source_target_pairs={{0,4},{1,5},{2,6},{3,7},{4,8},{5,9},{6,10},{7,11},{8,12},{9,13},{1... | collective-permute-start | bytes 12296 | tf_op jit(solution)/shard_map/ppermute | solution.py:264
  25.3 5.6 %collective-permute-start.7 = (f32[8,128]{1,0:T(8,128)S(1)}, f32[8,128]{1,0:T(8,128)S(1)}, u32[]{:S(2)}, u32[]{:S(2)}) collective-permute-start(f32[8,128]{1,0:T(8,128)S(1)} %get-tuple-element.40), channel_id=1, source_target_pairs={{0,8},{1,9},{2,10},{3,11},{4,12},{5,13},{6,14},{7,15},{8,0},{9,1},... | collective-permute-start | bytes 12296 | tf_op jit(solution)/shard_map/ppermute | solution.py:264
  30.9 10.1 %collective-permute-start.17 = (bf16[96,2048]{1,0:T(8,128)(2,1)S(1)}, bf16[96,2048]{1,0:T(8,128)(2,1)S(1)}, u32[]{:S(2)}, u32[]{:S(2)}) collective-permute-start(bf16[96,2048]{1,0:T(8,128)(2,1)S(1)} %copy-done.3), channel_id=1, source_target_pairs={{0,12},{1,13},{2,14},{3,15},{4,0},{5,1},{6,2},{7,3},{8,4},{9,5},{1... | collective-permute-start | bytes 1179656 | tf_op jit(solution)/shard_map/ppermute | solution.py:264
  33.4 8.2 %collective-permute-start.13 = (bf16[96,2048]{1,0:T(8,128)(2,1)S(1)}, bf16[96,2048]{1,0:T(8,128)(2,1)S(1)}, u32[]{:S(2)}, u32[]{:S(2)}) collective-permute-start(bf16[96,2048]{1,0:T(8,128)(2,1)S(1)} %collective-permute-done.10.a), channel_id=1, source_target_pairs={{0,1},{1,0},{2,3},{3,2},{4,5},{5,4},{6,7},{7,6},{8,9},{9,8},{10,11... | collective-permute-start | bytes 1179656 | tf_op jit(solution)/shard_map/ppermute | solution.py:266
  41.0 9.8 %collective-permute-start.18 = (bf16[96,2048]{1,0:T(8,128)(2,1)S(1)}, bf16[96,2048]{1,0:T(8,128)(2,1)S(1)}, u32[]{:S(2)}, u32[]{:S(2)}) collective-permute-start(bf16[96,2048]{1,0:T(8,128)(2,1)S(1)} %collective-permute-done.17.a), channel_id=1, source_target_pairs={{0,2},{1,3},{2,0},{3,1},{4,6},{5,7},{6,4},{7,5},{8,10},{9,11},{10,... | collective-permute-start | bytes 1179656 | tf_op jit(solution)/shard_map/ppermute | solution.py:265
  41.3 11.7 %collective-permute-start.11 = (bf16[96,2048]{1,0:T(8,128)(2,1)S(1)}, bf16[96,2048]{1,0:T(8,128)(2,1)S(1)}, u32[]{:S(2)}, u32[]{:S(2)}) collective-permute-start(bf16[96,2048]{1,0:T(8,128)(2,1)S(1)} %collective-permute-done.10.a), channel_id=1, source_target_pairs={{0,4},{1,5},{2,6},{3,7},{4,8},{5,9},{6,10},{7,11},{8,12},{9,13},{1... | collective-permute-start | bytes 1179656 | tf_op jit(solution)/shard_map/ppermute | solution.py:264
  47.3 15.1 %collective-permute-start.15 = (bf16[192,2048]{1,0:T(8,128)(2,1)S(1)}, bf16[192,2048]{1,0:T(8,128)(2,1)S(1)}, u32[]{:S(2)}, u32[]{:S(2)}) collective-permute-start(bf16[192,2048]{1,0:T(8,128)(2,1)S(1)} %get-tuple-element.50), channel_id=1, source_target_pairs={{0,1},{1,0},{2,3},{3,2},{4,5},{5,4},{6,7},{7,6},{8,9},{9,8},{10,11... | collective-permute-start | bytes 2359304 | tf_op jit(solution)/shard_map/ppermute | solution.py:266
  47.3 7.1 %collective-permute-start.19 = (bf16[96,2048]{1,0:T(8,128)(2,1)S(1)}, bf16[96,2048]{1,0:T(8,128)(2,1)S(1)}, u32[]{:S(2)}, u32[]{:S(2)}) collective-permute-start(bf16[96,2048]{1,0:T(8,128)(2,1)S(1)} %collective-permute-done.17.a), channel_id=1, source_target_pairs={{0,1},{1,0},{2,3},{3,2},{4,5},{5,4},{6,7},{7,6},{8,9},{9,8},{10,11... | collective-permute-start | bytes 1179656 | tf_op jit(solution)/shard_map/ppermute | solution.py:266
  52.9 9.4 %collective-permute-start.16 = (bf16[96,2048]{1,0:T(8,128)(2,1)S(1)}, bf16[96,2048]{1,0:T(8,128)(2,1)S(1)}, u32[]{:S(2)}, u32[]{:S(2)}) collective-permute-start(bf16[96,2048]{1,0:T(8,128)(2,1)S(1)} %collective-permute-done.11.a), channel_id=1, source_target_pairs={{0,2},{1,3},{2,0},{3,1},{4,6},{5,7},{6,4},{7,5},{8,10},{9,11},{10,... | collective-permute-start | bytes 1179656 | tf_op jit(solution)/shard_map/ppermute | solution.py:265
  54.4 15.8 %collective-permute-start.9 = (bf16[192,2048]{1,0:T(8,128)(2,1)S(1)}, bf16[192,2048]{1,0:T(8,128)(2,1)S(1)}, u32[]{:S(2)}, u32[]{:S(2)}) collective-permute-start(bf16[192,2048]{1,0:T(8,128)(2,1)S(1)} %get-tuple-element.45), channel_id=1, source_target_pairs={{0,1},{1,0},{2,3},{3,2},{4,5},{5,4},{6,7},{7,6},{8,9},{9,8},{10,11... | collective-permute-start | bytes 2359304 | tf_op jit(solution)/shard_map/ppermute | solution.py:266
  54.4 8.2 %collective-permute-start.21 = (bf16[96,2048]{1,0:T(8,128)(2,1)S(1)}, bf16[96,2048]{1,0:T(8,128)(2,1)S(1)}, u32[]{:S(2)}, u32[]{:S(2)}) collective-permute-start(bf16[96,2048]{1,0:T(8,128)(2,1)S(1)} %collective-permute-done.11.a), channel_id=1, source_target_pairs={{0,1},{1,0},{2,3},{3,2},{4,5},{5,4},{6,7},{7,6},{8,9},{9,8},{10,11... | collective-permute-start | bytes 1179656 | tf_op jit(solution)/shard_map/ppermute | solution.py:266
  70.4 29.1 %collective-permute-start.29 = (bf16[96,2048]{1,0:T(8,128)(2,1)S(1)}, bf16[96,2048]{1,0:T(8,128)(2,1)S(1)}, u32[]{:S(2)}, u32[]{:S(2)}) collective-permute-start(bf16[96,2048]{1,0:T(8,128)(2,1)S(1)} %get-tuple-element.66), channel_id=1, source_target_pairs={{0,2},{1,3},{2,0},{3,1},{4,6},{5,7},{6,4},{7,5},{8,10},{9,11},{10,... | collective-permute-start | bytes 1179656 | tf_op jit(solution)/shard_map/ppermute | solution.py:265
  72.1 18.7 %collective-permute-start.24 = (bf16[96,2048]{1,0:T(8,128)(2,1)S(1)}, bf16[96,2048]{1,0:T(8,128)(2,1)S(1)}, u32[]{:S(2)}, u32[]{:S(2)}) collective-permute-start(bf16[96,2048]{1,0:T(8,128)(2,1)S(1)} %add_convert_fusion.5), channel_id=1, source_target_pairs={{0,2},{1,3},{2,0},{3,1},{4,6},{5,7},{6,4},{7,5},{8,10},{9,11},{10,... | collective-permute-start | bytes 1179656 | tf_op jit(solution)/shard_map/ppermute | solution.py:265
  73.3 25.2 %collective-permute-start.27 = (bf16[96,2048]{1,0:T(8,128)(2,1)S(1)}, bf16[96,2048]{1,0:T(8,128)(2,1)S(1)}, u32[]{:S(2)}, u32[]{:S(2)}) collective-permute-start(bf16[96,2048]{1,0:T(8,128)(2,1)S(1)} %add_convert_fusion.3), channel_id=1, source_target_pairs={{0,2},{1,3},{2,0},{3,1},{4,6},{5,7},{6,4},{7,5},{8,10},{9,11},{10,... | collective-permute-start | bytes 1179656 | tf_op jit(solution)/shard_map/ppermute | solution.py:265
  91.0 13.2 %collective-permute-start.30 = (bf16[96,2048]{1,0:T(8,128)(2,1)S(1)}, bf16[96,2048]{1,0:T(8,128)(2,1)S(1)}, u32[]{:S(2)}, u32[]{:S(2)}) collective-permute-start(bf16[96,2048]{1,0:T(8,128)(2,1)S(1)} %add_convert_fusion.4), channel_id=1, source_target_pairs={{0,12},{1,13},{2,14},{3,15},{4,0},{5,1},{6,2},{7,3},{8,4},{9,5},{1... | collective-permute-start | bytes 1179656 | tf_op jit(solution)/shard_map/ppermute | solution.py:264
  98.6 14.0 %collective-permute-start.28 = (bf16[96,2048]{1,0:T(8,128)(2,1)S(1)}, bf16[96,2048]{1,0:T(8,128)(2,1)S(1)}, u32[]{:S(2)}, u32[]{:S(2)}) collective-permute-start(bf16[96,2048]{1,0:T(8,128)(2,1)S(1)} %add_convert_fusion.2), channel_id=1, source_target_pairs={{0,4},{1,5},{2,6},{3,7},{4,8},{5,9},{6,10},{7,11},{8,12},{9,13},{1... | collective-permute-start | bytes 1179656 | tf_op jit(solution)/shard_map/ppermute | solution.py:264
  98.8 13.8 %collective-permute-start.25 = (bf16[96,2048]{1,0:T(8,128)(2,1)S(1)}, bf16[96,2048]{1,0:T(8,128)(2,1)S(1)}, u32[]{:S(2)}, u32[]{:S(2)}) collective-permute-start(bf16[96,2048]{1,0:T(8,128)(2,1)S(1)} %add_convert_fusion.7), channel_id=1, source_target_pairs={{0,2},{1,3},{2,0},{3,1},{4,6},{5,7},{6,4},{7,5},{8,10},{9,11},{10,... | collective-permute-start | bytes 1179656 | tf_op jit(solution)/shard_map/ppermute | solution.py:265
  104.3 14.6 %collective-permute-start.31 = (bf16[96,2048]{1,0:T(8,128)(2,1)S(1)}, bf16[96,2048]{1,0:T(8,128)(2,1)S(1)}, u32[]{:S(2)}, u32[]{:S(2)}) collective-permute-start(bf16[96,2048]{1,0:T(8,128)(2,1)S(1)} %add_convert_fusion.1), channel_id=1, source_target_pairs={{0,12},{1,13},{2,14},{3,15},{4,0},{5,1},{6,2},{7,3},{8,4},{9,5},{1... | collective-permute-start | bytes 1179656 | tf_op jit(solution)/shard_map/ppermute | solution.py:264
  (12 other events, 68.3 us)

commit v3 on v2

--- a/solution.py
+++ b/solution.py
@@ -297,7 +297,9 @@
         name="weights",
     )(lengths, hbm(expert_ids.T), hbm(gate_probs.T))
     sent = after(tokens, own_w)
+    s1 = over_ring(sent, 1)
     y_w = over_y(own_w)
+    y_own = over_y(after(tokens, y_w))
     columns = pl.pallas_call(
         column_kernel,
         in_specs=[vmem] * 4,
@@ -305,12 +307,12 @@
         out_shape=[jax.ShapeDtypeStruct((8, lanes), jnp.float32)] * ring,
         compiler_params=small,
         name="columns",
-    )(after(own_w, matrices[0]), y_w, over_core(own_w), over_core(y_w))
-    s1, s3 = over_ring(sent, 1), over_ring(sent, 3)
-    s1 = after(s1, columns[0])
+    )(own_w, y_w, over_core(own_w), over_core(y_w))
     columns = [over_ring(column, k) for k, column in enumerate(columns)]
-    s3 = after(s3, *columns[1:])
+    s1 = after(s1, y_own, *columns[1:])
     s2 = over_ring(s1, 1)
+    s3 = over_ring(s2, 1)
+    y1, y2, y3 = over_y(s1), over_y(s2), over_y(s3)
     weight = pl.pallas_call(
         functools.partial(rank_kernel, spare_blocks),
         in_specs=[smem, smem] + [vmem] * ring,
@@ -328,24 +330,24 @@
         cd = over_core(cd)
         return f32(a) + f32(cd[:tok_rows]), bf16(f32(b) + f32(cd[tok_rows:]))
 
-    y_own = over_y(sent)
-    y1, y3 = over_y(s1), over_y(s3)
-    p0 = expert(0, tokens, y_own, over_core(sent), over_core(y_own))
-    y1 = after(y1, p0[0])
-    p1 = expert(1, s1, y1, over_core(s1), over_core(y1))
-    y3 = after(y3, p1[0])
-    p3 = expert(3, s3, y3, over_core(s3), over_core(y3))
-    y2 = after(over_y(s2), p3[0])
-    a1, b1 = merge_core(*p1)
-    p2 = expert(2, after(s2, b1), y2, over_core(s2), over_core(y2))
-
-    (a2, b2), (a3, b3), (a0, b0) = merge_core(*p2), merge_core(*p3), merge_core(*p0)
-    block1 = after(a1, b2) + f32(over_y(b1))
-    block2 = bf16(a2 + f32(over_y(b2)))
+    y1 = after(y1, matrices[0], weight)
+    p1 = expert(1, after(s1, s2), y1, over_core(s1), over_core(y1))
+    y2 = after(y2, p1[0])
+    p2 = expert(2, after(s2, s3), y2, over_core(s2), over_core(y2))
+    y3 = after(y3, p2[0])
+    a2, b2 = merge_core(p2[0], p2[1], after(p2[2], y3))
+    p3 = expert(3, after(s3, b2), y3, over_core(s3), over_core(y3))
+
+    (a1, b1), (a3, b3) = map(lambda p: merge_core(*p), (p1, p3))
+    block2 = bf16(a2 + f32(after(over_y(b2), p3[0])))
     hop = over_ring(block2, ring - 1)
-    block3 = bf16(a3 + f32(over_y(after(b3, b2))))
-    block0 = a0 + f32(over_y(after(b0, block2)))
+    own, y_own = after(tokens, b2), after(y_own, b2)
+    p0 = expert(0, after(own, block2, b3), y_own, over_core(own), over_core(y_own))
+    a0, b0 = merge_core(*p0)
+    block1 = a1 + f32(after(over_y(after(b1, b2)), block2, b3, p0[0]))
+    block3 = bf16(a3 + f32(over_y(b3)))
     hop = over_ring(bf16(block1 + f32(hop)), ring - 1)
+    block0 = a0 + f32(over_y(after(b0, b3)))
     return bf16(block0 + f32(over_ring(block3, 1)) + f32(hop))
 
 

time: 120 us -> 97.5 us (0.81)
  waiting for transfers between devices: 57.5 us -> 35 us
    ppermute x9, waiting for transfers between devices: 34.4 us -> 11.9 us  [dense_layer(): over_y = lambda a: lax.ppermute(a, 'ep', y_pairs)]
  transfers between devices with their start and end apart: 32 -> 32, of which waited for: 16 -> 18; matrix products, arithmetic and copies ran while one was open for 1% -> 1% of each run, Pallas kernels for 23% -> 28%
where the time goes in v3:
time: 97.5 us; the launch traced here: 97.3 us
  waiting for transfers between devices  35 us (36%)
  starting transfers between devices  31.2 us (32%)
  Pallas kernels  28.2 us (29%)
  other arithmetic  1.97 us (2%)
    pallas_call x4, Pallas kernels, expert_rows(): pl.pallas_call(functools.partial(expert_kernel, slot), in_specs=[anywhere...  22.4 us
    ppermute x9, waiting for transfers between devices, dense_layer(): over_ring = lambda a, k: lax.ppermute(a, 'ep', ring_pairs(k)) if k else a  19.8 us
    ppermute x9, starting transfers between devices, dense_layer(): over_ring = lambda a, k: lax.ppermute(a, 'ep', ring_pairs(k)) if k else a  17.2 us
    ppermute x9, waiting for transfers between devices, dense_layer(): over_y = lambda a: lax.ppermute(a, 'ep', y_pairs)  11.9 us
    ppermute x9, starting transfers between devices, dense_layer(): over_y = lambda a: lax.ppermute(a, 'ep', y_pairs)  11.6 us
    pallas_call x1, Pallas kernels, dense_layer(): pl.pallas_call(load_kernel, in_specs=[anywhere] * 3, out_specs=[vmem] * 3...  3.8 us
    ppermute x14, waiting for transfers between devices, dense_layer(): over_core = lambda a: lax.ppermute(a, 'ep', core_pairs)  3.2 us
    ppermute x14, starting transfers between devices, dense_layer(): over_core = lambda a: lax.ppermute(a, 'ep', core_pairs)  2.42 us
  transfers between devices with their start and end apart: 32, of which 18 were waited for; matrix products, arithmetic and copies ran while one was open for 1% of the time, Pallas kernels for 28%

profile of v3, /device:TPU:0, one launch (start us, length us, event | category | flops | bytes accessed | tf_op | source)
XLA Modules:
  0.0 97.3 jit_solution(8237951254298590022)
XLA Ops:
  1.9 3.0 %collective-permute-start.1 = (f32[16,128]{1,0:T(8,128)S(1)}, f32[16,128]{1,0:T(8,128)S(1)}, u32[]{:S(2)}, u32[]{:S(2)}) collective-permute-start(f32[16,128]{1,0:T(8,128)S(1)} %weights.1.w0), channel_id=1, source_target_pairs={{0,2},{1,3},{2,0},{3,1},{4,6},{5,7},{6,4},{7,5},{8,10},{9,11},{10,... | collective-permute-start | bytes 24584 | tf_op jit(solution)/shard_map/ppermute | solution.py:265
  5.0 1.6 %collective-permute-start = (bf16[96,2048]{1,0:T(8,128)(2,1)}, bf16[96,2048]{1,0:T(8,128)(2,1)S(1)}, u32[]{:S(2)}, u32[]{:S(2)}) collective-permute-start(bf16[96,2048]{1,0:T(8,128)(2,1)} %a), channel_id=1, source_target_pairs={{0,4},{1,5},{2,6},{3,7},{4,8},{5,9},{6,10},{7,11},{8,12},{9,13},{1... | collective-permute-start | bytes 1179656 | tf_op jit(solution)/shard_map/ppermute | solution.py:264
  6.6 2.0 %collective-permute-start.2 = (bf16[96,2048]{1,0:T(8,128)(2,1)}, bf16[96,2048]{1,0:T(8,128)(2,1)S(1)}, u32[]{:S(2)}, u32[]{:S(2)}) collective-permute-start(bf16[96,2048]{1,0:T(8,128)(2,1)} %a), channel_id=1, source_target_pairs={{0,2},{1,3},{2,0},{3,1},{4,6},{5,7},{6,4},{7,5},{8,10},{9,11},{10,... | collective-permute-start | bytes 1179656 | tf_op jit(solution)/shard_map/ppermute | solution.py:265
  10.0 1.6 %collective-permute-start.5 = (f32[8,128]{1,0:T(8,128)S(1)}, f32[8,128]{1,0:T(8,128)S(1)}, u32[]{:S(2)}, u32[]{:S(2)}) collective-permute-start(f32[8,128]{1,0:T(8,128)S(1)} %get-tuple-element.43), channel_id=1, source_target_pairs={{0,4},{1,5},{2,6},{3,7},{4,8},{5,9},{6,10},{7,11},{8,12},{9,13},{1... | collective-permute-start | bytes 12296 | tf_op jit(solution)/shard_map/ppermute | solution.py:264
  11.6 2.6 %collective-permute-start.6 = (f32[8,128]{1,0:T(8,128)S(1)}, f32[8,128]{1,0:T(8,128)S(1)}, u32[]{:S(2)}, u32[]{:S(2)}) collective-permute-start(f32[8,128]{1,0:T(8,128)S(1)} %get-tuple-element.44), channel_id=1, source_target_pairs={{0,8},{1,9},{2,10},{3,11},{4,12},{5,13},{6,14},{7,15},{8,0},{9,1},... | collective-permute-start | bytes 12296 | tf_op jit(solution)/shard_map/ppermute | solution.py:264
  15.5 2.4 %collective-permute-done.5.refs_1_ = f32[8,128]{1,0:T(8,128)S(1)} collective-permute-done((f32[8,128]{1,0:T(8,128)S(1)}, f32[8,128]{1,0:T(8,128)S(1)}, u32[]{:S(2)}, u32[]{:S(2)}) %collective-permute-start.5) | collective-permute-done | bytes 4128 | tf_op jit(solution)/shard_map/ppermute | solution.py:264
  18.5 1.6 %collective-permute-start.8 = (bf16[96,2048]{1,0:T(8,128)(2,1)S(1)}, bf16[96,2048]{1,0:T(8,128)(2,1)S(1)}, u32[]{:S(2)}, u32[]{:S(2)}) collective-permute-start(bf16[96,2048]{1,0:T(8,128)(2,1)S(1)} %collective-permute-done.a), channel_id=1, source_target_pairs={{0,4},{1,5},{2,6},{3,7},{4,8},{5,9},{6,10},{7,11},{8,12},{9,13},{1... | collective-permute-start | bytes 1179656 | tf_op jit(solution)/shard_map/ppermute | solution.py:264
  20.1 3.8 %load.1 = (bf16[2048,768]{1,0:T(8,128)(2,1)S(1)}, bf16[2048,768]{1,0:T(8,128)(2,1)S(1)}, bf16[768,2048]{1,0:T(8,128)(2,1)S(1)}) custom-call(bf16[2048,768]{1,0:T(8,128)(2,1)} %bitcast.7, bf16[2048,768]{1,0:T(8,128)(2,1)} %bitcast.8, bf16[768,2048]{1,0:T(8,128)(2,1)} %bitcast.9), custom_call_target="tpu_custom_call" | custom-call | tf_op jit(solution)/shard_map/load/pallas_call | solution.py:277
  24.7 3.5 %collective-permute-done.11.b = bf16[96,2048]{1,0:T(8,128)(2,1)S(1)} collective-permute-done((bf16[96,2048]{1,0:T(8,128)(2,1)S(1)}, bf16[96,2048]{1,0:T(8,128)(2,1)S(1)}, u32[]{:S(2)}, u32[]{:S(2)}) %collective-permute-start.11) | collective-permute-done | bytes 393248 | tf_op jit(solution)/shard_map/ppermute | solution.py:265
  28.2 1.9 %collective-permute-done.8.a = bf16[96,2048]{1,0:T(8,128)(2,1)S(1)} collective-permute-done((bf16[96,2048]{1,0:T(8,128)(2,1)S(1)}, bf16[96,2048]{1,0:T(8,128)(2,1)S(1)}, u32[]{:S(2)}, u32[]{:S(2)}) %collective-permute-start.8) | collective-permute-done | bytes 393248 | tf_op jit(solution)/shard_map/ppermute | solution.py:264
  30.0 1.7 %collective-permute-start.10 = (bf16[96,2048]{1,0:T(8,128)(2,1)S(1)}, bf16[96,2048]{1,0:T(8,128)(2,1)S(1)}, u32[]{:S(2)}, u32[]{:S(2)}) collective-permute-start(bf16[96,2048]{1,0:T(8,128)(2,1)S(1)} %collective-permute-done.8.a), channel_id=1, source_target_pairs={{0,2},{1,3},{2,0},{3,1},{4,6},{5,7},{6,4},{7,5},{8,10},{9,11},{10,... | collective-permute-start | bytes 1179656 | tf_op jit(solution)/shard_map/ppermute | solution.py:265
  31.7 5.7 %expert.4 = (bf16[96,2048]{1,0:T(8,128)(2,1)S(1)}, bf16[96,2048]{1,0:T(8,128)(2,1)S(1)}, bf16[192,2048]{1,0:T(8,128)(2,1)S(1)}) custom-call(bf16[96,2048]{1,0:T(8,128)(2,1)S(1)} %collective-permute-done.a, bf16[96,2048]{1,0:T(8,128)(2,1)S(1)} %collective-permute-done.11.b, bf16[96,2048]{1,0:T(8,128)(2,1)S(1)} %collective-permute-done.12.c, ...), custom_call_target="tpu_custom_call" | custom-call | flops 3623878656 | bytes 12582912 | tf_op jit(solution)/shard_map/expert/pallas_call | solution.py:224
  37.4 2.3 %collective-permute-done.10.b = bf16[96,2048]{1,0:T(8,128)(2,1)S(1)} collective-permute-done((bf16[96,2048]{1,0:T(8,128)(2,1)S(1)}, bf16[96,2048]{1,0:T(8,128)(2,1)S(1)}, u32[]{:S(2)}, u32[]{:S(2)}) %collective-permute-start.10) | collective-permute-done | bytes 393248 | tf_op jit(solution)/shard_map/ppermute | solution.py:265
  39.7 2.5 %collective-permute-done.9.a = bf16[96,2048]{1,0:T(8,128)(2,1)S(1)} collective-permute-done((bf16[96,2048]{1,0:T(8,128)(2,1)S(1)}, bf16[96,2048]{1,0:T(8,128)(2,1)S(1)}, u32[]{:S(2)}, u32[]{:S(2)}) %collective-permute-start.9) | collective-permute-done | bytes 393248 | tf_op jit(solution)/shard_map/ppermute | solution.py:264
  43.3 5.6 %expert.5 = (bf16[96,2048]{1,0:T(8,128)(2,1)S(1)}, bf16[96,2048]{1,0:T(8,128)(2,1)S(1)}, bf16[192,2048]{1,0:T(8,128)(2,1)S(1)}) custom-call(bf16[96,2048]{1,0:T(8,128)(2,1)S(1)} %collective-permute-done.8.a, bf16[96,2048]{1,0:T(8,128)(2,1)S(1)} %collective-permute-done.10.b, bf16[96,2048]{1,0:T(8,128)(2,1)S(1)} %collective-permute-done.14.c, ...), custom_call_target="tpu_custom_call" | custom-call | flops 3623878656 | bytes 12582912 | tf_op jit(solution)/shard_map/expert/pallas_call | solution.py:224
  48.9 2.4 %collective-permute-done.16.b = bf16[96,2048]{1,0:T(8,128)(2,1)S(1)} collective-permute-done((bf16[96,2048]{1,0:T(8,128)(2,1)S(1)}, bf16[96,2048]{1,0:T(8,128)(2,1)S(1)}, u32[]{:S(2)}, u32[]{:S(2)}) %collective-permute-start.16) | collective-permute-done | bytes 393248 | tf_op jit(solution)/shard_map/ppermute | solution.py:265
  55.8 5.6 %expert.6 = (bf16[96,2048]{1,0:T(8,128)(2,1)S(1)}, bf16[96,2048]{1,0:T(8,128)(2,1)S(1)}, bf16[192,2048]{1,0:T(8,128)(2,1)S(1)}) custom-call(bf16[96,2048]{1,0:T(8,128)(2,1)S(1)} %collective-permute-done.9.a, bf16[96,2048]{1,0:T(8,128)(2,1)S(1)} %collective-permute-done.16.b, bf16[96,2048]{1,0:T(8,128)(2,1)S(1)} %collective-permute-done.19.c, ...), custom_call_target="tpu_custom_call" | custom-call | flops 3623878656 | bytes 12582912 | tf_op jit(solution)/shard_map/expert/pallas_call | solution.py:224
  63.3 1.6 %collective-permute-done.18 = bf16[96,2048]{1,0:T(8,128)(2,1)S(1)} collective-permute-done((bf16[96,2048]{1,0:T(8,128)(2,1)S(1)}, bf16[96,2048]{1,0:T(8,128)(2,1)S(1)}, u32[]{:S(2)}, u32[]{:S(2)}) %collective-permute-start.18) | collective-permute-done | bytes 393248 | tf_op jit(solution)/shard_map/ppermute | solution.py:265
  65.0 2.7 %collective-permute-start.30 = (bf16[96,2048]{1,0:T(8,128)(2,1)S(1)}, bf16[96,2048]{1,0:T(8,128)(2,1)S(1)}, u32[]{:S(2)}, u32[]{:S(2)}) collective-permute-start(bf16[96,2048]{1,0:T(8,128)(2,1)S(1)} %add_convert_fusion.6), channel_id=1, source_target_pairs={{0,12},{1,13},{2,14},{3,15},{4,0},{5,1},{6,2},{7,3},{8,4},{9,5},{1... | collective-permute-start | bytes 1179656 | tf_op jit(solution)/shard_map/ppermute | solution.py:264
  68.4 5.6 %expert.7 = (bf16[96,2048]{1,0:T(8,128)(2,1)S(1)}, bf16[96,2048]{1,0:T(8,128)(2,1)S(1)}, bf16[192,2048]{1,0:T(8,128)(2,1)S(1)}) custom-call(bf16[96,2048]{1,0:T(8,128)(2,1)S(1)} %copy-done.3, bf16[96,2048]{1,0:T(8,128)(2,1)S(1)} %collective-permute-done.2.b, bf16[96,2048]{1,0:T(8,128)(2,1)S(1)} %collective-permute-done.22.c, ...), custom_call_target="tpu_custom_call" | custom-call | flops 3623878656 | bytes 12582912 | tf_op jit(solution)/shard_map/expert/pallas_call | solution.py:224
  75.8 4.3 %collective-permute-start.31 = (bf16[96,2048]{1,0:T(8,128)(2,1)S(1)}, bf16[96,2048]{1,0:T(8,128)(2,1)S(1)}, u32[]{:S(2)}, u32[]{:S(2)}) collective-permute-start(bf16[96,2048]{1,0:T(8,128)(2,1)S(1)} %add_convert_fusion.1), channel_id=1, source_target_pairs={{0,12},{1,13},{2,14},{3,15},{4,0},{5,1},{6,2},{7,3},{8,4},{9,5},{1... | collective-permute-start | bytes 1179656 | tf_op jit(solution)/shard_map/ppermute | solution.py:264
  80.1 2.0 %collective-permute-done.26 = bf16[96,2048]{1,0:T(8,128)(2,1)S(1)} collective-permute-done((bf16[96,2048]{1,0:T(8,128)(2,1)S(1)}, bf16[96,2048]{1,0:T(8,128)(2,1)S(1)}, u32[]{:S(2)}, u32[]{:S(2)}) %collective-permute-start.26) | collective-permute-done | bytes 393248 | tf_op jit(solution)/shard_map/ppermute | solution.py:265
  84.5 5.3 %collective-permute-done.31 = bf16[96,2048]{1,0:T(8,128)(2,1)S(1)} collective-permute-done((bf16[96,2048]{1,0:T(8,128)(2,1)S(1)}, bf16[96,2048]{1,0:T(8,128)(2,1)S(1)}, u32[]{:S(2)}, u32[]{:S(2)}) %collective-permute-start.31) | collective-permute-done | bytes 393248 | tf_op jit(solution)/shard_map/ppermute | solution.py:264
  89.7 6.5 %collective-permute-done.27 = bf16[96,2048]{1,0:T(8,128)(2,1)S(1)} collective-permute-done((bf16[96,2048]{1,0:T(8,128)(2,1)S(1)}, bf16[96,2048]{1,0:T(8,128)(2,1)S(1)}, u32[]{:S(2)}, u32[]{:S(2)}) %collective-permute-start.27) | collective-permute-done | bytes 393248 | tf_op jit(solution)/shard_map/ppermute | solution.py:264
  (64 shorter events, 19.6 us)
Async XLA Ops:
  1.9 4.7 %collective-permute-start.1 = (f32[16,128]{1,0:T(8,128)S(1)}, f32[16,128]{1,0:T(8,128)S(1)}, u32[]{:S(2)}, u32[]{:S(2)}) collective-permute-start(f32[16,128]{1,0:T(8,128)S(1)} %weights.1.w0), channel_id=1, source_target_pairs={{0,2},{1,3},{2,0},{3,1},{4,6},{5,7},{6,4},{7,5},{8,10},{9,11},{10,... | collective-permute-start | bytes 24584 | tf_op jit(solution)/shard_map/ppermute | solution.py:265
  5.0 13.0 %collective-permute-start = (bf16[96,2048]{1,0:T(8,128)(2,1)}, bf16[96,2048]{1,0:T(8,128)(2,1)S(1)}, u32[]{:S(2)}, u32[]{:S(2)}) collective-permute-start(bf16[96,2048]{1,0:T(8,128)(2,1)} %a), channel_id=1, source_target_pairs={{0,4},{1,5},{2,6},{3,7},{4,8},{5,9},{6,10},{7,11},{8,12},{9,13},{1... | collective-permute-start | bytes 1179656 | tf_op jit(solution)/shard_map/ppermute | solution.py:264
  6.6 11.3 %collective-permute-start.2 = (bf16[96,2048]{1,0:T(8,128)(2,1)}, bf16[96,2048]{1,0:T(8,128)(2,1)S(1)}, u32[]{:S(2)}, u32[]{:S(2)}) collective-permute-start(bf16[96,2048]{1,0:T(8,128)(2,1)} %a), channel_id=1, source_target_pairs={{0,2},{1,3},{2,0},{3,1},{4,6},{5,7},{6,4},{7,5},{8,10},{9,11},{10,... | collective-permute-start | bytes 1179656 | tf_op jit(solution)/shard_map/ppermute | solution.py:265
  10.0 7.9 %collective-permute-start.5 = (f32[8,128]{1,0:T(8,128)S(1)}, f32[8,128]{1,0:T(8,128)S(1)}, u32[]{:S(2)}, u32[]{:S(2)}) collective-permute-start(f32[8,128]{1,0:T(8,128)S(1)} %get-tuple-element.43), channel_id=1, source_target_pairs={{0,4},{1,5},{2,6},{3,7},{4,8},{5,9},{6,10},{7,11},{8,12},{9,13},{1... | collective-permute-start | bytes 12296 | tf_op jit(solution)/shard_map/ppermute | solution.py:264
  11.6 6.3 %collective-permute-start.6 = (f32[8,128]{1,0:T(8,128)S(1)}, f32[8,128]{1,0:T(8,128)S(1)}, u32[]{:S(2)}, u32[]{:S(2)}) collective-permute-start(f32[8,128]{1,0:T(8,128)S(1)} %get-tuple-element.44), channel_id=1, source_target_pairs={{0,8},{1,9},{2,10},{3,11},{4,12},{5,13},{6,14},{7,15},{8,0},{9,1},... | collective-permute-start | bytes 12296 | tf_op jit(solution)/shard_map/ppermute | solution.py:264
  17.9 10.2 %collective-permute-start.11 = (bf16[96,2048]{1,0:T(8,128)(2,1)S(1)}, bf16[96,2048]{1,0:T(8,128)(2,1)S(1)}, u32[]{:S(2)}, u32[]{:S(2)}) collective-permute-start(bf16[96,2048]{1,0:T(8,128)(2,1)S(1)} %collective-permute-done.a), channel_id=1, source_target_pairs={{0,2},{1,3},{2,0},{3,1},{4,6},{5,7},{6,4},{7,5},{8,10},{9,11},{10,... | collective-permute-start | bytes 1179656 | tf_op jit(solution)/shard_map/ppermute | solution.py:265
  18.5 11.5 %collective-permute-start.8 = (bf16[96,2048]{1,0:T(8,128)(2,1)S(1)}, bf16[96,2048]{1,0:T(8,128)(2,1)S(1)}, u32[]{:S(2)}, u32[]{:S(2)}) collective-permute-start(bf16[96,2048]{1,0:T(8,128)(2,1)S(1)} %collective-permute-done.a), channel_id=1, source_target_pairs={{0,4},{1,5},{2,6},{3,7},{4,8},{5,9},{6,10},{7,11},{8,12},{9,13},{1... | collective-permute-start | bytes 1179656 | tf_op jit(solution)/shard_map/ppermute | solution.py:264
  24.6 7.1 %collective-permute-start.12 = (bf16[96,2048]{1,0:T(8,128)(2,1)S(1)}, bf16[96,2048]{1,0:T(8,128)(2,1)S(1)}, u32[]{:S(2)}, u32[]{:S(2)}) collective-permute-start(bf16[96,2048]{1,0:T(8,128)(2,1)S(1)} %collective-permute-done.a), channel_id=1, source_target_pairs={{0,1},{1,0},{2,3},{3,2},{4,5},{5,4},{6,7},{7,6},{8,9},{9,8},{10,11... | collective-permute-start | bytes 1179656 | tf_op jit(solution)/shard_map/ppermute | solution.py:266
  30.0 9.7 %collective-permute-start.10 = (bf16[96,2048]{1,0:T(8,128)(2,1)S(1)}, bf16[96,2048]{1,0:T(8,128)(2,1)S(1)}, u32[]{:S(2)}, u32[]{:S(2)}) collective-permute-start(bf16[96,2048]{1,0:T(8,128)(2,1)S(1)} %collective-permute-done.8.a), channel_id=1, source_target_pairs={{0,2},{1,3},{2,0},{3,1},{4,6},{5,7},{6,4},{7,5},{8,10},{9,11},{10,... | collective-permute-start | bytes 1179656 | tf_op jit(solution)/shard_map/ppermute | solution.py:265
  31.7 10.5 %collective-permute-start.9 = (bf16[96,2048]{1,0:T(8,128)(2,1)S(1)}, bf16[96,2048]{1,0:T(8,128)(2,1)S(1)}, u32[]{:S(2)}, u32[]{:S(2)}) collective-permute-start(bf16[96,2048]{1,0:T(8,128)(2,1)S(1)} %collective-permute-done.8.a), channel_id=1, source_target_pairs={{0,4},{1,5},{2,6},{3,7},{4,8},{5,9},{6,10},{7,11},{8,12},{9,13},{1... | collective-permute-start | bytes 1179656 | tf_op jit(solution)/shard_map/ppermute | solution.py:264
  31.7 11.5 %collective-permute-start.14 = (bf16[96,2048]{1,0:T(8,128)(2,1)S(1)}, bf16[96,2048]{1,0:T(8,128)(2,1)S(1)}, u32[]{:S(2)}, u32[]{:S(2)}) collective-permute-start(bf16[96,2048]{1,0:T(8,128)(2,1)S(1)} %collective-permute-done.8.a), channel_id=1, source_target_pairs={{0,1},{1,0},{2,3},{3,2},{4,5},{5,4},{6,7},{7,6},{8,9},{9,8},{10,11... | collective-permute-start | bytes 1179656 | tf_op jit(solution)/shard_map/ppermute | solution.py:266
  42.2 9.0 %collective-permute-start.16 = (bf16[96,2048]{1,0:T(8,128)(2,1)S(1)}, bf16[96,2048]{1,0:T(8,128)(2,1)S(1)}, u32[]{:S(2)}, u32[]{:S(2)}) collective-permute-start(bf16[96,2048]{1,0:T(8,128)(2,1)S(1)} %collective-permute-done.9.a), channel_id=1, source_target_pairs={{0,2},{1,3},{2,0},{3,1},{4,6},{5,7},{6,4},{7,5},{8,10},{9,11},{10,... | collective-permute-start | bytes 1179656 | tf_op jit(solution)/shard_map/ppermute | solution.py:265
  51.2 10.3 %collective-permute-start.28 = (bf16[192,2048]{1,0:T(8,128)(2,1)S(1)}, bf16[192,2048]{1,0:T(8,128)(2,1)S(1)}, u32[]{:S(2)}, u32[]{:S(2)}) collective-permute-start(bf16[192,2048]{1,0:T(8,128)(2,1)S(1)} %get-tuple-element.73), channel_id=1, source_target_pairs={{0,1},{1,0},{2,3},{3,2},{4,5},{5,4},{6,7},{7,6},{8,9},{9,8},{10,11... | collective-permute-start | bytes 2359304 | tf_op jit(solution)/shard_map/ppermute | solution.py:266
  53.6 11.2 %collective-permute-start.18 = (bf16[96,2048]{1,0:T(8,128)(2,1)S(1)}, bf16[96,2048]{1,0:T(8,128)(2,1)S(1)}, u32[]{:S(2)}, u32[]{:S(2)}) collective-permute-start(bf16[96,2048]{1,0:T(8,128)(2,1)S(1)} %add_convert_fusion.7), channel_id=1, source_target_pairs={{0,2},{1,3},{2,0},{3,1},{4,6},{5,7},{6,4},{7,5},{8,10},{9,11},{10,... | collective-permute-start | bytes 1179656 | tf_op jit(solution)/shard_map/ppermute | solution.py:265
  61.4 6.3 %collective-permute-start.21 = (bf16[192,2048]{1,0:T(8,128)(2,1)S(1)}, bf16[192,2048]{1,0:T(8,128)(2,1)S(1)}, u32[]{:S(2)}, u32[]{:S(2)}) collective-permute-start(bf16[192,2048]{1,0:T(8,128)(2,1)S(1)} %get-tuple-element.66), channel_id=1, source_target_pairs={{0,1},{1,0},{2,3},{3,2},{4,5},{5,4},{6,7},{7,6},{8,9},{9,8},{10,11... | collective-permute-start | bytes 2359304 | tf_op jit(solution)/shard_map/ppermute | solution.py:266
  61.7 6.7 %collective-permute-start.23 = (bf16[96,2048]{1,0:T(8,128)(2,1)S(1)}, bf16[96,2048]{1,0:T(8,128)(2,1)S(1)}, u32[]{:S(2)}, u32[]{:S(2)}) collective-permute-start(bf16[96,2048]{1,0:T(8,128)(2,1)S(1)} %collective-permute-done.2.b), channel_id=1, source_target_pairs={{0,1},{1,0},{2,3},{3,2},{4,5},{5,4},{6,7},{7,6},{8,9},{9,8},{10,11... | collective-permute-start | bytes 1179656 | tf_op jit(solution)/shard_map/ppermute | solution.py:266
  62.1 6.3 %collective-permute-start.22 = (bf16[96,2048]{1,0:T(8,128)(2,1)S(1)}, bf16[96,2048]{1,0:T(8,128)(2,1)S(1)}, u32[]{:S(2)}, u32[]{:S(2)}) collective-permute-start(bf16[96,2048]{1,0:T(8,128)(2,1)S(1)} %copy-done.3), channel_id=1, source_target_pairs={{0,1},{1,0},{2,3},{3,2},{4,5},{5,4},{6,7},{7,6},{8,9},{9,8},{10,11... | collective-permute-start | bytes 1179656 | tf_op jit(solution)/shard_map/ppermute | solution.py:266
  62.3 11.9 %collective-permute-start.29 = (bf16[96,2048]{1,0:T(8,128)(2,1)S(1)}, bf16[96,2048]{1,0:T(8,128)(2,1)S(1)}, u32[]{:S(2)}, u32[]{:S(2)}) collective-permute-start(bf16[96,2048]{1,0:T(8,128)(2,1)S(1)} %add_convert_fusion.2), channel_id=1, source_target_pairs={{0,2},{1,3},{2,0},{3,1},{4,6},{5,7},{6,4},{7,5},{8,10},{9,11},{10,... | collective-permute-start | bytes 1179656 | tf_op jit(solution)/shard_map/ppermute | solution.py:265
  65.0 10.6 %collective-permute-start.30 = (bf16[96,2048]{1,0:T(8,128)(2,1)S(1)}, bf16[96,2048]{1,0:T(8,128)(2,1)S(1)}, u32[]{:S(2)}, u32[]{:S(2)}) collective-permute-start(bf16[96,2048]{1,0:T(8,128)(2,1)S(1)} %add_convert_fusion.6), channel_id=1, source_target_pairs={{0,12},{1,13},{2,14},{3,15},{4,0},{5,1},{6,2},{7,3},{8,4},{9,5},{1... | collective-permute-start | bytes 1179656 | tf_op jit(solution)/shard_map/ppermute | solution.py:264
  67.8 14.3 %collective-permute-start.26 = (bf16[96,2048]{1,0:T(8,128)(2,1)S(1)}, bf16[96,2048]{1,0:T(8,128)(2,1)S(1)}, u32[]{:S(2)}, u32[]{:S(2)}) collective-permute-start(bf16[96,2048]{1,0:T(8,128)(2,1)S(1)} %add_convert_fusion.5), channel_id=1, source_target_pairs={{0,2},{1,3},{2,0},{3,1},{4,6},{5,7},{6,4},{7,5},{8,10},{9,11},{10,... | collective-permute-start | bytes 1179656 | tf_op jit(solution)/shard_map/ppermute | solution.py:265
  74.0 9.8 %collective-permute-start.24 = (bf16[192,2048]{1,0:T(8,128)(2,1)S(1)}, bf16[192,2048]{1,0:T(8,128)(2,1)S(1)}, u32[]{:S(2)}, u32[]{:S(2)}) collective-permute-start(bf16[192,2048]{1,0:T(8,128)(2,1)S(1)} %get-tuple-element.70), channel_id=1, source_target_pairs={{0,1},{1,0},{2,3},{3,2},{4,5},{5,4},{6,7},{7,6},{8,9},{9,8},{10,11... | collective-permute-start | bytes 2359304 | tf_op jit(solution)/shard_map/ppermute | solution.py:266
  75.8 13.9 %collective-permute-start.31 = (bf16[96,2048]{1,0:T(8,128)(2,1)S(1)}, bf16[96,2048]{1,0:T(8,128)(2,1)S(1)}, u32[]{:S(2)}, u32[]{:S(2)}) collective-permute-start(bf16[96,2048]{1,0:T(8,128)(2,1)S(1)} %add_convert_fusion.1), channel_id=1, source_target_pairs={{0,12},{1,13},{2,14},{3,15},{4,0},{5,1},{6,2},{7,3},{8,4},{9,5},{1... | collective-permute-start | bytes 1179656 | tf_op jit(solution)/shard_map/ppermute | solution.py:264
  82.2 14.0 %collective-permute-start.27 = (bf16[96,2048]{1,0:T(8,128)(2,1)S(1)}, bf16[96,2048]{1,0:T(8,128)(2,1)S(1)}, u32[]{:S(2)}, u32[]{:S(2)}) collective-permute-start(bf16[96,2048]{1,0:T(8,128)(2,1)S(1)} %add_convert_fusion.3), channel_id=1, source_target_pairs={{0,4},{1,5},{2,6},{3,7},{4,8},{5,9},{6,10},{7,11},{8,12},{9,13},{1... | collective-permute-start | bytes 1179656 | tf_op jit(solution)/shard_map/ppermute | solution.py:264
  83.9 12.3 %collective-permute-start.25 = (bf16[96,2048]{1,0:T(8,128)(2,1)S(1)}, bf16[96,2048]{1,0:T(8,128)(2,1)S(1)}, u32[]{:S(2)}, u32[]{:S(2)}) collective-permute-start(bf16[96,2048]{1,0:T(8,128)(2,1)S(1)} %add_convert_fusion.4), channel_id=1, source_target_pairs={{0,2},{1,3},{2,0},{3,1},{4,6},{5,7},{6,4},{7,5},{8,10},{9,11},{10,... | collective-permute-start | bytes 1179656 | tf_op jit(solution)/shard_map/ppermute | solution.py:265
  (12 other events, 39.9 us)

commit v4 on v3

--- a/solution.py
+++ b/solution.py
@@ -97,10 +97,11 @@
     return mixed_sum.astype(jnp.bfloat16)
 
 
-def weight_kernel(lengths, ids_ref, probs_ref, out, ids, probs, sems):
+def weight_kernel(lengths_ref, ids_ref, probs_ref, out, lengths, ids, probs, sems):
     copies = [
         pltpu.make_async_copy(ids_ref, ids, sems.at[0]),
         pltpu.make_async_copy(probs_ref, probs, sems.at[1]),
+        pltpu.make_async_copy(lengths_ref, lengths, sems.at[2]),
     ]
     for copy in copies:
         copy.start()
@@ -285,17 +286,18 @@
     )(*matrices)
     own_w = pl.pallas_call(
         weight_kernel,
-        in_specs=[smem, anywhere, anywhere],
+        in_specs=[anywhere] * 3,
         out_specs=vmem,
         out_shape=jax.ShapeDtypeStruct((devices, lanes), jnp.float32),
         scratch_shapes=[
+            pltpu.SMEM(lengths.shape, jnp.int32),
             pltpu.VMEM(expert_ids.shape[::-1], jnp.int32),
             pltpu.VMEM(gate_probs.shape[::-1], jnp.float32),
-            pltpu.SemaphoreType.DMA((2,)),
+            pltpu.SemaphoreType.DMA((3,)),
         ],
         compiler_params=small,
         name="weights",
-    )(lengths, hbm(expert_ids.T), hbm(gate_probs.T))
+    )(hbm(lengths), hbm(expert_ids.T), hbm(gate_probs.T))
     sent = after(tokens, own_w)
     s1 = over_ring(sent, 1)
     y_w = over_y(own_w)

time: 97.5 us -> 96.4 us (0.989)
  no operation moved by 1% of the time
where the time goes in v4:
time: 96.4 us; the launch traced here: 96.2 us
  waiting for transfers between devices  35 us (36%)
  starting transfers between devices  31.2 us (32%)
  Pallas kernels  27.8 us (29%)
  other arithmetic  1.97 us (2%)
    pallas_call x4, Pallas kernels, expert_rows(): pl.pallas_call(functools.partial(expert_kernel, slot), in_specs=[anywhere...  22.4 us
    ppermute x9, waiting for transfers between devices, dense_layer(): over_ring = lambda a, k: lax.ppermute(a, 'ep', ring_pairs(k)) if k else a  19.8 us
    ppermute x9, starting transfers between devices, dense_layer(): over_ring = lambda a, k: lax.ppermute(a, 'ep', ring_pairs(k)) if k else a  17.2 us
    ppermute x9, waiting for transfers between devices, dense_layer(): over_y = lambda a: lax.ppermute(a, 'ep', y_pairs)  11.9 us
    ppermute x9, starting transfers between devices, dense_layer(): over_y = lambda a: lax.ppermute(a, 'ep', y_pairs)  11.6 us
    pallas_call x1, Pallas kernels, dense_layer(): pl.pallas_call(load_kernel, in_specs=[anywhere] * 3, out_specs=[vmem] * 3...  3.8 us
    ppermute x14, waiting for transfers between devices, dense_layer(): over_core = lambda a: lax.ppermute(a, 'ep', core_pairs)  3.2 us
    ppermute x14, starting transfers between devices, dense_layer(): over_core = lambda a: lax.ppermute(a, 'ep', core_pairs)  2.42 us
  transfers between devices with their start and end apart: 32, of which 18 were waited for; matrix products, arithmetic and copies ran while one was open for 1% of the time, Pallas kernels for 28%

profile of v4, /device:TPU:0, one launch (start us, length us, event | category | flops | bytes accessed | tf_op | source)
XLA Modules:
  0.0 96.2 jit_solution(1253879093079549515)
XLA Ops:
  0.8 3.0 %collective-permute-start.1 = (f32[16,128]{1,0:T(8,128)S(1)}, f32[16,128]{1,0:T(8,128)S(1)}, u32[]{:S(2)}, u32[]{:S(2)}) collective-permute-start(f32[16,128]{1,0:T(8,128)S(1)} %weights.1.w0), channel_id=1, source_target_pairs={{0,2},{1,3},{2,0},{3,1},{4,6},{5,7},{6,4},{7,5},{8,10},{9,11},{10,... | collective-permute-start | bytes 24584 | tf_op jit(solution)/shard_map/ppermute | solution.py:266
  3.9 1.6 %collective-permute-start = (bf16[96,2048]{1,0:T(8,128)(2,1)}, bf16[96,2048]{1,0:T(8,128)(2,1)S(1)}, u32[]{:S(2)}, u32[]{:S(2)}) collective-permute-start(bf16[96,2048]{1,0:T(8,128)(2,1)} %a), channel_id=1, source_target_pairs={{0,4},{1,5},{2,6},{3,7},{4,8},{5,9},{6,10},{7,11},{8,12},{9,13},{1... | collective-permute-start | bytes 1179656 | tf_op jit(solution)/shard_map/ppermute | solution.py:265
  5.5 2.0 %collective-permute-start.2 = (bf16[96,2048]{1,0:T(8,128)(2,1)}, bf16[96,2048]{1,0:T(8,128)(2,1)S(1)}, u32[]{:S(2)}, u32[]{:S(2)}) collective-permute-start(bf16[96,2048]{1,0:T(8,128)(2,1)} %a), channel_id=1, source_target_pairs={{0,2},{1,3},{2,0},{3,1},{4,6},{5,7},{6,4},{7,5},{8,10},{9,11},{10,... | collective-permute-start | bytes 1179656 | tf_op jit(solution)/shard_map/ppermute | solution.py:266
  8.9 1.6 %collective-permute-start.5 = (f32[8,128]{1,0:T(8,128)S(1)}, f32[8,128]{1,0:T(8,128)S(1)}, u32[]{:S(2)}, u32[]{:S(2)}) collective-permute-start(f32[8,128]{1,0:T(8,128)S(1)} %get-tuple-element.43), channel_id=1, source_target_pairs={{0,4},{1,5},{2,6},{3,7},{4,8},{5,9},{6,10},{7,11},{8,12},{9,13},{1... | collective-permute-start | bytes 12296 | tf_op jit(solution)/shard_map/ppermute | solution.py:265
  10.5 2.6 %collective-permute-start.6 = (f32[8,128]{1,0:T(8,128)S(1)}, f32[8,128]{1,0:T(8,128)S(1)}, u32[]{:S(2)}, u32[]{:S(2)}) collective-permute-start(f32[8,128]{1,0:T(8,128)S(1)} %get-tuple-element.44), channel_id=1, source_target_pairs={{0,8},{1,9},{2,10},{3,11},{4,12},{5,13},{6,14},{7,15},{8,0},{9,1},... | collective-permute-start | bytes 12296 | tf_op jit(solution)/shard_map/ppermute | solution.py:265
  14.5 2.4 %collective-permute-done.5.refs_1_ = f32[8,128]{1,0:T(8,128)S(1)} collective-permute-done((f32[8,128]{1,0:T(8,128)S(1)}, f32[8,128]{1,0:T(8,128)S(1)}, u32[]{:S(2)}, u32[]{:S(2)}) %collective-permute-start.5) | collective-permute-done | bytes 4128 | tf_op jit(solution)/shard_map/ppermute | solution.py:265
  17.4 1.6 %collective-permute-start.8 = (bf16[96,2048]{1,0:T(8,128)(2,1)S(1)}, bf16[96,2048]{1,0:T(8,128)(2,1)S(1)}, u32[]{:S(2)}, u32[]{:S(2)}) collective-permute-start(bf16[96,2048]{1,0:T(8,128)(2,1)S(1)} %collective-permute-done.a), channel_id=1, source_target_pairs={{0,4},{1,5},{2,6},{3,7},{4,8},{5,9},{6,10},{7,11},{8,12},{9,13},{1... | collective-permute-start | bytes 1179656 | tf_op jit(solution)/shard_map/ppermute | solution.py:265
  19.0 3.8 %load.1 = (bf16[2048,768]{1,0:T(8,128)(2,1)S(1)}, bf16[2048,768]{1,0:T(8,128)(2,1)S(1)}, bf16[768,2048]{1,0:T(8,128)(2,1)S(1)}) custom-call(bf16[2048,768]{1,0:T(8,128)(2,1)} %bitcast.7, bf16[2048,768]{1,0:T(8,128)(2,1)} %bitcast.8, bf16[768,2048]{1,0:T(8,128)(2,1)} %bitcast.9), custom_call_target="tpu_custom_call" | custom-call | tf_op jit(solution)/shard_map/load/pallas_call | solution.py:278
  23.6 3.5 %collective-permute-done.11.b = bf16[96,2048]{1,0:T(8,128)(2,1)S(1)} collective-permute-done((bf16[96,2048]{1,0:T(8,128)(2,1)S(1)}, bf16[96,2048]{1,0:T(8,128)(2,1)S(1)}, u32[]{:S(2)}, u32[]{:S(2)}) %collective-permute-start.11) | collective-permute-done | bytes 393248 | tf_op jit(solution)/shard_map/ppermute | solution.py:266
  27.1 1.9 %collective-permute-done.8.a = bf16[96,2048]{1,0:T(8,128)(2,1)S(1)} collective-permute-done((bf16[96,2048]{1,0:T(8,128)(2,1)S(1)}, bf16[96,2048]{1,0:T(8,128)(2,1)S(1)}, u32[]{:S(2)}, u32[]{:S(2)}) %collective-permute-start.8) | collective-permute-done | bytes 393248 | tf_op jit(solution)/shard_map/ppermute | solution.py:265
  28.9 1.7 %collective-permute-start.10 = (bf16[96,2048]{1,0:T(8,128)(2,1)S(1)}, bf16[96,2048]{1,0:T(8,128)(2,1)S(1)}, u32[]{:S(2)}, u32[]{:S(2)}) collective-permute-start(bf16[96,2048]{1,0:T(8,128)(2,1)S(1)} %collective-permute-done.8.a), channel_id=1, source_target_pairs={{0,2},{1,3},{2,0},{3,1},{4,6},{5,7},{6,4},{7,5},{8,10},{9,11},{10,... | collective-permute-start | bytes 1179656 | tf_op jit(solution)/shard_map/ppermute | solution.py:266
  30.6 5.7 %expert.4 = (bf16[96,2048]{1,0:T(8,128)(2,1)S(1)}, bf16[96,2048]{1,0:T(8,128)(2,1)S(1)}, bf16[192,2048]{1,0:T(8,128)(2,1)S(1)}) custom-call(bf16[96,2048]{1,0:T(8,128)(2,1)S(1)} %collective-permute-done.a, bf16[96,2048]{1,0:T(8,128)(2,1)S(1)} %collective-permute-done.11.b, bf16[96,2048]{1,0:T(8,128)(2,1)S(1)} %collective-permute-done.12.c, ...), custom_call_target="tpu_custom_call" | custom-call | flops 3623878656 | bytes 12582912 | tf_op jit(solution)/shard_map/expert/pallas_call | solution.py:225
  36.3 2.3 %collective-permute-done.10.b = bf16[96,2048]{1,0:T(8,128)(2,1)S(1)} collective-permute-done((bf16[96,2048]{1,0:T(8,128)(2,1)S(1)}, bf16[96,2048]{1,0:T(8,128)(2,1)S(1)}, u32[]{:S(2)}, u32[]{:S(2)}) %collective-permute-start.10) | collective-permute-done | bytes 393248 | tf_op jit(solution)/shard_map/ppermute | solution.py:266
  38.6 2.5 %collective-permute-done.9.a = bf16[96,2048]{1,0:T(8,128)(2,1)S(1)} collective-permute-done((bf16[96,2048]{1,0:T(8,128)(2,1)S(1)}, bf16[96,2048]{1,0:T(8,128)(2,1)S(1)}, u32[]{:S(2)}, u32[]{:S(2)}) %collective-permute-start.9) | collective-permute-done | bytes 393248 | tf_op jit(solution)/shard_map/ppermute | solution.py:265
  42.2 5.6 %expert.5 = (bf16[96,2048]{1,0:T(8,128)(2,1)S(1)}, bf16[96,2048]{1,0:T(8,128)(2,1)S(1)}, bf16[192,2048]{1,0:T(8,128)(2,1)S(1)}) custom-call(bf16[96,2048]{1,0:T(8,128)(2,1)S(1)} %collective-permute-done.8.a, bf16[96,2048]{1,0:T(8,128)(2,1)S(1)} %collective-permute-done.10.b, bf16[96,2048]{1,0:T(8,128)(2,1)S(1)} %collective-permute-done.14.c, ...), custom_call_target="tpu_custom_call" | custom-call | flops 3623878656 | bytes 12582912 | tf_op jit(solution)/shard_map/expert/pallas_call | solution.py:225
  47.8 2.4 %collective-permute-done.16.b = bf16[96,2048]{1,0:T(8,128)(2,1)S(1)} collective-permute-done((bf16[96,2048]{1,0:T(8,128)(2,1)S(1)}, bf16[96,2048]{1,0:T(8,128)(2,1)S(1)}, u32[]{:S(2)}, u32[]{:S(2)}) %collective-permute-start.16) | collective-permute-done | bytes 393248 | tf_op jit(solution)/shard_map/ppermute | solution.py:266
  54.7 5.6 %expert.6 = (bf16[96,2048]{1,0:T(8,128)(2,1)S(1)}, bf16[96,2048]{1,0:T(8,128)(2,1)S(1)}, bf16[192,2048]{1,0:T(8,128)(2,1)S(1)}) custom-call(bf16[96,2048]{1,0:T(8,128)(2,1)S(1)} %collective-permute-done.9.a, bf16[96,2048]{1,0:T(8,128)(2,1)S(1)} %collective-permute-done.16.b, bf16[96,2048]{1,0:T(8,128)(2,1)S(1)} %collective-permute-done.19.c, ...), custom_call_target="tpu_custom_call" | custom-call | flops 3623878656 | bytes 12582912 | tf_op jit(solution)/shard_map/expert/pallas_call | solution.py:225
  62.2 1.6 %collective-permute-done.18 = bf16[96,2048]{1,0:T(8,128)(2,1)S(1)} collective-permute-done((bf16[96,2048]{1,0:T(8,128)(2,1)S(1)}, bf16[96,2048]{1,0:T(8,128)(2,1)S(1)}, u32[]{:S(2)}, u32[]{:S(2)}) %collective-permute-start.18) | collective-permute-done | bytes 393248 | tf_op jit(solution)/shard_map/ppermute | solution.py:266
  63.9 2.7 %collective-permute-start.30 = (bf16[96,2048]{1,0:T(8,128)(2,1)S(1)}, bf16[96,2048]{1,0:T(8,128)(2,1)S(1)}, u32[]{:S(2)}, u32[]{:S(2)}) collective-permute-start(bf16[96,2048]{1,0:T(8,128)(2,1)S(1)} %add_convert_fusion.6), channel_id=1, source_target_pairs={{0,12},{1,13},{2,14},{3,15},{4,0},{5,1},{6,2},{7,3},{8,4},{9,5},{1... | collective-permute-start | bytes 1179656 | tf_op jit(solution)/shard_map/ppermute | solution.py:265
  67.3 5.6 %expert.7 = (bf16[96,2048]{1,0:T(8,128)(2,1)S(1)}, bf16[96,2048]{1,0:T(8,128)(2,1)S(1)}, bf16[192,2048]{1,0:T(8,128)(2,1)S(1)}) custom-call(bf16[96,2048]{1,0:T(8,128)(2,1)S(1)} %copy-done.2, bf16[96,2048]{1,0:T(8,128)(2,1)S(1)} %collective-permute-done.2.b, bf16[96,2048]{1,0:T(8,128)(2,1)S(1)} %collective-permute-done.22.c, ...), custom_call_target="tpu_custom_call" | custom-call | flops 3623878656 | bytes 12582912 | tf_op jit(solution)/shard_map/expert/pallas_call | solution.py:225
  74.7 4.3 %collective-permute-start.31 = (bf16[96,2048]{1,0:T(8,128)(2,1)S(1)}, bf16[96,2048]{1,0:T(8,128)(2,1)S(1)}, u32[]{:S(2)}, u32[]{:S(2)}) collective-permute-start(bf16[96,2048]{1,0:T(8,128)(2,1)S(1)} %add_convert_fusion.1), channel_id=1, source_target_pairs={{0,12},{1,13},{2,14},{3,15},{4,0},{5,1},{6,2},{7,3},{8,4},{9,5},{1... | collective-permute-start | bytes 1179656 | tf_op jit(solution)/shard_map/ppermute | solution.py:265
  79.0 2.0 %collective-permute-done.26 = bf16[96,2048]{1,0:T(8,128)(2,1)S(1)} collective-permute-done((bf16[96,2048]{1,0:T(8,128)(2,1)S(1)}, bf16[96,2048]{1,0:T(8,128)(2,1)S(1)}, u32[]{:S(2)}, u32[]{:S(2)}) %collective-permute-start.26) | collective-permute-done | bytes 393248 | tf_op jit(solution)/shard_map/ppermute | solution.py:266
  83.4 5.3 %collective-permute-done.31 = bf16[96,2048]{1,0:T(8,128)(2,1)S(1)} collective-permute-done((bf16[96,2048]{1,0:T(8,128)(2,1)S(1)}, bf16[96,2048]{1,0:T(8,128)(2,1)S(1)}, u32[]{:S(2)}, u32[]{:S(2)}) %collective-permute-start.31) | collective-permute-done | bytes 393248 | tf_op jit(solution)/shard_map/ppermute | solution.py:265
  88.6 6.5 %collective-permute-done.27 = bf16[96,2048]{1,0:T(8,128)(2,1)S(1)} collective-permute-done((bf16[96,2048]{1,0:T(8,128)(2,1)S(1)}, bf16[96,2048]{1,0:T(8,128)(2,1)S(1)}, u32[]{:S(2)}, u32[]{:S(2)}) %collective-permute-start.27) | collective-permute-done | bytes 393248 | tf_op jit(solution)/shard_map/ppermute | solution.py:265
  (62 shorter events, 18.5 us)
Async XLA Ops:
  0.8 4.7 %collective-permute-start.1 = (f32[16,128]{1,0:T(8,128)S(1)}, f32[16,128]{1,0:T(8,128)S(1)}, u32[]{:S(2)}, u32[]{:S(2)}) collective-permute-start(f32[16,128]{1,0:T(8,128)S(1)} %weights.1.w0), channel_id=1, source_target_pairs={{0,2},{1,3},{2,0},{3,1},{4,6},{5,7},{6,4},{7,5},{8,10},{9,11},{10,... | collective-permute-start | bytes 24584 | tf_op jit(solution)/shard_map/ppermute | solution.py:266
  3.9 13.0 %collective-permute-start = (bf16[96,2048]{1,0:T(8,128)(2,1)}, bf16[96,2048]{1,0:T(8,128)(2,1)S(1)}, u32[]{:S(2)}, u32[]{:S(2)}) collective-permute-start(bf16[96,2048]{1,0:T(8,128)(2,1)} %a), channel_id=1, source_target_pairs={{0,4},{1,5},{2,6},{3,7},{4,8},{5,9},{6,10},{7,11},{8,12},{9,13},{1... | collective-permute-start | bytes 1179656 | tf_op jit(solution)/shard_map/ppermute | solution.py:265
  5.5 11.3 %collective-permute-start.2 = (bf16[96,2048]{1,0:T(8,128)(2,1)}, bf16[96,2048]{1,0:T(8,128)(2,1)S(1)}, u32[]{:S(2)}, u32[]{:S(2)}) collective-permute-start(bf16[96,2048]{1,0:T(8,128)(2,1)} %a), channel_id=1, source_target_pairs={{0,2},{1,3},{2,0},{3,1},{4,6},{5,7},{6,4},{7,5},{8,10},{9,11},{10,... | collective-permute-start | bytes 1179656 | tf_op jit(solution)/shard_map/ppermute | solution.py:266
  8.9 7.9 %collective-permute-start.5 = (f32[8,128]{1,0:T(8,128)S(1)}, f32[8,128]{1,0:T(8,128)S(1)}, u32[]{:S(2)}, u32[]{:S(2)}) collective-permute-start(f32[8,128]{1,0:T(8,128)S(1)} %get-tuple-element.43), channel_id=1, source_target_pairs={{0,4},{1,5},{2,6},{3,7},{4,8},{5,9},{6,10},{7,11},{8,12},{9,13},{1... | collective-permute-start | bytes 12296 | tf_op jit(solution)/shard_map/ppermute | solution.py:265
  10.5 6.3 %collective-permute-start.6 = (f32[8,128]{1,0:T(8,128)S(1)}, f32[8,128]{1,0:T(8,128)S(1)}, u32[]{:S(2)}, u32[]{:S(2)}) collective-permute-start(f32[8,128]{1,0:T(8,128)S(1)} %get-tuple-element.44), channel_id=1, source_target_pairs={{0,8},{1,9},{2,10},{3,11},{4,12},{5,13},{6,14},{7,15},{8,0},{9,1},... | collective-permute-start | bytes 12296 | tf_op jit(solution)/shard_map/ppermute | solution.py:265
  16.8 10.2 %collective-permute-start.11 = (bf16[96,2048]{1,0:T(8,128)(2,1)S(1)}, bf16[96,2048]{1,0:T(8,128)(2,1)S(1)}, u32[]{:S(2)}, u32[]{:S(2)}) collective-permute-start(bf16[96,2048]{1,0:T(8,128)(2,1)S(1)} %collective-permute-done.a), channel_id=1, source_target_pairs={{0,2},{1,3},{2,0},{3,1},{4,6},{5,7},{6,4},{7,5},{8,10},{9,11},{10,... | collective-permute-start | bytes 1179656 | tf_op jit(solution)/shard_map/ppermute | solution.py:266
  17.4 11.5 %collective-permute-start.8 = (bf16[96,2048]{1,0:T(8,128)(2,1)S(1)}, bf16[96,2048]{1,0:T(8,128)(2,1)S(1)}, u32[]{:S(2)}, u32[]{:S(2)}) collective-permute-start(bf16[96,2048]{1,0:T(8,128)(2,1)S(1)} %collective-permute-done.a), channel_id=1, source_target_pairs={{0,4},{1,5},{2,6},{3,7},{4,8},{5,9},{6,10},{7,11},{8,12},{9,13},{1... | collective-permute-start | bytes 1179656 | tf_op jit(solution)/shard_map/ppermute | solution.py:265
  23.5 7.1 %collective-permute-start.12 = (bf16[96,2048]{1,0:T(8,128)(2,1)S(1)}, bf16[96,2048]{1,0:T(8,128)(2,1)S(1)}, u32[]{:S(2)}, u32[]{:S(2)}) collective-permute-start(bf16[96,2048]{1,0:T(8,128)(2,1)S(1)} %collective-permute-done.a), channel_id=1, source_target_pairs={{0,1},{1,0},{2,3},{3,2},{4,5},{5,4},{6,7},{7,6},{8,9},{9,8},{10,11... | collective-permute-start | bytes 1179656 | tf_op jit(solution)/shard_map/ppermute | solution.py:267
  28.9 9.7 %collective-permute-start.10 = (bf16[96,2048]{1,0:T(8,128)(2,1)S(1)}, bf16[96,2048]{1,0:T(8,128)(2,1)S(1)}, u32[]{:S(2)}, u32[]{:S(2)}) collective-permute-start(bf16[96,2048]{1,0:T(8,128)(2,1)S(1)} %collective-permute-done.8.a), channel_id=1, source_target_pairs={{0,2},{1,3},{2,0},{3,1},{4,6},{5,7},{6,4},{7,5},{8,10},{9,11},{10,... | collective-permute-start | bytes 1179656 | tf_op jit(solution)/shard_map/ppermute | solution.py:266
  30.6 10.5 %collective-permute-start.9 = (bf16[96,2048]{1,0:T(8,128)(2,1)S(1)}, bf16[96,2048]{1,0:T(8,128)(2,1)S(1)}, u32[]{:S(2)}, u32[]{:S(2)}) collective-permute-start(bf16[96,2048]{1,0:T(8,128)(2,1)S(1)} %collective-permute-done.8.a), channel_id=1, source_target_pairs={{0,4},{1,5},{2,6},{3,7},{4,8},{5,9},{6,10},{7,11},{8,12},{9,13},{1... | collective-permute-start | bytes 1179656 | tf_op jit(solution)/shard_map/ppermute | solution.py:265
  30.6 11.5 %collective-permute-start.14 = (bf16[96,2048]{1,0:T(8,128)(2,1)S(1)}, bf16[96,2048]{1,0:T(8,128)(2,1)S(1)}, u32[]{:S(2)}, u32[]{:S(2)}) collective-permute-start(bf16[96,2048]{1,0:T(8,128)(2,1)S(1)} %collective-permute-done.8.a), channel_id=1, source_target_pairs={{0,1},{1,0},{2,3},{3,2},{4,5},{5,4},{6,7},{7,6},{8,9},{9,8},{10,11... | collective-permute-start | bytes 1179656 | tf_op jit(solution)/shard_map/ppermute | solution.py:267
  41.1 9.0 %collective-permute-start.16 = (bf16[96,2048]{1,0:T(8,128)(2,1)S(1)}, bf16[96,2048]{1,0:T(8,128)(2,1)S(1)}, u32[]{:S(2)}, u32[]{:S(2)}) collective-permute-start(bf16[96,2048]{1,0:T(8,128)(2,1)S(1)} %collective-permute-done.9.a), channel_id=1, source_target_pairs={{0,2},{1,3},{2,0},{3,1},{4,6},{5,7},{6,4},{7,5},{8,10},{9,11},{10,... | collective-permute-start | bytes 1179656 | tf_op jit(solution)/shard_map/ppermute | solution.py:266
  50.1 10.3 %collective-permute-start.28 = (bf16[192,2048]{1,0:T(8,128)(2,1)S(1)}, bf16[192,2048]{1,0:T(8,128)(2,1)S(1)}, u32[]{:S(2)}, u32[]{:S(2)}) collective-permute-start(bf16[192,2048]{1,0:T(8,128)(2,1)S(1)} %get-tuple-element.73), channel_id=1, source_target_pairs={{0,1},{1,0},{2,3},{3,2},{4,5},{5,4},{6,7},{7,6},{8,9},{9,8},{10,11... | collective-permute-start | bytes 2359304 | tf_op jit(solution)/shard_map/ppermute | solution.py:267
  52.5 11.2 %collective-permute-start.18 = (bf16[96,2048]{1,0:T(8,128)(2,1)S(1)}, bf16[96,2048]{1,0:T(8,128)(2,1)S(1)}, u32[]{:S(2)}, u32[]{:S(2)}) collective-permute-start(bf16[96,2048]{1,0:T(8,128)(2,1)S(1)} %add_convert_fusion.7), channel_id=1, source_target_pairs={{0,2},{1,3},{2,0},{3,1},{4,6},{5,7},{6,4},{7,5},{8,10},{9,11},{10,... | collective-permute-start | bytes 1179656 | tf_op jit(solution)/shard_map/ppermute | solution.py:266
  60.3 6.3 %collective-permute-start.21 = (bf16[192,2048]{1,0:T(8,128)(2,1)S(1)}, bf16[192,2048]{1,0:T(8,128)(2,1)S(1)}, u32[]{:S(2)}, u32[]{:S(2)}) collective-permute-start(bf16[192,2048]{1,0:T(8,128)(2,1)S(1)} %get-tuple-element.66), channel_id=1, source_target_pairs={{0,1},{1,0},{2,3},{3,2},{4,5},{5,4},{6,7},{7,6},{8,9},{9,8},{10,11... | collective-permute-start | bytes 2359304 | tf_op jit(solution)/shard_map/ppermute | solution.py:267
  60.6 6.7 %collective-permute-start.23 = (bf16[96,2048]{1,0:T(8,128)(2,1)S(1)}, bf16[96,2048]{1,0:T(8,128)(2,1)S(1)}, u32[]{:S(2)}, u32[]{:S(2)}) collective-permute-start(bf16[96,2048]{1,0:T(8,128)(2,1)S(1)} %collective-permute-done.2.b), channel_id=1, source_target_pairs={{0,1},{1,0},{2,3},{3,2},{4,5},{5,4},{6,7},{7,6},{8,9},{9,8},{10,11... | collective-permute-start | bytes 1179656 | tf_op jit(solution)/shard_map/ppermute | solution.py:267
  61.0 6.3 %collective-permute-start.22 = (bf16[96,2048]{1,0:T(8,128)(2,1)S(1)}, bf16[96,2048]{1,0:T(8,128)(2,1)S(1)}, u32[]{:S(2)}, u32[]{:S(2)}) collective-permute-start(bf16[96,2048]{1,0:T(8,128)(2,1)S(1)} %copy-done.2), channel_id=1, source_target_pairs={{0,1},{1,0},{2,3},{3,2},{4,5},{5,4},{6,7},{7,6},{8,9},{9,8},{10,11... | collective-permute-start | bytes 1179656 | tf_op jit(solution)/shard_map/ppermute | solution.py:267
  61.2 11.9 %collective-permute-start.29 = (bf16[96,2048]{1,0:T(8,128)(2,1)S(1)}, bf16[96,2048]{1,0:T(8,128)(2,1)S(1)}, u32[]{:S(2)}, u32[]{:S(2)}) collective-permute-start(bf16[96,2048]{1,0:T(8,128)(2,1)S(1)} %add_convert_fusion.2), channel_id=1, source_target_pairs={{0,2},{1,3},{2,0},{3,1},{4,6},{5,7},{6,4},{7,5},{8,10},{9,11},{10,... | collective-permute-start | bytes 1179656 | tf_op jit(solution)/shard_map/ppermute | solution.py:266
  63.9 10.6 %collective-permute-start.30 = (bf16[96,2048]{1,0:T(8,128)(2,1)S(1)}, bf16[96,2048]{1,0:T(8,128)(2,1)S(1)}, u32[]{:S(2)}, u32[]{:S(2)}) collective-permute-start(bf16[96,2048]{1,0:T(8,128)(2,1)S(1)} %add_convert_fusion.6), channel_id=1, source_target_pairs={{0,12},{1,13},{2,14},{3,15},{4,0},{5,1},{6,2},{7,3},{8,4},{9,5},{1... | collective-permute-start | bytes 1179656 | tf_op jit(solution)/shard_map/ppermute | solution.py:265
  66.7 14.3 %collective-permute-start.26 = (bf16[96,2048]{1,0:T(8,128)(2,1)S(1)}, bf16[96,2048]{1,0:T(8,128)(2,1)S(1)}, u32[]{:S(2)}, u32[]{:S(2)}) collective-permute-start(bf16[96,2048]{1,0:T(8,128)(2,1)S(1)} %add_convert_fusion.5), channel_id=1, source_target_pairs={{0,2},{1,3},{2,0},{3,1},{4,6},{5,7},{6,4},{7,5},{8,10},{9,11},{10,... | collective-permute-start | bytes 1179656 | tf_op jit(solution)/shard_map/ppermute | solution.py:266
  72.9 9.8 %collective-permute-start.24 = (bf16[192,2048]{1,0:T(8,128)(2,1)S(1)}, bf16[192,2048]{1,0:T(8,128)(2,1)S(1)}, u32[]{:S(2)}, u32[]{:S(2)}) collective-permute-start(bf16[192,2048]{1,0:T(8,128)(2,1)S(1)} %get-tuple-element.70), channel_id=1, source_target_pairs={{0,1},{1,0},{2,3},{3,2},{4,5},{5,4},{6,7},{7,6},{8,9},{9,8},{10,11... | collective-permute-start | bytes 2359304 | tf_op jit(solution)/shard_map/ppermute | solution.py:267
  74.7 13.9 %collective-permute-start.31 = (bf16[96,2048]{1,0:T(8,128)(2,1)S(1)}, bf16[96,2048]{1,0:T(8,128)(2,1)S(1)}, u32[]{:S(2)}, u32[]{:S(2)}) collective-permute-start(bf16[96,2048]{1,0:T(8,128)(2,1)S(1)} %add_convert_fusion.1), channel_id=1, source_target_pairs={{0,12},{1,13},{2,14},{3,15},{4,0},{5,1},{6,2},{7,3},{8,4},{9,5},{1... | collective-permute-start | bytes 1179656 | tf_op jit(solution)/shard_map/ppermute | solution.py:265
  81.1 14.0 %collective-permute-start.27 = (bf16[96,2048]{1,0:T(8,128)(2,1)S(1)}, bf16[96,2048]{1,0:T(8,128)(2,1)S(1)}, u32[]{:S(2)}, u32[]{:S(2)}) collective-permute-start(bf16[96,2048]{1,0:T(8,128)(2,1)S(1)} %add_convert_fusion.3), channel_id=1, source_target_pairs={{0,4},{1,5},{2,6},{3,7},{4,8},{5,9},{6,10},{7,11},{8,12},{9,13},{1... | collective-permute-start | bytes 1179656 | tf_op jit(solution)/shard_map/ppermute | solution.py:265
  82.8 12.3 %collective-permute-start.25 = (bf16[96,2048]{1,0:T(8,128)(2,1)S(1)}, bf16[96,2048]{1,0:T(8,128)(2,1)S(1)}, u32[]{:S(2)}, u32[]{:S(2)}) collective-permute-start(bf16[96,2048]{1,0:T(8,128)(2,1)S(1)} %add_convert_fusion.4), channel_id=1, source_target_pairs={{0,2},{1,3},{2,0},{3,1},{4,6},{5,7},{6,4},{7,5},{8,10},{9,11},{10,... | collective-permute-start | bytes 1179656 | tf_op jit(solution)/shard_map/ppermute | solution.py:266
  (11 other events, 39.3 us)

commit v5 on v4

--- a/solution.py
+++ b/solution.py
@@ -341,8 +341,12 @@
     p3 = expert(3, after(s3, b2), y3, over_core(s3), over_core(y3))
 
     (a1, b1), (a3, b3) = map(lambda p: merge_core(*p), (p1, p3))
-    block2 = bf16(a2 + f32(after(over_y(b2), p3[0])))
-    hop = over_ring(block2, ring - 1)
+    half = tok_rows // 32 * 16
+    y_b2, y_low = over_y(b2[:half]), after(over_y(b2[half:]), p3[0])
+    top = bf16(a2[:half] + f32(after(y_b2, p3[0])))
+    hop = over_ring(top, ring - 1)
+    block2 = bf16(a2[half:] + f32(after(y_low, top)))
+    hop = jnp.concatenate([hop, over_ring(block2, ring - 1)])
     own, y_own = after(tokens, b2), after(y_own, b2)
     p0 = expert(0, after(own, block2, b3), y_own, over_core(own), over_core(y_own))
     a0, b0 = merge_core(*p0)

time: 96.4 us -> 96.2 us (level)
  waiting for transfers between devices: 35 us -> 33.5 us
  starting transfers between devices: 31.2 us -> 32.4 us
    ppermute x9 -> x10, starting transfers between devices: 11.6 us -> 12.8 us  [dense_layer(): over_y = lambda a: lax.ppermute(a, 'ep', y_pairs)]
    ppermute x9 -> x10, waiting for transfers between devices: 19.8 us -> 18.8 us  [dense_layer(): over_ring = lambda a, k: lax.ppermute(a, 'ep', ring_pairs(k)) if k else a]
    ppermute x9 -> x10, waiting for transfers between devices: 11.9 us -> 12.2 us  [dense_layer(): over_y = lambda a: lax.ppermute(a, 'ep', y_pairs)]
    ppermute x9 -> x10, starting transfers between devices: 17.2 us -> 17.3 us  [dense_layer(): over_ring = lambda a, k: lax.ppermute(a, 'ep', ring_pairs(k)) if k else a]
  transfers between devices with their start and end apart: 32 -> 34, of which waited for: 18 -> 15; matrix products, arithmetic and copies ran while one was open for 1% -> 1% of each run, Pallas kernels for 28% -> 28%
where the time goes in v5:
time: 96.2 us; the launch traced here: 96 us
  waiting for transfers between devices  33.5 us (35%)
  starting transfers between devices  32.4 us (34%)
  Pallas kernels  27.8 us (29%)
  other arithmetic  2.05 us (2%)
    pallas_call x4, Pallas kernels, expert_rows(): pl.pallas_call(functools.partial(expert_kernel, slot), in_specs=[anywhere...  22.4 us
    ppermute x10, waiting for transfers between devices, dense_layer(): over_ring = lambda a, k: lax.ppermute(a, 'ep', ring_pairs(k)) if k else a  18.8 us
    ppermute x10, starting transfers between devices, dense_layer(): over_ring = lambda a, k: lax.ppermute(a, 'ep', ring_pairs(k)) if k else a  17.3 us
    ppermute x10, starting transfers between devices, dense_layer(): over_y = lambda a: lax.ppermute(a, 'ep', y_pairs)  12.8 us
    ppermute x10, waiting for transfers between devices, dense_layer(): over_y = lambda a: lax.ppermute(a, 'ep', y_pairs)  12.2 us
    pallas_call x1, Pallas kernels, dense_layer(): pl.pallas_call(load_kernel, in_specs=[anywhere] * 3, out_specs=[vmem] * 3...  3.8 us
    ppermute x14, waiting for transfers between devices, dense_layer(): over_core = lambda a: lax.ppermute(a, 'ep', core_pairs)  2.52 us
    ppermute x14, starting transfers between devices, dense_layer(): over_core = lambda a: lax.ppermute(a, 'ep', core_pairs)  2.29 us
  transfers between devices with their start and end apart: 34, of which 15 were waited for; matrix products, arithmetic and copies ran while one was open for 1% of the time, Pallas kernels for 28%

profile of v5, /device:TPU:0, one launch (start us, length us, event | category | flops | bytes accessed | tf_op | source)
XLA Modules:
  0.0 96.0 jit_solution(2877401042909973800)
XLA Ops:
  0.8 3.0 %collective-permute-start.1 = (f32[16,128]{1,0:T(8,128)S(1)}, f32[16,128]{1,0:T(8,128)S(1)}, u32[]{:S(2)}, u32[]{:S(2)}) collective-permute-start(f32[16,128]{1,0:T(8,128)S(1)} %weights.1.w0), channel_id=1, source_target_pairs={{0,2},{1,3},{2,0},{3,1},{4,6},{5,7},{6,4},{7,5},{8,10},{9,11},{10,... | collective-permute-start | bytes 24584 | tf_op jit(solution)/shard_map/ppermute | solution.py:266
  5.5 2.0 %collective-permute-start.2 = (bf16[96,2048]{1,0:T(8,128)(2,1)}, bf16[96,2048]{1,0:T(8,128)(2,1)S(1)}, u32[]{:S(2)}, u32[]{:S(2)}) collective-permute-start(bf16[96,2048]{1,0:T(8,128)(2,1)} %a), channel_id=1, source_target_pairs={{0,2},{1,3},{2,0},{3,1},{4,6},{5,7},{6,4},{7,5},{8,10},{9,11},{10,... | collective-permute-start | bytes 1179656 | tf_op jit(solution)/shard_map/ppermute | solution.py:266
  8.9 1.6 %collective-permute-start.5 = (f32[8,128]{1,0:T(8,128)S(1)}, f32[8,128]{1,0:T(8,128)S(1)}, u32[]{:S(2)}, u32[]{:S(2)}) collective-permute-start(f32[8,128]{1,0:T(8,128)S(1)} %get-tuple-element.45), channel_id=1, source_target_pairs={{0,4},{1,5},{2,6},{3,7},{4,8},{5,9},{6,10},{7,11},{8,12},{9,13},{1... | collective-permute-start | bytes 12296 | tf_op jit(solution)/shard_map/ppermute | solution.py:265
  10.5 2.6 %collective-permute-start.6 = (f32[8,128]{1,0:T(8,128)S(1)}, f32[8,128]{1,0:T(8,128)S(1)}, u32[]{:S(2)}, u32[]{:S(2)}) collective-permute-start(f32[8,128]{1,0:T(8,128)S(1)} %get-tuple-element.46), channel_id=1, source_target_pairs={{0,8},{1,9},{2,10},{3,11},{4,12},{5,13},{6,14},{7,15},{8,0},{9,1},... | collective-permute-start | bytes 12296 | tf_op jit(solution)/shard_map/ppermute | solution.py:265
  14.5 2.4 %collective-permute-done.5.refs_1_ = f32[8,128]{1,0:T(8,128)S(1)} collective-permute-done((f32[8,128]{1,0:T(8,128)S(1)}, f32[8,128]{1,0:T(8,128)S(1)}, u32[]{:S(2)}, u32[]{:S(2)}) %collective-permute-start.5) | collective-permute-done | bytes 4128 | tf_op jit(solution)/shard_map/ppermute | solution.py:265
  17.4 1.6 %collective-permute-start.8 = (bf16[96,2048]{1,0:T(8,128)(2,1)S(1)}, bf16[96,2048]{1,0:T(8,128)(2,1)S(1)}, u32[]{:S(2)}, u32[]{:S(2)}) collective-permute-start(bf16[96,2048]{1,0:T(8,128)(2,1)S(1)} %collective-permute-done.a), channel_id=1, source_target_pairs={{0,4},{1,5},{2,6},{3,7},{4,8},{5,9},{6,10},{7,11},{8,12},{9,13},{1... | collective-permute-start | bytes 1179656 | tf_op jit(solution)/shard_map/ppermute | solution.py:265
  19.0 3.8 %load.1 = (bf16[2048,768]{1,0:T(8,128)(2,1)S(1)}, bf16[2048,768]{1,0:T(8,128)(2,1)S(1)}, bf16[768,2048]{1,0:T(8,128)(2,1)S(1)}) custom-call(bf16[2048,768]{1,0:T(8,128)(2,1)} %bitcast.7, bf16[2048,768]{1,0:T(8,128)(2,1)} %bitcast.8, bf16[768,2048]{1,0:T(8,128)(2,1)} %bitcast.9), custom_call_target="tpu_custom_call" | custom-call | tf_op jit(solution)/shard_map/load/pallas_call | solution.py:278
  23.6 3.5 %collective-permute-done.11.b = bf16[96,2048]{1,0:T(8,128)(2,1)S(1)} collective-permute-done((bf16[96,2048]{1,0:T(8,128)(2,1)S(1)}, bf16[96,2048]{1,0:T(8,128)(2,1)S(1)}, u32[]{:S(2)}, u32[]{:S(2)}) %collective-permute-start.11) | collective-permute-done | bytes 393248 | tf_op jit(solution)/shard_map/ppermute | solution.py:266
  27.1 1.9 %collective-permute-done.8.a = bf16[96,2048]{1,0:T(8,128)(2,1)S(1)} collective-permute-done((bf16[96,2048]{1,0:T(8,128)(2,1)S(1)}, bf16[96,2048]{1,0:T(8,128)(2,1)S(1)}, u32[]{:S(2)}, u32[]{:S(2)}) %collective-permute-start.8) | collective-permute-done | bytes 393248 | tf_op jit(solution)/shard_map/ppermute | solution.py:265
  28.9 1.7 %collective-permute-start.10 = (bf16[96,2048]{1,0:T(8,128)(2,1)S(1)}, bf16[96,2048]{1,0:T(8,128)(2,1)S(1)}, u32[]{:S(2)}, u32[]{:S(2)}) collective-permute-start(bf16[96,2048]{1,0:T(8,128)(2,1)S(1)} %collective-permute-done.8.a), channel_id=1, source_target_pairs={{0,2},{1,3},{2,0},{3,1},{4,6},{5,7},{6,4},{7,5},{8,10},{9,11},{10,... | collective-permute-start | bytes 1179656 | tf_op jit(solution)/shard_map/ppermute | solution.py:266
  30.6 5.7 %expert.4 = (bf16[96,2048]{1,0:T(8,128)(2,1)S(1)}, bf16[96,2048]{1,0:T(8,128)(2,1)S(1)}, bf16[192,2048]{1,0:T(8,128)(2,1)S(1)}) custom-call(bf16[96,2048]{1,0:T(8,128)(2,1)S(1)} %collective-permute-done.a, bf16[96,2048]{1,0:T(8,128)(2,1)S(1)} %collective-permute-done.11.b, bf16[96,2048]{1,0:T(8,128)(2,1)S(1)} %collective-permute-done.12.c, ...), custom_call_target="tpu_custom_call" | custom-call | flops 3623878656 | bytes 12582912 | tf_op jit(solution)/shard_map/expert/pallas_call | solution.py:225
  36.3 2.3 %collective-permute-done.10.b = bf16[96,2048]{1,0:T(8,128)(2,1)S(1)} collective-permute-done((bf16[96,2048]{1,0:T(8,128)(2,1)S(1)}, bf16[96,2048]{1,0:T(8,128)(2,1)S(1)}, u32[]{:S(2)}, u32[]{:S(2)}) %collective-permute-start.10) | collective-permute-done | bytes 393248 | tf_op jit(solution)/shard_map/ppermute | solution.py:266
  39.1 2.0 %collective-permute-done.9.a = bf16[96,2048]{1,0:T(8,128)(2,1)S(1)} collective-permute-done((bf16[96,2048]{1,0:T(8,128)(2,1)S(1)}, bf16[96,2048]{1,0:T(8,128)(2,1)S(1)}, u32[]{:S(2)}, u32[]{:S(2)}) %collective-permute-start.9) | collective-permute-done | bytes 393248 | tf_op jit(solution)/shard_map/ppermute | solution.py:265
  42.2 5.6 %expert.5 = (bf16[96,2048]{1,0:T(8,128)(2,1)S(1)}, bf16[96,2048]{1,0:T(8,128)(2,1)S(1)}, bf16[192,2048]{1,0:T(8,128)(2,1)S(1)}) custom-call(bf16[96,2048]{1,0:T(8,128)(2,1)S(1)} %collective-permute-done.8.a, bf16[96,2048]{1,0:T(8,128)(2,1)S(1)} %collective-permute-done.10.b, bf16[96,2048]{1,0:T(8,128)(2,1)S(1)} %collective-permute-done.14.c, ...), custom_call_target="tpu_custom_call" | custom-call | flops 3623878656 | bytes 12582912 | tf_op jit(solution)/shard_map/expert/pallas_call | solution.py:225
  47.8 2.4 %collective-permute-done.16.b = bf16[96,2048]{1,0:T(8,128)(2,1)S(1)} collective-permute-done((bf16[96,2048]{1,0:T(8,128)(2,1)S(1)}, bf16[96,2048]{1,0:T(8,128)(2,1)S(1)}, u32[]{:S(2)}, u32[]{:S(2)}) %collective-permute-start.16) | collective-permute-done | bytes 393248 | tf_op jit(solution)/shard_map/ppermute | solution.py:266
  50.8 1.7 %collective-permute-done.17 = bf16[192,2048]{1,0:T(8,128)(2,1)S(1)} collective-permute-done((bf16[192,2048]{1,0:T(8,128)(2,1)S(1)}, bf16[192,2048]{1,0:T(8,128)(2,1)S(1)}, u32[]{:S(2)}, u32[]{:S(2)}) %collective-permute-start.17) | collective-permute-done | bytes 786464 | tf_op jit(solution)/shard_map/ppermute | solution.py:267
  54.8 5.6 %expert.6 = (bf16[96,2048]{1,0:T(8,128)(2,1)S(1)}, bf16[96,2048]{1,0:T(8,128)(2,1)S(1)}, bf16[192,2048]{1,0:T(8,128)(2,1)S(1)}) custom-call(bf16[96,2048]{1,0:T(8,128)(2,1)S(1)} %collective-permute-done.9.a, bf16[96,2048]{1,0:T(8,128)(2,1)S(1)} %collective-permute-done.16.b, bf16[96,2048]{1,0:T(8,128)(2,1)S(1)} %collective-permute-done.19.c, ...), custom_call_target="tpu_custom_call" | custom-call | flops 3623878656 | bytes 12582912 | tf_op jit(solution)/shard_map/expert/pallas_call | solution.py:225
  62.0 1.9 %collective-permute-done.18 = bf16[48,2048]{1,0:T(8,128)(2,1)S(1)} collective-permute-done((bf16[48,2048]{1,0:T(8,128)(2,1)S(1)}, bf16[48,2048]{1,0:T(8,128)(2,1)S(1)}, u32[]{:S(2)}, u32[]{:S(2)}) %collective-permute-start.18) | collective-permute-done | bytes 196640 | tf_op jit(solution)/shard_map/ppermute | solution.py:266
  64.0 2.5 %collective-permute-start.31 = (bf16[48,2048]{1,0:T(8,128)(2,1)S(1)}, bf16[48,2048]{1,0:T(8,128)(2,1)S(1)}, u32[]{:S(2)}, u32[]{:S(2)}) collective-permute-start(bf16[48,2048]{1,0:T(8,128)(2,1)S(1)} %fusion), channel_id=1, source_target_pairs={{0,12},{1,13},{2,14},{3,15},{4,0},{5,1},{6,2},{7,3},{8,4},{9,5},{1... | collective-permute-start | bytes 589832 | tf_op jit(solution)/shard_map/ppermute | solution.py:265
  67.7 5.6 %expert.7 = (bf16[96,2048]{1,0:T(8,128)(2,1)S(1)}, bf16[96,2048]{1,0:T(8,128)(2,1)S(1)}, bf16[192,2048]{1,0:T(8,128)(2,1)S(1)}) custom-call(bf16[96,2048]{1,0:T(8,128)(2,1)S(1)} %copy-done.2, bf16[96,2048]{1,0:T(8,128)(2,1)S(1)} %collective-permute-done.2.b, bf16[96,2048]{1,0:T(8,128)(2,1)S(1)} %collective-permute-done.23.c, ...), custom_call_target="tpu_custom_call" | custom-call | flops 3623878656 | bytes 12582912 | tf_op jit(solution)/shard_map/expert/pallas_call | solution.py:225
  74.6 4.3 %collective-permute-start.33 = (bf16[96,2048]{1,0:T(8,128)(2,1)S(1)}, bf16[96,2048]{1,0:T(8,128)(2,1)S(1)}, u32[]{:S(2)}, u32[]{:S(2)}) collective-permute-start(bf16[96,2048]{1,0:T(8,128)(2,1)S(1)} %add_convert_fusion.1), channel_id=1, source_target_pairs={{0,12},{1,13},{2,14},{3,15},{4,0},{5,1},{6,2},{7,3},{8,4},{9,5},{1... | collective-permute-start | bytes 1179656 | tf_op jit(solution)/shard_map/ppermute | solution.py:265
  78.9 2.1 %collective-permute-done.27 = bf16[96,2048]{1,0:T(8,128)(2,1)S(1)} collective-permute-done((bf16[96,2048]{1,0:T(8,128)(2,1)S(1)}, bf16[96,2048]{1,0:T(8,128)(2,1)S(1)}, u32[]{:S(2)}, u32[]{:S(2)}) %collective-permute-start.27) | collective-permute-done | bytes 393248 | tf_op jit(solution)/shard_map/ppermute | solution.py:266
  83.3 5.2 %collective-permute-done.33 = bf16[96,2048]{1,0:T(8,128)(2,1)S(1)} collective-permute-done((bf16[96,2048]{1,0:T(8,128)(2,1)S(1)}, bf16[96,2048]{1,0:T(8,128)(2,1)S(1)}, u32[]{:S(2)}, u32[]{:S(2)}) %collective-permute-start.33) | collective-permute-done | bytes 393248 | tf_op jit(solution)/shard_map/ppermute | solution.py:265
  88.5 6.5 %collective-permute-done.28 = bf16[96,2048]{1,0:T(8,128)(2,1)S(1)} collective-permute-done((bf16[96,2048]{1,0:T(8,128)(2,1)S(1)}, bf16[96,2048]{1,0:T(8,128)(2,1)S(1)}, u32[]{:S(2)}, u32[]{:S(2)}) %collective-permute-start.28) | collective-permute-done | bytes 393248 | tf_op jit(solution)/shard_map/ppermute | solution.py:265
  (68 shorter events, 18.6 us)
Async XLA Ops:
  3.9 13.0 %collective-permute-start = (bf16[96,2048]{1,0:T(8,128)(2,1)}, bf16[96,2048]{1,0:T(8,128)(2,1)S(1)}, u32[]{:S(2)}, u32[]{:S(2)}) collective-permute-start(bf16[96,2048]{1,0:T(8,128)(2,1)} %a), channel_id=1, source_target_pairs={{0,4},{1,5},{2,6},{3,7},{4,8},{5,9},{6,10},{7,11},{8,12},{9,13},{1... | collective-permute-start | bytes 1179656 | tf_op jit(solution)/shard_map/ppermute | solution.py:265
  5.5 11.3 %collective-permute-start.2 = (bf16[96,2048]{1,0:T(8,128)(2,1)}, bf16[96,2048]{1,0:T(8,128)(2,1)S(1)}, u32[]{:S(2)}, u32[]{:S(2)}) collective-permute-start(bf16[96,2048]{1,0:T(8,128)(2,1)} %a), channel_id=1, source_target_pairs={{0,2},{1,3},{2,0},{3,1},{4,6},{5,7},{6,4},{7,5},{8,10},{9,11},{10,... | collective-permute-start | bytes 1179656 | tf_op jit(solution)/shard_map/ppermute | solution.py:266
  8.9 7.9 %collective-permute-start.5 = (f32[8,128]{1,0:T(8,128)S(1)}, f32[8,128]{1,0:T(8,128)S(1)}, u32[]{:S(2)}, u32[]{:S(2)}) collective-permute-start(f32[8,128]{1,0:T(8,128)S(1)} %get-tuple-element.45), channel_id=1, source_target_pairs={{0,4},{1,5},{2,6},{3,7},{4,8},{5,9},{6,10},{7,11},{8,12},{9,13},{1... | collective-permute-start | bytes 12296 | tf_op jit(solution)/shard_map/ppermute | solution.py:265
  10.5 6.3 %collective-permute-start.6 = (f32[8,128]{1,0:T(8,128)S(1)}, f32[8,128]{1,0:T(8,128)S(1)}, u32[]{:S(2)}, u32[]{:S(2)}) collective-permute-start(f32[8,128]{1,0:T(8,128)S(1)} %get-tuple-element.46), channel_id=1, source_target_pairs={{0,8},{1,9},{2,10},{3,11},{4,12},{5,13},{6,14},{7,15},{8,0},{9,1},... | collective-permute-start | bytes 12296 | tf_op jit(solution)/shard_map/ppermute | solution.py:265
  16.8 10.2 %collective-permute-start.11 = (bf16[96,2048]{1,0:T(8,128)(2,1)S(1)}, bf16[96,2048]{1,0:T(8,128)(2,1)S(1)}, u32[]{:S(2)}, u32[]{:S(2)}) collective-permute-start(bf16[96,2048]{1,0:T(8,128)(2,1)S(1)} %collective-permute-done.a), channel_id=1, source_target_pairs={{0,2},{1,3},{2,0},{3,1},{4,6},{5,7},{6,4},{7,5},{8,10},{9,11},{10,... | collective-permute-start | bytes 1179656 | tf_op jit(solution)/shard_map/ppermute | solution.py:266
  17.4 11.5 %collective-permute-start.8 = (bf16[96,2048]{1,0:T(8,128)(2,1)S(1)}, bf16[96,2048]{1,0:T(8,128)(2,1)S(1)}, u32[]{:S(2)}, u32[]{:S(2)}) collective-permute-start(bf16[96,2048]{1,0:T(8,128)(2,1)S(1)} %collective-permute-done.a), channel_id=1, source_target_pairs={{0,4},{1,5},{2,6},{3,7},{4,8},{5,9},{6,10},{7,11},{8,12},{9,13},{1... | collective-permute-start | bytes 1179656 | tf_op jit(solution)/shard_map/ppermute | solution.py:265
  23.5 7.1 %collective-permute-start.12 = (bf16[96,2048]{1,0:T(8,128)(2,1)S(1)}, bf16[96,2048]{1,0:T(8,128)(2,1)S(1)}, u32[]{:S(2)}, u32[]{:S(2)}) collective-permute-start(bf16[96,2048]{1,0:T(8,128)(2,1)S(1)} %collective-permute-done.a), channel_id=1, source_target_pairs={{0,1},{1,0},{2,3},{3,2},{4,5},{5,4},{6,7},{7,6},{8,9},{9,8},{10,11... | collective-permute-start | bytes 1179656 | tf_op jit(solution)/shard_map/ppermute | solution.py:267
  28.9 9.7 %collective-permute-start.10 = (bf16[96,2048]{1,0:T(8,128)(2,1)S(1)}, bf16[96,2048]{1,0:T(8,128)(2,1)S(1)}, u32[]{:S(2)}, u32[]{:S(2)}) collective-permute-start(bf16[96,2048]{1,0:T(8,128)(2,1)S(1)} %collective-permute-done.8.a), channel_id=1, source_target_pairs={{0,2},{1,3},{2,0},{3,1},{4,6},{5,7},{6,4},{7,5},{8,10},{9,11},{10,... | collective-permute-start | bytes 1179656 | tf_op jit(solution)/shard_map/ppermute | solution.py:266
  30.6 10.5 %collective-permute-start.9 = (bf16[96,2048]{1,0:T(8,128)(2,1)S(1)}, bf16[96,2048]{1,0:T(8,128)(2,1)S(1)}, u32[]{:S(2)}, u32[]{:S(2)}) collective-permute-start(bf16[96,2048]{1,0:T(8,128)(2,1)S(1)} %collective-permute-done.8.a), channel_id=1, source_target_pairs={{0,4},{1,5},{2,6},{3,7},{4,8},{5,9},{6,10},{7,11},{8,12},{9,13},{1... | collective-permute-start | bytes 1179656 | tf_op jit(solution)/shard_map/ppermute | solution.py:265
  30.6 11.5 %collective-permute-start.14 = (bf16[96,2048]{1,0:T(8,128)(2,1)S(1)}, bf16[96,2048]{1,0:T(8,128)(2,1)S(1)}, u32[]{:S(2)}, u32[]{:S(2)}) collective-permute-start(bf16[96,2048]{1,0:T(8,128)(2,1)S(1)} %collective-permute-done.8.a), channel_id=1, source_target_pairs={{0,1},{1,0},{2,3},{3,2},{4,5},{5,4},{6,7},{7,6},{8,9},{9,8},{10,11... | collective-permute-start | bytes 1179656 | tf_op jit(solution)/shard_map/ppermute | solution.py:267
  38.6 12.1 %collective-permute-start.29 = (bf16[192,2048]{1,0:T(8,128)(2,1)S(1)}, bf16[192,2048]{1,0:T(8,128)(2,1)S(1)}, u32[]{:S(2)}, u32[]{:S(2)}) collective-permute-start(bf16[192,2048]{1,0:T(8,128)(2,1)S(1)} %get-tuple-element.77), channel_id=1, source_target_pairs={{0,1},{1,0},{2,3},{3,2},{4,5},{5,4},{6,7},{7,6},{8,9},{9,8},{10,11... | collective-permute-start | bytes 2359304 | tf_op jit(solution)/shard_map/ppermute | solution.py:267
  41.1 9.0 %collective-permute-start.16 = (bf16[96,2048]{1,0:T(8,128)(2,1)S(1)}, bf16[96,2048]{1,0:T(8,128)(2,1)S(1)}, u32[]{:S(2)}, u32[]{:S(2)}) collective-permute-start(bf16[96,2048]{1,0:T(8,128)(2,1)S(1)} %collective-permute-done.9.a), channel_id=1, source_target_pairs={{0,2},{1,3},{2,0},{3,1},{4,6},{5,7},{6,4},{7,5},{8,10},{9,11},{10,... | collective-permute-start | bytes 1179656 | tf_op jit(solution)/shard_map/ppermute | solution.py:266
  52.7 8.4 %collective-permute-start.21 = (bf16[48,2048]{1,0:T(8,128)(2,1)S(1)}, bf16[48,2048]{1,0:T(8,128)(2,1)S(1)}, u32[]{:S(2)}, u32[]{:S(2)}) collective-permute-start(bf16[48,2048]{1,0:T(8,128)(2,1)S(1)} %get-tuple-element.83), channel_id=1, source_target_pairs={{0,2},{1,3},{2,0},{3,1},{4,6},{5,7},{6,4},{7,5},{8,10},{9,11},{10,... | collective-permute-start | bytes 589832 | tf_op jit(solution)/shard_map/ppermute | solution.py:266
  53.7 10.2 %collective-permute-start.18 = (bf16[48,2048]{1,0:T(8,128)(2,1)S(1)}, bf16[48,2048]{1,0:T(8,128)(2,1)S(1)}, u32[]{:S(2)}, u32[]{:S(2)}) collective-permute-start(bf16[48,2048]{1,0:T(8,128)(2,1)S(1)} %get-tuple-element.84), channel_id=1, source_target_pairs={{0,2},{1,3},{2,0},{3,1},{4,6},{5,7},{6,4},{7,5},{8,10},{9,11},{10,... | collective-permute-start | bytes 589832 | tf_op jit(solution)/shard_map/ppermute | solution.py:266
  60.5 6.4 %collective-permute-start.24 = (bf16[96,2048]{1,0:T(8,128)(2,1)S(1)}, bf16[96,2048]{1,0:T(8,128)(2,1)S(1)}, u32[]{:S(2)}, u32[]{:S(2)}) collective-permute-start(bf16[96,2048]{1,0:T(8,128)(2,1)S(1)} %collective-permute-done.2.b), channel_id=1, source_target_pairs={{0,1},{1,0},{2,3},{3,2},{4,5},{5,4},{6,7},{7,6},{8,9},{9,8},{10,11... | collective-permute-start | bytes 1179656 | tf_op jit(solution)/shard_map/ppermute | solution.py:267
  61.0 6.7 %collective-permute-start.23 = (bf16[96,2048]{1,0:T(8,128)(2,1)S(1)}, bf16[96,2048]{1,0:T(8,128)(2,1)S(1)}, u32[]{:S(2)}, u32[]{:S(2)}) collective-permute-start(bf16[96,2048]{1,0:T(8,128)(2,1)S(1)} %copy-done.2), channel_id=1, source_target_pairs={{0,1},{1,0},{2,3},{3,2},{4,5},{5,4},{6,7},{7,6},{8,9},{9,8},{10,11... | collective-permute-start | bytes 1179656 | tf_op jit(solution)/shard_map/ppermute | solution.py:267
  61.1 12.3 %collective-permute-start.30 = (bf16[96,2048]{1,0:T(8,128)(2,1)S(1)}, bf16[96,2048]{1,0:T(8,128)(2,1)S(1)}, u32[]{:S(2)}, u32[]{:S(2)}) collective-permute-start(bf16[96,2048]{1,0:T(8,128)(2,1)S(1)} %add_convert_fusion.2), channel_id=1, source_target_pairs={{0,2},{1,3},{2,0},{3,1},{4,6},{5,7},{6,4},{7,5},{8,10},{9,11},{10,... | collective-permute-start | bytes 1179656 | tf_op jit(solution)/shard_map/ppermute | solution.py:266
  64.0 10.4 %collective-permute-start.31 = (bf16[48,2048]{1,0:T(8,128)(2,1)S(1)}, bf16[48,2048]{1,0:T(8,128)(2,1)S(1)}, u32[]{:S(2)}, u32[]{:S(2)}) collective-permute-start(bf16[48,2048]{1,0:T(8,128)(2,1)S(1)} %fusion), channel_id=1, source_target_pairs={{0,12},{1,13},{2,14},{3,15},{4,0},{5,1},{6,2},{7,3},{8,4},{9,5},{1... | collective-permute-start | bytes 589832 | tf_op jit(solution)/shard_map/ppermute | solution.py:265
  66.5 7.8 %collective-permute-start.32 = (bf16[48,2048]{1,0:T(8,128)(2,1)S(1)}, bf16[48,2048]{1,0:T(8,128)(2,1)S(1)}, u32[]{:S(2)}, u32[]{:S(2)}) collective-permute-start(bf16[48,2048]{1,0:T(8,128)(2,1)S(1)} %fusion.1), channel_id=1, source_target_pairs={{0,12},{1,13},{2,14},{3,15},{4,0},{5,1},{6,2},{7,3},{8,4},{9,5},{1... | collective-permute-start | bytes 589832 | tf_op jit(solution)/shard_map/ppermute | solution.py:265
  66.9 14.1 %collective-permute-start.27 = (bf16[96,2048]{1,0:T(8,128)(2,1)S(1)}, bf16[96,2048]{1,0:T(8,128)(2,1)S(1)}, u32[]{:S(2)}, u32[]{:S(2)}) collective-permute-start(bf16[96,2048]{1,0:T(8,128)(2,1)S(1)} %add_convert_fusion.5), channel_id=1, source_target_pairs={{0,2},{1,3},{2,0},{3,1},{4,6},{5,7},{6,4},{7,5},{8,10},{9,11},{10,... | collective-permute-start | bytes 1179656 | tf_op jit(solution)/shard_map/ppermute | solution.py:266
  73.3 9.4 %collective-permute-start.25 = (bf16[192,2048]{1,0:T(8,128)(2,1)S(1)}, bf16[192,2048]{1,0:T(8,128)(2,1)S(1)}, u32[]{:S(2)}, u32[]{:S(2)}) collective-permute-start(bf16[192,2048]{1,0:T(8,128)(2,1)S(1)} %get-tuple-element.74), channel_id=1, source_target_pairs={{0,1},{1,0},{2,3},{3,2},{4,5},{5,4},{6,7},{7,6},{8,9},{9,8},{10,11... | collective-permute-start | bytes 2359304 | tf_op jit(solution)/shard_map/ppermute | solution.py:267
  74.6 13.9 %collective-permute-start.33 = (bf16[96,2048]{1,0:T(8,128)(2,1)S(1)}, bf16[96,2048]{1,0:T(8,128)(2,1)S(1)}, u32[]{:S(2)}, u32[]{:S(2)}) collective-permute-start(bf16[96,2048]{1,0:T(8,128)(2,1)S(1)} %add_convert_fusion.1), channel_id=1, source_target_pairs={{0,12},{1,13},{2,14},{3,15},{4,0},{5,1},{6,2},{7,3},{8,4},{9,5},{1... | collective-permute-start | bytes 1179656 | tf_op jit(solution)/shard_map/ppermute | solution.py:265
  81.1 13.8 %collective-permute-start.28 = (bf16[96,2048]{1,0:T(8,128)(2,1)S(1)}, bf16[96,2048]{1,0:T(8,128)(2,1)S(1)}, u32[]{:S(2)}, u32[]{:S(2)}) collective-permute-start(bf16[96,2048]{1,0:T(8,128)(2,1)S(1)} %add_convert_fusion.3), channel_id=1, source_target_pairs={{0,4},{1,5},{2,6},{3,7},{4,8},{5,9},{6,10},{7,11},{8,12},{9,13},{1... | collective-permute-start | bytes 1179656 | tf_op jit(solution)/shard_map/ppermute | solution.py:265
  82.8 12.2 %collective-permute-start.26 = (bf16[96,2048]{1,0:T(8,128)(2,1)S(1)}, bf16[96,2048]{1,0:T(8,128)(2,1)S(1)}, u32[]{:S(2)}, u32[]{:S(2)}) collective-permute-start(bf16[96,2048]{1,0:T(8,128)(2,1)S(1)} %add_convert_fusion.4), channel_id=1, source_target_pairs={{0,2},{1,3},{2,0},{3,1},{4,6},{5,7},{6,4},{7,5},{8,10},{9,11},{10,... | collective-permute-start | bytes 1179656 | tf_op jit(solution)/shard_map/ppermute | solution.py:266
  (13 other events, 50.1 us)
